TPU v7x, 32 devices: a whole 2x2x4 slice. The times are simulated.
32 devices in a mesh: seq: 8 (over y, x, core), fsdp: 4 (over z).
Axes of the slice: x: 2, y: 2, z: 4, core: 2. Of those that a mesh axis runs over, the one named last changes fastest.
Arguments:
- tokens: bfloat16 [4, 3072, 768], P('fsdp', 'seq'), may hold values from -18 to 18, as said below
- lengths: int32 [4], P('fsdp'), may hold values from 768 to 3072, as said below
- w_qkv: bfloat16 [768, 2304], P('fsdp'), may hold values from -1 to 1, as said below
- q_bias: bfloat16 [768], P('fsdp'), may hold values from -2.5 to 2.5
- v_bias: bfloat16 [768], P('fsdp'), may hold values from -2.5 to 2.5
- w_out: bfloat16 [768, 768], P('fsdp'), may hold values from -1.25 to 1.25
- out_bias: bfloat16 [768], P('fsdp'), may hold values from -4 to 4
- ln1_gain: bfloat16 [768], P('fsdp'), may hold values from 0.5 to 1.5
- ln1_bias: bfloat16 [768], P('fsdp'), may hold values from -2.5 to 2.5
- w_in: bfloat16 [768, 3072], P('fsdp'), may hold values from -0.21875 to 0.21875
- in_bias: bfloat16 [3072], P('fsdp'), may hold values from -2.5 to 2.5
- w_back: bfloat16 [3072, 768], P('fsdp'), may hold values from -0.15625 to 0.15625
- back_bias: bfloat16 [768], P('fsdp'), may hold values from -2.5 to 2.5
- ln2_gain: bfloat16 [768], P('fsdp'), may hold values from 0.5 to 1.5
- ln2_bias: bfloat16 [768], P('fsdp'), may hold values from -2.5 to 2.5
- cotangent: bfloat16 [4, 3072, 768], P('fsdp', 'seq'), may hold values from -6 to 6
Outputs:
- output: bfloat16 [4, 3072, 768], P('fsdp', 'seq')
- grad_tokens: bfloat16 [4, 3072, 768], P('fsdp', 'seq')
- g_w_qkv: float32 [768, 2304], P('fsdp')
- g_q_bias: float32 [768], P('fsdp')
- g_v_bias: float32 [768], P('fsdp')
- g_w_out: float32 [768, 768], P('fsdp')
- g_out_bias: float32 [768], P('fsdp')
- g_ln1_gain: float32 [768], P('fsdp')
- g_ln1_bias: float32 [768], P('fsdp')
- g_w_in: float32 [768, 3072], P('fsdp')
- g_in_bias: float32 [3072], P('fsdp')
- g_w_back: float32 [3072, 768], P('fsdp')
- g_back_bias: float32 [768], P('fsdp')
- g_ln2_gain: float32 [768], P('fsdp')
- g_ln2_bias: float32 [768], P('fsdp')
Inputs may be any that keep to these rules, and one draw needn't show every extreme that they name: `lengths`: every sequence has at least 768 valid positions, and one sequence is full. `tokens`: real-valued entries of order one. `w_qkv`: real-valued entries of order 768 ** -0.5.
All inputs are finite; a program needn't handle non-finite values.
Results may differ from a plain program's by a relative error of at most 0.025.
Values may be sent and summed in bfloat16 or wider, within the bound.
A program may use at most 320 MiB of HBM per device.

v0:
```python
import jax
import jax.numpy as jnp
from jax import lax
from jax.sharding import PartitionSpec as P

HEADS = 12


masked_score = -1e30


def passed_along(block, axis, distance):
    devices = range(lax.axis_size(axis))
    route = [((i - distance) % len(devices), i) for i in devices]
    return lax.ppermute(block, axis, route)


def norm_forward(hidden, gain_vec, shift_vec):
    average = jnp.mean(hidden, axis=-1, keepdims=True)
    centred = hidden - average
    variance = jnp.mean(centred * centred, axis=-1, keepdims=True)
    inverse = lax.rsqrt(variance + 1e-05)
    normed = centred * inverse
    return (normed * gain_vec + shift_vec, normed, inverse)


def norm_backward(grad_norm, normed, inverse, gain_vec):
    scaled = grad_norm * gain_vec
    grad_input = inverse * (
        scaled
        - jnp.mean(scaled, axis=-1, keepdims=True)
        - normed * jnp.mean(scaled * normed, axis=-1, keepdims=True)
    )
    return (grad_input, jnp.sum(grad_norm * normed, axis=0), jnp.sum(grad_norm, axis=0))


def forward_tile(state_in, query_heads, key_pair, length):
    old_max, old_sum, old_acc = state_in
    key_rows = key_pair.shape[0]
    head_count = query_heads.shape[1]
    head_size = query_heads.shape[2]
    key_heads = key_pair[:, 0].reshape(key_rows, head_count, head_size)
    value_heads = key_pair[:, 1].reshape(key_rows, head_count, head_size)
    key_ok = jnp.arange(key_rows, dtype=jnp.int32) < length
    scores = jnp.einsum(
        "qhd,khd->hqk", query_heads, key_heads, preferred_element_type=jnp.float32
    ) * head_size ** (-0.5)
    scores = jnp.where(key_ok[None, None, :], scores, masked_score)
    new_max = jnp.maximum(old_max, jnp.max(scores, axis=2))
    prob_tile = jnp.where(key_ok[None, None, :], jnp.exp(scores - new_max[:, :, None]), 0.0)
    new_sum = jnp.sum(prob_tile, axis=2)
    new_acc = jnp.einsum(
        "hqk,khd->hqd",
        prob_tile.astype(jnp.bfloat16),
        value_heads,
        preferred_element_type=jnp.float32,
    )
    return (new_max, new_sum, new_acc)


def backward_tile(query_pair, log_total, delta, key_pair, key_start, length):
    query_rows = query_pair.shape[0]
    key_rows = key_pair.shape[0]
    model_width = query_pair.shape[2]
    head_count = log_total.shape[0]
    head_size = model_width // head_count
    score_scale = head_size ** (-0.5)
    query_heads = query_pair[:, 0].reshape(query_rows, head_count, head_size)
    grad_heads = query_pair[:, 1].reshape(query_rows, head_count, head_size)
    key_heads = key_pair[:, 0].reshape(key_rows, head_count, head_size)
    value_heads = key_pair[:, 1].reshape(key_rows, head_count, head_size)
    key_ok = key_start + jnp.arange(key_rows, dtype=jnp.int32) < length
    scores = (
        jnp.einsum("qhd,khd->hqk", query_heads, key_heads, preferred_element_type=jnp.float32)
        * score_scale
    )
    prob_tile = jnp.where(key_ok[None, None, :], jnp.exp(scores - log_total[:, :, None]), 0.0)
    grad_values = jnp.einsum(
        "hqk,qhd->khd",
        prob_tile.astype(jnp.bfloat16),
        grad_heads,
        preferred_element_type=jnp.float32,
    )
    grad_probs = jnp.einsum(
        "qhd,khd->hqk", grad_heads, value_heads, preferred_element_type=jnp.float32
    )
    grad_scores = (prob_tile * (grad_probs - delta[:, :, None])).astype(jnp.bfloat16)
    grad_queries = (
        jnp.einsum("hqk,khd->qhd", grad_scores, key_heads, preferred_element_type=jnp.float32)
        * score_scale
    )
    grad_keys = (
        jnp.einsum("hqk,qhd->khd", grad_scores, query_heads, preferred_element_type=jnp.float32)
        * score_scale
    )
    grad_pair = jnp.stack([grad_keys, grad_values], axis=1).reshape(key_rows, 2, model_width)
    return (grad_queries.reshape(query_rows, model_width), grad_pair)


def on_device(
    tokens,
    lengths,
    w_qkv,
    q_bias,
    v_bias,
    w_out,
    out_bias,
    ln1_gain,
    ln1_bias,
    w_in,
    in_bias,
    w_back,
    back_bias,
    ln2_gain,
    ln2_bias,
    cotangent,
):
    gathered = (
        lax.all_gather(w_qkv, "fsdp", axis=0, tiled=True),
        lax.all_gather(q_bias, "fsdp", axis=0, tiled=True),
        lax.all_gather(v_bias, "fsdp", axis=0, tiled=True),
        lax.all_gather(w_out, "fsdp", axis=0, tiled=True),
        lax.all_gather(out_bias, "fsdp", axis=0, tiled=True),
        lax.all_gather(ln1_gain, "fsdp", axis=0, tiled=True),
        lax.all_gather(ln1_bias, "fsdp", axis=0, tiled=True),
        lax.all_gather(w_in, "fsdp", axis=0, tiled=True),
        lax.all_gather(in_bias, "fsdp", axis=0, tiled=True),
        lax.all_gather(w_back, "fsdp", axis=0, tiled=True),
        lax.all_gather(back_bias, "fsdp", axis=0, tiled=True),
        lax.all_gather(ln2_gain, "fsdp", axis=0, tiled=True),
        lax.all_gather(ln2_bias, "fsdp", axis=0, tiled=True),
    )
    (
        full_qkv,
        full_qbias,
        full_vbias,
        full_out,
        full_obias,
        full_g1,
        full_n1,
        full_in,
        full_ibias,
        full_back,
        full_bbias,
        full_g2,
        full_n2,
    ) = gathered
    f32 = jnp.float32
    seq_index = lax.axis_index("seq")
    seq_count = lax.axis_size("seq")
    token_rows = tokens.shape[1]
    model_width = tokens.shape[2]
    head_count = HEADS
    head_size = model_width // head_count
    length = lengths[0]
    my_start = seq_index * token_rows
    row_valid = (my_start + jnp.arange(token_rows, dtype=jnp.int32) < length).astype(f32)
    inputs_b = tokens[0]
    inputs_f = inputs_b.astype(f32)
    bias_all = jnp.concatenate(
        [full_qbias.astype(f32), jnp.zeros((model_width,), f32), full_vbias.astype(f32)]
    )
    projected = (jnp.dot(inputs_b, full_qkv, preferred_element_type=f32) + bias_all).astype(
        jnp.bfloat16
    )
    query_heads = projected[:, :model_width].reshape(token_rows, head_count, head_size)
    key_pair = projected[:, model_width:].reshape(token_rows, 2, model_width)
    init_state = (
        jnp.full((head_count, token_rows), masked_score, f32),
        jnp.zeros((head_count, token_rows), f32),
        jnp.zeros((head_count, token_rows, head_size), f32),
    )
    pieces = lax.all_gather(key_pair, "seq", axis=0, tiled=True)
    run_max, run_sum, run_acc = forward_tile(init_state, query_heads, pieces, length)
    positive = run_sum > 0.0
    safe_sum = jnp.where(positive, run_sum, 1.0)
    attended_heads = jnp.where(positive[:, :, None], run_acc / safe_sum[:, :, None], 0.0)
    log_total = jnp.where(positive, run_max + jnp.log(safe_sum), 0.0)
    attended_f = attended_heads.transpose(1, 0, 2).reshape(token_rows, model_width)
    attended_b = attended_f.astype(jnp.bfloat16)
    branch_f = jnp.dot(attended_b, full_out, preferred_element_type=f32) + full_obias.astype(f32)
    first_norm, normed_one, inverse_one = norm_forward(
        inputs_f + branch_f, full_g1.astype(f32), full_n1.astype(f32)
    )
    first_low = first_norm.astype(jnp.bfloat16)
    inner_act = jnp.dot(first_low, full_in, preferred_element_type=f32) + full_ibias.astype(f32)
    activated_b = jax.nn.gelu(inner_act, approximate=False).astype(jnp.bfloat16)
    second = jnp.dot(activated_b, full_back, preferred_element_type=f32) + full_bbias.astype(f32)
    result, normed_two, inverse_two = norm_forward(
        first_norm + second, full_g2.astype(f32), full_n2.astype(f32)
    )
    output = (result * row_valid[:, None]).astype(jnp.bfloat16)
    grad_result = cotangent[0].astype(f32) * row_valid[:, None]
    grad_h2, g_ln2_gain, g_ln2_bias = norm_backward(
        grad_result, normed_two, inverse_two, full_g2.astype(f32)
    )
    grad_second = grad_h2.astype(jnp.bfloat16)
    g_w_back = jnp.einsum("tf,td->fd", activated_b, grad_second, preferred_element_type=f32)
    g_back_bias = jnp.sum(grad_second.astype(f32), axis=0)
    grad_act = jnp.einsum("td,fd->tf", grad_second, full_back, preferred_element_type=f32)
    gelu_value, gelu_pull = jax.vjp(
        lambda values_in: jax.nn.gelu(values_in, approximate=False), inner_act
    )
    grad_inner = gelu_pull(grad_act)[0].astype(jnp.bfloat16)
    g_w_in = jnp.einsum("td,tf->df", first_low, grad_inner, preferred_element_type=f32)
    g_in_bias = jnp.sum(grad_inner.astype(f32), axis=0)
    grad_first = grad_h2 + jnp.einsum("tf,df->td", grad_inner, full_in, preferred_element_type=f32)
    grad_h1, g_ln1_gain, g_ln1_bias = norm_backward(
        grad_first, normed_one, inverse_one, full_g1.astype(f32)
    )
    grad_branch = grad_h1.astype(jnp.bfloat16)
    g_w_out = jnp.einsum("tc,td->cd", attended_b, grad_branch, preferred_element_type=f32)
    g_out_bias = jnp.sum(grad_branch.astype(f32), axis=0)
    grad_attended = jnp.einsum(
        "td,cd->tc", grad_branch, full_out, preferred_element_type=f32
    ).astype(jnp.bfloat16)
    delta = jnp.sum(
        (grad_attended.astype(f32) * attended_f).reshape(token_rows, head_count, head_size), axis=2
    ).T
    query_pair = jnp.stack([projected[:, :model_width], grad_attended], axis=1)
    zero_rows = jnp.zeros((token_rows, model_width), f32)
    zero_pair = jnp.zeros((token_rows, 2, model_width), f32)

    def visit_keys(hop_index, grad_q, moving_pair, grad_pair):
        anchor = (seq_index - hop_index) % seq_count
        add_q, add_pair = backward_tile(
            query_pair, log_total, delta, moving_pair, anchor * token_rows, length
        )
        return (grad_q + add_q, grad_pair + add_pair)

    def return_key_grads(grad_pair):
        return passed_along(grad_pair.astype(jnp.bfloat16), "seq", 1).astype(grad_pair.dtype)

    def key_hop(hop_index, loop_state):
        grad_q, moving_pair, grad_pair = loop_state
        grad_q, grad_pair = visit_keys(hop_index, grad_q, moving_pair, grad_pair)
        moved = passed_along(moving_pair, "seq", 1)
        return (grad_q, moved, return_key_grads(grad_pair))

    grad_q, moving_pair, grad_pair = lax.fori_loop(
        0, seq_count - 1, key_hop, (zero_rows, key_pair, zero_pair)
    )
    grad_q, grad_pair = visit_keys(seq_count - 1, grad_q, moving_pair, grad_pair)
    grad_pair = return_key_grads(grad_pair)
    grad_projected = jnp.concatenate(
        [grad_q, grad_pair.reshape(token_rows, 2 * model_width)], axis=1
    ).astype(jnp.bfloat16)
    g_w_qkv = jnp.einsum("td,te->de", inputs_b, grad_projected, preferred_element_type=f32)
    grad_proj_f = grad_projected.astype(f32)
    g_q_bias = jnp.sum(grad_proj_f[:, :model_width], axis=0)
    g_v_bias = jnp.sum(grad_proj_f[:, 2 * model_width :], axis=0)
    grad_input = grad_h1 + jnp.einsum(
        "te,de->td", grad_projected, full_qkv, preferred_element_type=f32
    )
    local_grads = (
        g_w_qkv,
        g_q_bias,
        g_v_bias,
        g_w_out,
        g_out_bias,
        g_ln1_gain,
        g_ln1_bias,
        g_w_in,
        g_in_bias,
        g_w_back,
        g_back_bias,
        g_ln2_gain,
        g_ln2_bias,
    )
    owned = (
        lax.psum_scatter(
            local_grads[0].astype(jnp.bfloat16), "fsdp", scatter_dimension=0, tiled=True
        ).astype(jnp.float32),
        lax.psum_scatter(
            local_grads[1].astype(jnp.bfloat16), "fsdp", scatter_dimension=0, tiled=True
        ).astype(jnp.float32),
        lax.psum_scatter(
            local_grads[2].astype(jnp.bfloat16), "fsdp", scatter_dimension=0, tiled=True
        ).astype(jnp.float32),
        lax.psum_scatter(
            local_grads[3].astype(jnp.bfloat16), "fsdp", scatter_dimension=0, tiled=True
        ).astype(jnp.float32),
        lax.psum_scatter(
            local_grads[4].astype(jnp.bfloat16), "fsdp", scatter_dimension=0, tiled=True
        ).astype(jnp.float32),
        lax.psum_scatter(
            local_grads[5].astype(jnp.bfloat16), "fsdp", scatter_dimension=0, tiled=True
        ).astype(jnp.float32),
        lax.psum_scatter(
            local_grads[6].astype(jnp.bfloat16), "fsdp", scatter_dimension=0, tiled=True
        ).astype(jnp.float32),
        lax.psum_scatter(
            local_grads[7].astype(jnp.bfloat16), "fsdp", scatter_dimension=0, tiled=True
        ).astype(jnp.float32),
        lax.psum_scatter(
            local_grads[8].astype(jnp.bfloat16), "fsdp", scatter_dimension=0, tiled=True
        ).astype(jnp.float32),
        lax.psum_scatter(
            local_grads[9].astype(jnp.bfloat16), "fsdp", scatter_dimension=0, tiled=True
        ).astype(jnp.float32),
        lax.psum_scatter(
            local_grads[10].astype(jnp.bfloat16), "fsdp", scatter_dimension=0, tiled=True
        ).astype(jnp.float32),
        lax.psum_scatter(
            local_grads[11].astype(jnp.bfloat16), "fsdp", scatter_dimension=0, tiled=True
        ).astype(jnp.float32),
        lax.psum_scatter(
            local_grads[12].astype(jnp.bfloat16), "fsdp", scatter_dimension=0, tiled=True
        ).astype(jnp.float32),
    )
    totals = (
        lax.psum(owned[0].astype(jnp.bfloat16), "seq").astype(jnp.float32),
        lax.psum(owned[1].astype(jnp.bfloat16), "seq").astype(jnp.float32),
        lax.psum(owned[2].astype(jnp.bfloat16), "seq").astype(jnp.float32),
        lax.psum(owned[3].astype(jnp.bfloat16), "seq").astype(jnp.float32),
        lax.psum(owned[4].astype(jnp.bfloat16), "seq").astype(jnp.float32),
        lax.psum(owned[5].astype(jnp.bfloat16), "seq").astype(jnp.float32),
        lax.psum(owned[6].astype(jnp.bfloat16), "seq").astype(jnp.float32),
        lax.psum(owned[7].astype(jnp.bfloat16), "seq").astype(jnp.float32),
        lax.psum(owned[8].astype(jnp.bfloat16), "seq").astype(jnp.float32),
        lax.psum(owned[9].astype(jnp.bfloat16), "seq").astype(jnp.float32),
        lax.psum(owned[10].astype(jnp.bfloat16), "seq").astype(jnp.float32),
        lax.psum(owned[11].astype(jnp.bfloat16), "seq").astype(jnp.float32),
        lax.psum(owned[12].astype(jnp.bfloat16), "seq").astype(jnp.float32),
    )
    return (output[None], grad_input.astype(jnp.bfloat16)[None]) + tuple(totals)


def solution(mesh):
    return jax.shard_map(
        on_device,
        mesh=mesh,
        in_specs=(
            P("fsdp", "seq", None),
            P("fsdp"),
            P("fsdp", None),
            P("fsdp"),
            P("fsdp"),
            P("fsdp", None),
            P("fsdp"),
            P("fsdp"),
            P("fsdp"),
            P("fsdp", None),
            P("fsdp"),
            P("fsdp", None),
            P("fsdp"),
            P("fsdp"),
            P("fsdp"),
            P("fsdp", "seq", None),
        ),
        out_specs=(
            P("fsdp", "seq", None),
            P("fsdp", "seq", None),
            P("fsdp", None),
            P("fsdp"),
            P("fsdp"),
            P("fsdp", None),
            P("fsdp"),
            P("fsdp"),
            P("fsdp"),
            P("fsdp", None),
            P("fsdp"),
            P("fsdp", None),
            P("fsdp"),
            P("fsdp"),
            P("fsdp"),
        ),
        check_vma=False,
    )
```

profile of v0, /device:TPU:1, one launch (start us, length us, event | category | flops | bytes accessed | tf_op | source)
XLA Modules:
  0.0 1093.0 jit_solution(14057378559241198975)
XLA Ops:
  15.8 17.2 %all-reduce.20 = (bf16[768]{0:T(1024)(128)(2,1)S(1)}, bf16[768]{0:T(1024)(128)(2,1)S(1)}, bf16[768]{0:T(1024)(128)(2,1)S(1)}, bf16[768]{0:T(1024)(128)(2,1)S(1)}...) all-reduce(bf16[768]{0:T(1024)(128)(2,1)S(1)} %dynamic-update-slice, ...), channel_id=1, replica_groups=mesh['seq'=8,'fsdp'=4] {'fsdp'}, use_global_device_ids=true, to_apply=%add.1 | all-reduce | flops 5376 | bytes 21504
  33.1 48.8 %all-gather.7.cloned.1.call-done = bf16[768,2304]{1,0:T(8,128)(2,1)} async-done(((bf16[192,2304]{1,0:T(8,128)(2,1)}), bf16[768,2304]{1,0:T(8,128)(2,1)}) %all-gather.7.cloned.1.call-update) | async-done | bytes 3538960 | tf_op jit(solution)/shard_map/all_gather | solution.py:119
  81.9 3.7 fusion.21
  91.1 10.4 all-gather
  103.2 3.3 copy.58
  106.8 38.6 %all-gather.9.cloned.1.call-done = bf16[3072,2,768]{2,1,0:T(2,128)(2,1)} async-done(((bf16[384,2,768]{2,1,0:T(2,128)(2,1)}), bf16[3072,2,768]{2,1,0:T(2,128)(2,1)}) %all-gather.9.cloned.1.call-update) | async-done | bytes 9437200 | tf_op jit(solution)/shard_map/all_gather | solution.py:173
  145.3 19.5 %fusion.75 = (bf16[3072,1,768]{2,1,0:T(2,128)(2,1)}, bf16[3072,1,768]{2,1,0:T(2,128)(2,1)}) fusion(bf16[3072,2,768]{2,1,0:T(2,128)(2,1)} %all-gather.9.cloned.1.call-done), kind=kLoop, calls=%fused_computation.134 | loop fusion | bytes 18874368 | tf_op jit(solution)/shard_map/slice | solution.py:42
  164.8 19.8 %copy.54 = bf16[3072,1,768]{0,2,1:T(8,128)(2,1)} copy(bf16[3072,1,768]{2,1,0:T(2,128)(2,1)} %get-tuple-element.439) | data formatting | bytes 9437184 | tf_op jit(solution)/shard_map/slice | solution.py:42
  184.6 23.5 %fusion.7 = (f32[12,384]{1,0:T(8,128)S(1)}, f32[12,384,3072]{2,1,0:T(8,128)}) fusion(pred[3072]{0:T(1024)(128)(4,1)S(1)} %iota_compare_fusion, bf16[384,12,64]{0,2,1:T(8,128)(2,1)S(1)} %bitcast.141, bf16[3072,12,64]{0,2,1:T(8,128)(2,1)} %bitcast.147), kind=kOutput, calls=%fused_computation.15 | convolution fusion | flops 1854402048 | bytes 61953024 | tf_op jit(solution)/shard_map/qhd,khd->hqk/dot_general | solution.py:45
  208.8 18.8 %fusion.9 = f32[12,384]{1,0:T(8,128)S(1)} fusion(f32[12,384,3072]{2,1,0:T(8,128)} %get-tuple-element.446, f32[12,384]{1,0:T(8,128)S(1)} %broadcast_maximum_fusion, pred[3072]{0:T(1024)(128)(4,1)S(1)} %iota_compare_fusion), kind=kLoop, calls=%fused_computation.17 | loop fusion | flops 70774272 | bytes 56663040 | tf_op jit(solution)/shard_map/reduce_sum | solution.py:51
  228.2 19.8 %copy.55 = bf16[3072,1,768]{0,2,1:T(8,128)(2,1)} copy(bf16[3072,1,768]{2,1,0:T(2,128)(2,1)} %get-tuple-element.440) | data formatting | bytes 9437184 | tf_op jit(solution)/shard_map/slice | solution.py:43
  248.0 22.0 %divide_select_fusion = f32[384,12,64]{0,2,1:T(8,128)S(1)} fusion(bf16[3072,12,64]{0,2,1:T(8,128)(2,1)} %bitcast.154, f32[12,384,3072]{2,1,0:T(8,128)} %get-tuple-element.446, f32[12,384]{1,0:T(8,128)S(1)} %broadcast_maximum_fusion, pred[3072]{0:T(1024)(128)(4,1)S(1)} %iota_compare_fusion, f32[384,12]{0,1:T(8,128)S(1)} %bitcast_select_fusion, ...), kind=kOutput, calls=%fused_computation.88 | convolution fusion | flops 1883308032 | bytes 62565888 | tf_op jit(solution)/shard_map/hqk,khd->hqd/dot_general | solution.py:52
  274.6 15.9 %multiply_convert_fusion.2 = (bf16[384,3072]{1,0:T(8,128)(2,1)}, f32[384,3072]{1,0:T(8,128)}, f32[384,3072]{1,0:T(8,128)}) fusion(f32[3072]{0:T(1024)} %bitcast.167, bf16[768,3072]{1,0:T(8,128)(2,1)} %all-gather.13.cloned.1.call-done, f32[384,768]{1,0:T(8,128)S(1)} %get-tuple-element.448, f32[768]{0:T(1024)} %convert_element_type.247, ...), kind=kOutput, calls=%fused_computation.29 | convolution fusion | flops 1891270656 | bytes 17716224 | tf_op jit(solution)/shard_map/dot_general | solution.py:186
  290.5 65.9 %all-gather.15.cloned.1.call-done = bf16[3072,768]{1,0:T(8,128)(2,1)} async-done(((bf16[768,768]{1,0:T(8,128)(2,1)}), bf16[3072,768]{1,0:T(8,128)(2,1)}) %all-gather.15.cloned.1.call-update) | async-done | bytes 4718608 | tf_op jit(solution)/shard_map/all_gather | solution.py:128
  356.4 5.3 fusion.79
  364.5 7.0 fusion.80
  371.6 2.9 multiply_reduce_fusion
  378.2 307.5 %while.20 = (s32[]{:T(128)}, f32[384,768]{0,1:T(8,128)}, bf16[384,2,768]{0,2,1:T(8,128)(2,1)}, f32[384,2,768]{0,2,1:T(8,128)}, s32[]{:T(128)}, /*index=5*/s32[]{...) while((s32[]{:T(128)}, f32[384,768]{0,1:T(8,128)}, ...), condition=%wide.region_12.13_spmd.clone, body=%wide.region_11.12_spmd.clone.sunk | while | flops 1154286336 | bytes 99884848 | solution.py:240
  378.3 2.8 copy.79
  386.6 3.6 multiply_convert_fusion.5
  398.1 10.6 collective-permute-done.1
  408.8 2.8 convert_element_type.366
  411.6 9.8 collective-permute-done
  421.5 2.8 copy.79
  429.8 3.6 multiply_convert_fusion.5
  442.2 10.6 collective-permute-done.1
  452.8 2.8 convert_element_type.366
  455.6 9.8 collective-permute-done
  465.5 2.8 copy.79
  473.8 3.6 multiply_convert_fusion.5
  486.2 10.6 collective-permute-done.1
  499.6 9.8 collective-permute-done
  509.5 2.8 copy.79
  517.8 3.6 multiply_convert_fusion.5
  531.1 9.8 collective-permute-done.1
  543.6 9.8 collective-permute-done
  553.5 2.8 copy.79
  561.9 3.6 multiply_convert_fusion.5
  576.0 8.9 collective-permute-done.1
  587.7 9.8 collective-permute-done
  597.5 2.8 copy.79
  605.9 3.6 multiply_convert_fusion.5
  620.9 8.0 collective-permute-done.1
  631.7 9.8 collective-permute-done
  641.6 2.8 copy.79
  649.9 3.6 multiply_convert_fusion.5
  659.4 3.6 collective-permute-start
  665.8 7.1 collective-permute-done.1
  672.9 2.8 convert_element_type.366
  675.7 9.8 collective-permute-done
  689.7 2.9 multiply_convert_fusion.1
  698.7 11.6 %collective-permute-done.2 = bf16[384,2,768]{0,2,1:T(8,128)(2,1)S(1)} collective-permute-done((bf16[384,2,768]{0,2,1:T(8,128)(2,1)S(1)}, bf16[384,2,768]{0,2,1:T(8,128)(2,1)S(1)}, u32[]{:S(2)}, u32[]{:S(2)}) %collective-permute-start.2) | collective-permute-done | bytes 1179680 | tf_op jit(solution)/shard_map/ppermute | solution.py:15
  713.3 4.1 copy.63
  720.9 6.5 convolution_convert_fusion
  728.7 6.8 convolution_convert_fusion.1
  735.6 53.6 %reduce-scatter.13.cloned.1.call-done = bf16[192,2304]{1,0:T(8,128)(2,1)} async-done(((bf16[768,2304]{1,0:T(8,128)(2,1)}), bf16[192,2304]{1,0:T(8,128)(2,1)}) %reduce-scatter.13.cloned.1.call-update) | async-done | bytes 884752
  791.7 29.3 %reduce-scatter.7.cloned.1.call-done = bf16[192,768]{1,0:T(8,128)(2,1)} async-done(((bf16[768,768]{1,0:T(8,128)(2,1)}), bf16[192,768]{1,0:T(8,128)(2,1)}) %reduce-scatter.7.cloned.1.call-update) | async-done | bytes 294928 | tf_op jit(solution)/shard_map/reduce_scatter | solution.py:280
  821.0 86.5 %reduce-scatter.11.cloned.1.call-done = bf16[768,768]{1,0:T(8,128)(2,1)} async-done(((bf16[3072,768]{1,0:T(8,128)(2,1)}), bf16[768,768]{1,0:T(8,128)(2,1)}) %reduce-scatter.11.cloned.1.call-update) | async-done | bytes 1179664 | tf_op jit(solution)/shard_map/reduce_scatter | solution.py:298
  907.6 88.1 %reduce-scatter.9.cloned.1.call-done = bf16[192,3072]{1,0:T(8,128)(2,1)} async-done(((bf16[768,3072]{1,0:T(8,128)(2,1)}), bf16[192,3072]{1,0:T(8,128)(2,1)}) %reduce-scatter.9.cloned.1.call-update) | async-done | bytes 1179664 | tf_op jit(solution)/shard_map/reduce_scatter | solution.py:292
  998.2 14.6 %all-reduce.19 = (bf16[768]{0:T(1024)(128)(2,1)S(1)}, bf16[768]{0:T(1024)(128)(2,1)S(1)}, bf16[768]{0:T(1024)(128)(2,1)S(1)}, bf16[768]{0:T(1024)(128)(2,1)S(1)}...) all-reduce(bf16[768]{0:T(1024)(128)(2,1)S(1)} %dynamic-update-slice, ...), channel_id=1, replica_groups=mesh['seq'=8,'fsdp'=4] {'fsdp'}, use_global_device_ids=true, to_apply=%add.7 | all-reduce | flops 9984 | bytes 39936
  1013.5 16.1 %all-reduce.17 = (bf16[192]{0:T(256)(128)(2,1)S(1)}, bf16[192]{0:T(256)(128)(2,1)S(1)}, bf16[192]{0:T(256)(128)(2,1)S(1)}, bf16[192]{0:T(256)(128)(2,1)S(1)}, bf...) all-reduce(bf16[192]{0:T(256)(128)(2,1)S(1)} %dynamic-slice.9, ...), channel_id=1, replica_groups=mesh['seq'=8,'fsdp'=4] {'seq'}, use_global_device_ids=true, to_apply=%region_17.18 | all-reduce | flops 2304 | bytes 9216 | tf_op jit(solution)/shard_map/psum | solution.py:313
  1035.8 4.8 fusion.32
  1040.6 38.2 %all-reduce.23.cloned.1.call-done = (bf16[192,2304]{0,1:T(8,128)(2,1)}, bf16[192,768]{1,0:T(8,128)(2,1)}, bf16[192,3072]{1,0:T(8,128)(2,1)}, bf16[768,768]{1,0:T(8,128)(2,1)}) async-done(((bf16[192,2304]{0,1:T(8,128)(2,1)}, bf16[192,768]{1,0:T(8,128)(2,1)}, bf16[192,3072]{1,0:T(8,128)(2,1)}, bf16[768,768]{1,0:T(8,128)(2,1)}), (bf16[192,2304]{0,1:T(8,128)(2,1)}, bf16[192,768]{1,0:T(8,128)(2,1)}, ...) | async-done | bytes 3538960 | tf_op jit(solution)/shard_map/psum | solution.py:312
  1078.8 3.0 convert_element_type.283
  (466 shorter events, 173.4 us)
Async XLA Ops:
  7.2 74.7 %all-gather.7.cloned.1.call-start = ((), (), s32[]{:S(2)}) async-start(), calls=%async_computation.4 | async-start | bytes 4423680 | tf_op jit(solution)/shard_map/all_gather | solution.py:119
  7.9 137.4 %all-gather.9.cloned.1.call-start = ((), (), s32[]{:S(2)}) async-start(), calls=%async_computation.5 | async-start | bytes 10616832 | tf_op jit(solution)/shard_map/all_gather | solution.py:173
  85.6 17.6 %copy-start.20 = (bf16[384,2304]{1,0:T(8,128)(2,1)}, bf16[384,2304]{1,0:T(8,128)(2,1)S(1)}, u32[]{:S(2)}) copy-start(bf16[384,2304]{1,0:T(8,128)(2,1)S(1)} %fusion.21) | copy-start | bytes 5308420
  87.2 184.2 %all-gather.11.cloned.1.call-start = ((), (), s32[]{:S(2)}) async-start(), calls=%async_computation.6 | async-start | bytes 1474560 | tf_op jit(solution)/shard_map/all_gather | solution.py:122
  88.0 186.6 %all-gather.13.cloned.1.call-start = ((), (), s32[]{:S(2)}) async-start(), calls=%async_computation.7 | async-start | bytes 5898240 | tf_op jit(solution)/shard_map/all_gather | solution.py:126
  88.5 267.9 %all-gather.15.cloned.1.call-start = ((), (), s32[]{:S(2)}) async-start(), calls=%async_computation.8 | async-start | bytes 5898240 | tf_op jit(solution)/shard_map/all_gather | solution.py:128
  89.1 700.1 %reduce-scatter.13.cloned.1.call-start = ((), (), s32[]{:S(2)}) async-start(), calls=%async_computation.12 | async-start | bytes 4423680
  90.5 265.9 %copy-start.45 = (f32[768]{0:T(1024)}, f32[768]{0:T(1024)S(1)}, u32[]{:S(2)}) copy-start(f32[768]{0:T(1024)S(1)} %convert_element_type.246) | copy-start | bytes 9220
  273.5 101.0 %copy-start.16 = (f32[384,768]{1,0:T(8,128)}, f32[384,768]{1,0:T(8,128)S(1)}, u32[]{:S(2)}) copy-start(f32[384,768]{1,0:T(8,128)S(1)} %get-tuple-element.448) | copy-start | bytes 3538948
  273.5 101.0 %copy-start.43 = (f32[384]{0:T(512)}, f32[384]{0:T(512)S(1)}, u32[]{:S(2)}) copy-start(f32[384]{0:T(512)S(1)} %broadcast_multiply_fusion.5) | copy-start | bytes 4612
  273.8 100.7 %copy-start.50 = (f32[384]{0:T(512)}, f32[384]{0:T(512)S(1)}, u32[]{:S(2)}) copy-start(f32[384]{0:T(512)S(1)} %add_rsqrt_fusion.1) | copy-start | bytes 4612
  274.6 81.9 %copy-start.56 = (f32[768]{0:T(1024)S(1)}, f32[768]{0:T(1024)}, u32[]{:S(2)}) copy-start(f32[768]{0:T(1024)} %convert_element_type.247) | copy-start | bytes 9220
  274.6 81.9 %copy-start.58 = (f32[768]{0:T(1024)S(1)}, f32[768]{0:T(1024)}, u32[]{:S(2)}) copy-start(f32[768]{0:T(1024)} %convert_element_type.251) | copy-start | bytes 9220
  393.6 15.2 %collective-permute-start.1 = (bf16[384,2,768]{0,2,1:T(8,128)(2,1)}, bf16[384,2,768]{0,2,1:T(8,128)(2,1)}, u32[]{:S(2)}, u32[]{:S(2)}) collective-permute-start(bf16[384,2,768]{0,2,1:T(8,128)(2,1)} %fusion.143), channel_id=1, source_target_pairs={{28,0},{0,4},{4,8},{8,12},{12,16},{16,20},{20,24},{24,28},{29,1},{... | collective-permute-start | bytes 3538952 | tf_op jit(solution)/shard_map/while/body/eval_jaxpr/ppermute | solution.py:15
  395.3 26.1 %collective-permute-start = (bf16[384,2,768]{0,2,1:T(8,128)(2,1)}, bf16[384,2,768]{0,2,1:T(8,128)(2,1)}, u32[]{:S(2)}, u32[]{:S(2)}) collective-permute-start(bf16[384,2,768]{0,2,1:T(8,128)(2,1)} %copy.79), channel_id=1, source_target_pairs={{28,0},{0,4},{4,8},{8,12},{12,16},{16,20},{20,24},{24,28},{29,1},{... | collective-permute-start | bytes 3538952 | tf_op jit(solution)/shard_map/while/body/eval_jaxpr/ppermute | solution.py:15
  398.1 23.3 %copy-start.6 = (f32[384,768]{0,1:T(8,128)}, f32[384,768]{0,1:T(8,128)S(1)}, u32[]{:S(2)}) copy-start(f32[384,768]{0,1:T(8,128)S(1)} %bitcast_add_fusion.3) | copy-start | bytes 3538948 | tf_op jit(solution)/shard_map/while
  398.1 23.3 %copy-start.2 = (bf16[384,768]{0,1:T(8,128)(2,1)S(1)}, bf16[384,768]{0,1:T(8,128)(2,1)}, u32[]{:S(2)}) copy-start(bf16[384,768]{0,1:T(8,128)(2,1)} %copy-done.1) | copy-start | bytes 1769476 | tf_op jit(solution)/shard_map/while
  398.1 23.3 %copy-start.33 = (bf16[384,768]{0,1:T(8,128)(2,1)S(1)}, bf16[384,768]{0,1:T(8,128)(2,1)}, u32[]{:S(2)}) copy-start(bf16[384,768]{0,1:T(8,128)(2,1)} %copy-done.32) | copy-start | bytes 1769476 | tf_op jit(solution)/shard_map/while
  398.1 23.3 %copy-start.40 = (f32[12,384]{1,0:T(8,128)S(1)}, f32[12,384]{1,0:T(8,128)}, u32[]{:S(2)}) copy-start(f32[12,384]{1,0:T(8,128)} %get-tuple-element.639) | copy-start | bytes 55300 | tf_op jit(solution)/shard_map/while
  436.8 15.9 %collective-permute-start.1 = (bf16[384,2,768]{0,2,1:T(8,128)(2,1)}, bf16[384,2,768]{0,2,1:T(8,128)(2,1)}, u32[]{:S(2)}, u32[]{:S(2)}) collective-permute-start(bf16[384,2,768]{0,2,1:T(8,128)(2,1)} %fusion.143), channel_id=1, source_target_pairs={{28,0},{0,4},{4,8},{8,12},{12,16},{16,20},{20,24},{24,28},{29,1},{... | collective-permute-start | bytes 3538952 | tf_op jit(solution)/shard_map/while/body/eval_jaxpr/ppermute | solution.py:15
  439.3 26.1 %collective-permute-start = (bf16[384,2,768]{0,2,1:T(8,128)(2,1)}, bf16[384,2,768]{0,2,1:T(8,128)(2,1)}, u32[]{:S(2)}, u32[]{:S(2)}) collective-permute-start(bf16[384,2,768]{0,2,1:T(8,128)(2,1)} %copy.79), channel_id=1, source_target_pairs={{28,0},{0,4},{4,8},{8,12},{12,16},{16,20},{20,24},{24,28},{29,1},{... | collective-permute-start | bytes 3538952 | tf_op jit(solution)/shard_map/while/body/eval_jaxpr/ppermute | solution.py:15
  442.1 23.3 %copy-start.6 = (f32[384,768]{0,1:T(8,128)}, f32[384,768]{0,1:T(8,128)S(1)}, u32[]{:S(2)}) copy-start(f32[384,768]{0,1:T(8,128)S(1)} %bitcast_add_fusion.3) | copy-start | bytes 3538948 | tf_op jit(solution)/shard_map/while
  442.1 23.3 %copy-start.2 = (bf16[384,768]{0,1:T(8,128)(2,1)S(1)}, bf16[384,768]{0,1:T(8,128)(2,1)}, u32[]{:S(2)}) copy-start(bf16[384,768]{0,1:T(8,128)(2,1)} %copy-done.1) | copy-start | bytes 1769476 | tf_op jit(solution)/shard_map/while
  442.1 23.3 %copy-start.33 = (bf16[384,768]{0,1:T(8,128)(2,1)S(1)}, bf16[384,768]{0,1:T(8,128)(2,1)}, u32[]{:S(2)}) copy-start(bf16[384,768]{0,1:T(8,128)(2,1)} %copy-done.32) | copy-start | bytes 1769476 | tf_op jit(solution)/shard_map/while
  442.2 23.3 %copy-start.40 = (f32[12,384]{1,0:T(8,128)S(1)}, f32[12,384]{1,0:T(8,128)}, u32[]{:S(2)}) copy-start(f32[12,384]{1,0:T(8,128)} %get-tuple-element.639) | copy-start | bytes 55300 | tf_op jit(solution)/shard_map/while
  480.8 16.0 %collective-permute-start.1 = (bf16[384,2,768]{0,2,1:T(8,128)(2,1)}, bf16[384,2,768]{0,2,1:T(8,128)(2,1)}, u32[]{:S(2)}, u32[]{:S(2)}) collective-permute-start(bf16[384,2,768]{0,2,1:T(8,128)(2,1)} %fusion.143), channel_id=1, source_target_pairs={{28,0},{0,4},{4,8},{8,12},{12,16},{16,20},{20,24},{24,28},{29,1},{... | collective-permute-start | bytes 3538952 | tf_op jit(solution)/shard_map/while/body/eval_jaxpr/ppermute | solution.py:15
  483.3 26.1 %collective-permute-start = (bf16[384,2,768]{0,2,1:T(8,128)(2,1)}, bf16[384,2,768]{0,2,1:T(8,128)(2,1)}, u32[]{:S(2)}, u32[]{:S(2)}) collective-permute-start(bf16[384,2,768]{0,2,1:T(8,128)(2,1)} %copy.79), channel_id=1, source_target_pairs={{28,0},{0,4},{4,8},{8,12},{12,16},{16,20},{20,24},{24,28},{29,1},{... | collective-permute-start | bytes 3538952 | tf_op jit(solution)/shard_map/while/body/eval_jaxpr/ppermute | solution.py:15
  486.1 23.3 %copy-start.6 = (f32[384,768]{0,1:T(8,128)}, f32[384,768]{0,1:T(8,128)S(1)}, u32[]{:S(2)}) copy-start(f32[384,768]{0,1:T(8,128)S(1)} %bitcast_add_fusion.3) | copy-start | bytes 3538948 | tf_op jit(solution)/shard_map/while
  486.1 23.3 %copy-start.2 = (bf16[384,768]{0,1:T(8,128)(2,1)S(1)}, bf16[384,768]{0,1:T(8,128)(2,1)}, u32[]{:S(2)}) copy-start(bf16[384,768]{0,1:T(8,128)(2,1)} %copy-done.1) | copy-start | bytes 1769476 | tf_op jit(solution)/shard_map/while
  486.2 23.3 %copy-start.33 = (bf16[384,768]{0,1:T(8,128)(2,1)S(1)}, bf16[384,768]{0,1:T(8,128)(2,1)}, u32[]{:S(2)}) copy-start(bf16[384,768]{0,1:T(8,128)(2,1)} %copy-done.32) | copy-start | bytes 1769476 | tf_op jit(solution)/shard_map/while
  486.2 23.3 %copy-start.40 = (f32[12,384]{1,0:T(8,128)S(1)}, f32[12,384]{1,0:T(8,128)}, u32[]{:S(2)}) copy-start(f32[12,384]{1,0:T(8,128)} %get-tuple-element.639) | copy-start | bytes 55300 | tf_op jit(solution)/shard_map/while
  524.9 16.0 %collective-permute-start.1 = (bf16[384,2,768]{0,2,1:T(8,128)(2,1)}, bf16[384,2,768]{0,2,1:T(8,128)(2,1)}, u32[]{:S(2)}, u32[]{:S(2)}) collective-permute-start(bf16[384,2,768]{0,2,1:T(8,128)(2,1)} %fusion.143), channel_id=1, source_target_pairs={{28,0},{0,4},{4,8},{8,12},{12,16},{16,20},{20,24},{24,28},{29,1},{... | collective-permute-start | bytes 3538952 | tf_op jit(solution)/shard_map/while/body/eval_jaxpr/ppermute | solution.py:15
  527.4 26.1 %collective-permute-start = (bf16[384,2,768]{0,2,1:T(8,128)(2,1)}, bf16[384,2,768]{0,2,1:T(8,128)(2,1)}, u32[]{:S(2)}, u32[]{:S(2)}) collective-permute-start(bf16[384,2,768]{0,2,1:T(8,128)(2,1)} %copy.79), channel_id=1, source_target_pairs={{28,0},{0,4},{4,8},{8,12},{12,16},{16,20},{20,24},{24,28},{29,1},{... | collective-permute-start | bytes 3538952 | tf_op jit(solution)/shard_map/while/body/eval_jaxpr/ppermute | solution.py:15
  531.0 22.4 %copy-start.6 = (f32[384,768]{0,1:T(8,128)}, f32[384,768]{0,1:T(8,128)S(1)}, u32[]{:S(2)}) copy-start(f32[384,768]{0,1:T(8,128)S(1)} %bitcast_add_fusion.3) | copy-start | bytes 3538948 | tf_op jit(solution)/shard_map/while
  531.0 22.4 %copy-start.2 = (bf16[384,768]{0,1:T(8,128)(2,1)S(1)}, bf16[384,768]{0,1:T(8,128)(2,1)}, u32[]{:S(2)}) copy-start(bf16[384,768]{0,1:T(8,128)(2,1)} %copy-done.1) | copy-start | bytes 1769476 | tf_op jit(solution)/shard_map/while
  531.0 22.4 %copy-start.33 = (bf16[384,768]{0,1:T(8,128)(2,1)S(1)}, bf16[384,768]{0,1:T(8,128)(2,1)}, u32[]{:S(2)}) copy-start(bf16[384,768]{0,1:T(8,128)(2,1)} %copy-done.32) | copy-start | bytes 1769476 | tf_op jit(solution)/shard_map/while
  531.0 22.4 %copy-start.40 = (f32[12,384]{1,0:T(8,128)S(1)}, f32[12,384]{1,0:T(8,128)}, u32[]{:S(2)}) copy-start(f32[12,384]{1,0:T(8,128)} %get-tuple-element.639) | copy-start | bytes 55300 | tf_op jit(solution)/shard_map/while
  568.9 16.0 %collective-permute-start.1 = (bf16[384,2,768]{0,2,1:T(8,128)(2,1)}, bf16[384,2,768]{0,2,1:T(8,128)(2,1)}, u32[]{:S(2)}, u32[]{:S(2)}) collective-permute-start(bf16[384,2,768]{0,2,1:T(8,128)(2,1)} %fusion.143), channel_id=1, source_target_pairs={{28,0},{0,4},{4,8},{8,12},{12,16},{16,20},{20,24},{24,28},{29,1},{... | collective-permute-start | bytes 3538952 | tf_op jit(solution)/shard_map/while/body/eval_jaxpr/ppermute | solution.py:15
  571.4 26.1 %collective-permute-start = (bf16[384,2,768]{0,2,1:T(8,128)(2,1)}, bf16[384,2,768]{0,2,1:T(8,128)(2,1)}, u32[]{:S(2)}, u32[]{:S(2)}) collective-permute-start(bf16[384,2,768]{0,2,1:T(8,128)(2,1)} %copy.79), channel_id=1, source_target_pairs={{28,0},{0,4},{4,8},{8,12},{12,16},{16,20},{20,24},{24,28},{29,1},{... | collective-permute-start | bytes 3538952 | tf_op jit(solution)/shard_map/while/body/eval_jaxpr/ppermute | solution.py:15
  575.9 21.6 %copy-start.6 = (f32[384,768]{0,1:T(8,128)}, f32[384,768]{0,1:T(8,128)S(1)}, u32[]{:S(2)}) copy-start(f32[384,768]{0,1:T(8,128)S(1)} %bitcast_add_fusion.3) | copy-start | bytes 3538948 | tf_op jit(solution)/shard_map/while
  575.9 21.5 %copy-start.2 = (bf16[384,768]{0,1:T(8,128)(2,1)S(1)}, bf16[384,768]{0,1:T(8,128)(2,1)}, u32[]{:S(2)}) copy-start(bf16[384,768]{0,1:T(8,128)(2,1)} %copy-done.1) | copy-start | bytes 1769476 | tf_op jit(solution)/shard_map/while
  575.9 21.5 %copy-start.33 = (bf16[384,768]{0,1:T(8,128)(2,1)S(1)}, bf16[384,768]{0,1:T(8,128)(2,1)}, u32[]{:S(2)}) copy-start(bf16[384,768]{0,1:T(8,128)(2,1)} %copy-done.32) | copy-start | bytes 1769476 | tf_op jit(solution)/shard_map/while
  576.0 21.5 %copy-start.40 = (f32[12,384]{1,0:T(8,128)S(1)}, f32[12,384]{1,0:T(8,128)}, u32[]{:S(2)}) copy-start(f32[12,384]{1,0:T(8,128)} %get-tuple-element.639) | copy-start | bytes 55300 | tf_op jit(solution)/shard_map/while
  612.9 16.0 %collective-permute-start.1 = (bf16[384,2,768]{0,2,1:T(8,128)(2,1)}, bf16[384,2,768]{0,2,1:T(8,128)(2,1)}, u32[]{:S(2)}, u32[]{:S(2)}) collective-permute-start(bf16[384,2,768]{0,2,1:T(8,128)(2,1)} %fusion.143), channel_id=1, source_target_pairs={{28,0},{0,4},{4,8},{8,12},{12,16},{16,20},{20,24},{24,28},{29,1},{... | collective-permute-start | bytes 3538952 | tf_op jit(solution)/shard_map/while/body/eval_jaxpr/ppermute | solution.py:15
  615.4 26.1 %collective-permute-start = (bf16[384,2,768]{0,2,1:T(8,128)(2,1)}, bf16[384,2,768]{0,2,1:T(8,128)(2,1)}, u32[]{:S(2)}, u32[]{:S(2)}) collective-permute-start(bf16[384,2,768]{0,2,1:T(8,128)(2,1)} %copy.79), channel_id=1, source_target_pairs={{28,0},{0,4},{4,8},{8,12},{12,16},{16,20},{20,24},{24,28},{29,1},{... | collective-permute-start | bytes 3538952 | tf_op jit(solution)/shard_map/while/body/eval_jaxpr/ppermute | solution.py:15
  620.8 20.7 %copy-start.6 = (f32[384,768]{0,1:T(8,128)}, f32[384,768]{0,1:T(8,128)S(1)}, u32[]{:S(2)}) copy-start(f32[384,768]{0,1:T(8,128)S(1)} %bitcast_add_fusion.3) | copy-start | bytes 3538948 | tf_op jit(solution)/shard_map/while
  620.8 20.6 %copy-start.2 = (bf16[384,768]{0,1:T(8,128)(2,1)S(1)}, bf16[384,768]{0,1:T(8,128)(2,1)}, u32[]{:S(2)}) copy-start(bf16[384,768]{0,1:T(8,128)(2,1)} %copy-done.1) | copy-start | bytes 1769476 | tf_op jit(solution)/shard_map/while
  620.9 20.6 %copy-start.33 = (bf16[384,768]{0,1:T(8,128)(2,1)S(1)}, bf16[384,768]{0,1:T(8,128)(2,1)}, u32[]{:S(2)}) copy-start(bf16[384,768]{0,1:T(8,128)(2,1)} %copy-done.32) | copy-start | bytes 1769476 | tf_op jit(solution)/shard_map/while
  620.9 20.6 %copy-start.40 = (f32[12,384]{1,0:T(8,128)S(1)}, f32[12,384]{1,0:T(8,128)}, u32[]{:S(2)}) copy-start(f32[12,384]{1,0:T(8,128)} %get-tuple-element.639) | copy-start | bytes 55300 | tf_op jit(solution)/shard_map/while
  656.9 16.0 %collective-permute-start.1 = (bf16[384,2,768]{0,2,1:T(8,128)(2,1)}, bf16[384,2,768]{0,2,1:T(8,128)(2,1)}, u32[]{:S(2)}, u32[]{:S(2)}) collective-permute-start(bf16[384,2,768]{0,2,1:T(8,128)(2,1)} %fusion.143), channel_id=1, source_target_pairs={{28,0},{0,4},{4,8},{8,12},{12,16},{16,20},{20,24},{24,28},{29,1},{... | collective-permute-start | bytes 3538952 | tf_op jit(solution)/shard_map/while/body/eval_jaxpr/ppermute | solution.py:15
  659.4 26.1 %collective-permute-start = (bf16[384,2,768]{0,2,1:T(8,128)(2,1)}, bf16[384,2,768]{0,2,1:T(8,128)(2,1)}, u32[]{:S(2)}, u32[]{:S(2)}) collective-permute-start(bf16[384,2,768]{0,2,1:T(8,128)(2,1)} %copy.79), channel_id=1, source_target_pairs={{28,0},{0,4},{4,8},{8,12},{12,16},{16,20},{20,24},{24,28},{29,1},{... | collective-permute-start | bytes 3538952 | tf_op jit(solution)/shard_map/while/body/eval_jaxpr/ppermute | solution.py:15
  665.8 19.8 %copy-start.6 = (f32[384,768]{0,1:T(8,128)}, f32[384,768]{0,1:T(8,128)S(1)}, u32[]{:S(2)}) copy-start(f32[384,768]{0,1:T(8,128)S(1)} %bitcast_add_fusion.3) | copy-start | bytes 3538948 | tf_op jit(solution)/shard_map/while
  665.8 19.8 %copy-start.2 = (bf16[384,768]{0,1:T(8,128)(2,1)S(1)}, bf16[384,768]{0,1:T(8,128)(2,1)}, u32[]{:S(2)}) copy-start(bf16[384,768]{0,1:T(8,128)(2,1)} %copy-done.1) | copy-start | bytes 1769476 | tf_op jit(solution)/shard_map/while
  665.8 19.7 %copy-start.33 = (bf16[384,768]{0,1:T(8,128)(2,1)S(1)}, bf16[384,768]{0,1:T(8,128)(2,1)}, u32[]{:S(2)}) copy-start(bf16[384,768]{0,1:T(8,128)(2,1)} %copy-done.32) | copy-start | bytes 1769476 | tf_op jit(solution)/shard_map/while
  665.8 19.7 %copy-start.40 = (f32[12,384]{1,0:T(8,128)S(1)}, f32[12,384]{1,0:T(8,128)}, u32[]{:S(2)}) copy-start(f32[12,384]{1,0:T(8,128)} %get-tuple-element.639) | copy-start | bytes 55300 | tf_op jit(solution)/shard_map/while
  694.6 15.7 %collective-permute-start.2 = (bf16[384,2,768]{0,2,1:T(8,128)(2,1)S(1)}, bf16[384,2,768]{0,2,1:T(8,128)(2,1)S(1)}, u32[]{:S(2)}, u32[]{:S(2)}) collective-permute-start(bf16[384,2,768]{0,2,1:T(8,128)(2,1)S(1)} %fusion.25), channel_id=1, source_target_pairs={{28,0},{0,4},{4,8},{8,12},{12,16},{16,20},{20,24},{24,28},{29,1},{... | collective-permute-start | bytes 3538952 | tf_op jit(solution)/shard_map/ppermute | solution.py:15
  717.5 103.6 %reduce-scatter.7.cloned.1.call-start = ((), (), s32[]{:S(2)}) async-start(), calls=%async_computation.9 | async-start | bytes 1474560 | tf_op jit(solution)/shard_map/reduce_scatter | solution.py:280
  720.9 186.7 %reduce-scatter.11.cloned.1.call-start = ((), (), s32[]{:S(2)}) async-start(), calls=%async_computation.11 | async-start | bytes 5898240 | tf_op jit(solution)/shard_map/reduce_scatter | solution.py:298
  727.5 268.2 %reduce-scatter.9.cloned.1.call-start = ((), (), s32[]{:S(2)}) async-start(), calls=%async_computation.10 | async-start | bytes 5898240 | tf_op jit(solution)/shard_map/reduce_scatter | solution.py:292
  735.5 343.3 %all-reduce.23.cloned.1.call-start = ((), (), s32[]{:S(2)}) async-start(), calls=%async_computation.13 | async-start | bytes 7667712 | tf_op jit(solution)/shard_map/psum | solution.py:312
  791.7 205.3 %copy-start.65 = (bf16[192]{0:T(256)(128)(2,1)S(1)}, bf16[192]{0:T(256)(128)(2,1)}, u32[]{:S(2)}) copy-start(bf16[192]{0:T(256)(128)(2,1)} %param.32) | copy-start | bytes 1156
  791.7 205.5 %copy-start.23 = (bf16[384,768]{0,1:T(8,128)(2,1)S(1)}, bf16[384,768]{0,1:T(8,128)(2,1)}, u32[]{:S(2)}) copy-start(bf16[384,768]{0,1:T(8,128)(2,1)} %copy-done.22) | copy-start | bytes 1769476
  791.7 205.5 %copy-start.28 = (bf16[384,2,768]{0,2,1:T(8,128)(2,1)S(1)}, bf16[384,2,768]{0,2,1:T(8,128)(2,1)}, u32[]{:S(2)}) copy-start(bf16[384,2,768]{0,2,1:T(8,128)(2,1)} %copy-done.27) | copy-start | bytes 3538948
  997.6 37.2 %copy-start.9 = (f32[384,768]{1,0:T(8,128)S(1)}, f32[384,768]{1,0:T(8,128)}, u32[]{:S(2)}) copy-start(f32[384,768]{1,0:T(8,128)} %copy-done.8) | copy-start | bytes 3538948
  (99 other events, 319.9 us)
Sparse Core Ops, SparseCore 0:
  9.6 72.2 all-gather.6
  87.3 57.9 all-gather.8
  146.9 29.4 all-gather.10
  177.8 89.1 all-gather.12
  268.4 87.9 all-gather.14
  717.6 71.5 reduce-scatter.12
  791.5 29.4 reduce-scatter.6
  823.3 84.1 reduce-scatter.10
  909.9 85.7 reduce-scatter.8
  999.9 78.9 all-reduce.22
where the time goes:
time: 1100 us; the launch traced here: 1090 us
  waiting for transfers between devices  597 us (54%)
  matrix products  187 us (17%)
  local copies, waits for them, and re-layouts  127 us (12%)
  other arithmetic  75.6 us (7%)
  blocking collectives  58.3 us (5%)
  starting transfers between devices  28.6 us (3%)
  between operations  17.7 us (2%)
    ppermute x15, waiting for transfers between devices, passed_along(): return lax.ppermute(block, axis, route)  146 us
    reduce_scatter x1, waiting for transfers between devices, on_device(): lax.psum_scatter(local_grads[7].astype(jnp.bfloat16), 'fsdp', scatter_dim...  88.1 us
    reduce_scatter x1, waiting for transfers between devices, on_device(): lax.psum_scatter(local_grads[9].astype(jnp.bfloat16), 'fsdp', scatter_dim...  86.5 us
    all_gather x1, waiting for transfers between devices, on_device(): lax.all_gather(w_back, 'fsdp', axis=0, tiled=True)  65.9 us
    unnamed x11, waiting for transfers between devices  56.2 us
    all_gather x1, waiting for transfers between devices, on_device(): lax.all_gather(w_qkv, 'fsdp', axis=0, tiled=True)  48.8 us
    slice x2, local copies, waits for them, and re-layouts, forward_tile(): key_heads = key_pair[:, 0].reshape(key_rows, head_count, head_size)  39.3 us
    all_gather x1, waiting for transfers between devices, on_device(): pieces = lax.all_gather(key_pair, 'seq', axis=0, tiled=True)  38.6 us
  transfers between devices with their start and end apart: 25, of which 23 were waited for; matrix products, arithmetic and copies ran while one was open for 21% of the time, Pallas kernels for 0%

commit v1 on v0

--- a/solution.py
+++ b/solution.py
@@ -1,9 +1,982 @@
+import functools
+import math
+
 import jax
 import jax.numpy as jnp
 from jax import lax
+from jax.experimental import pallas as pl
+from jax.experimental.pallas import tpu as pltpu
 from jax.sharding import PartitionSpec as P
 
 HEADS = 12
+bf16 = jnp.bfloat16
+f32 = jnp.float32
+MESH = pl.DeviceIdType.MESH
+LOG2E = math.log2(math.e)
+NT = (((1,), (1,)), ((), ()))
+NN = (((1,), (0,)), ((), ()))
+
+PLANES = 4
+CHIPS = 4
+GROUP_HEADS = 3
+PACKED = (12, 24, 13, 25, 0, 1, 2, None, 14, 26)
+KV_TILE = (0, 1, 4)
+PACK = 640
+
+
+def dot(a, b, dims=NN):
+    return lax.dot_general(a, b, dims, preferred_element_type=f32)
+
+
+class Net:
+    def __init__(self, send_sems, recv_sems):
+        self.send_sems, self.recv_sems = send_sems, recv_sems
+        self.specs = {}
+
+    def add(self, name, src, dst, device):
+        self.specs[name] = (len(self.specs), src, dst, device)
+
+    def get(self, name):
+        k, src, dst, device = self.specs[name]
+        return pltpu.make_async_remote_copy(
+            src_ref=src(),
+            dst_ref=dst(),
+            send_sem=self.send_sems.at[k],
+            recv_sem=self.recv_sems.at[k],
+            device_id=device,
+            device_id_type=MESH,
+        )
+
+    def start(self, *names):
+        for name in names:
+            self.get(name).start()
+
+    def recv(self, *names):
+        for name in names:
+            self.get(name).wait_recv()
+
+    def sent(self, *names):
+        for name in names:
+            self.get(name).wait_send()
+
+
+class Local:
+    def __init__(self, sems):
+        self.sems = sems
+        self.specs = {}
+
+    def add(self, name, src, dst):
+        self.specs[name] = (len(self.specs), src, dst)
+
+    def get(self, name):
+        k, src, dst = self.specs[name]
+        return pltpu.make_async_copy(src(), dst(), self.sems.at[k])
+
+    def start(self, *names):
+        for name in names:
+            self.get(name).start()
+
+    def wait(self, *names):
+        for name in names:
+            self.get(name).wait()
+
+
+def coordinates():
+    s, z = lax.axis_index("seq"), lax.axis_index("fsdp")
+    core = lax.rem(s, 2)
+    chip = lax.div(s, 2)
+    return s, z, core, chip
+
+
+def flip(value, mask):
+    low, high = lax.rem(value, 2), lax.div(value, 2)
+    if mask & 1:
+        low = 1 - low
+    if mask & 2:
+        high = 1 - high
+    return high * 2 + low
+
+
+def hello(devices):
+    barrier = pltpu.get_barrier_semaphore()
+    for device in devices:
+        pl.semaphore_signal(barrier, inc=1, device_id=device, device_id_type=MESH)
+
+
+def met(count):
+    pl.semaphore_wait(pltpu.get_barrier_semaphore(), count)
+
+
+def greet(devices):
+    hello(devices)
+    met(len(devices))
+
+
+def lanes_of(rows=1):
+    return lax.broadcasted_iota(jnp.int32, (rows, 128), 1)
+
+
+def split3(column):
+    hi = column.astype(bf16).astype(f32)
+    mid = (column - hi).astype(bf16).astype(f32)
+    return hi, mid, column - hi - mid
+
+
+def forward_kernel(
+    length_ref, tok_ref, wraw_ref, win_ref, wback_ref, wout_ref, small_ref,
+    q_out, k_out, v_out, o_out, tok_out, att_out, small_out, win_full, wback_full, wout_full, wq_full,
+    tok, wqv, q_s, k_s, v_s, o_s, att, atts, kvs, kvr, small, wraw, wq_ref, send_sems, recv_sems, local_sems,
+):
+    s, z, core, chip = coordinates()
+    other = 1 - core
+    rows = tok_ref.shape[0]
+    half = rows // 2
+    shard = wq_ref.shape[1]
+    piece = shard // 2
+    peer = [None] + [(flip(chip, j) * 2 + core, z) for j in (1, 2, 3)]
+    mate = (chip * 2 + other, z)
+    plane = [None] + [(s, flip(z, dz)) for dz in (1, 2, 3)]
+    zs = [z] + [flip(z, dz) for dz in (1, 2, 3)]
+    net, loc = Net(send_sems, recv_sems), Local(local_sems)
+    width = win_full.shape[1] // 8
+    back = wback_full.shape[0] // PLANES
+    bpiece = back // 8
+    arrays = ("out", "in", "back", "qkv")
+
+    def part(a, zz, m, c):
+        if a == "in":
+            return win_full.at[pl.ds(pl.multiple_of(zz * shard, 16), shard), pl.ds(pl.multiple_of((m * 4 + c) * width, 128), width)]
+        if a == "back":
+            return wback_full.at[pl.ds(pl.multiple_of(zz * back + (m * 4 + c) * bpiece, 16), bpiece), :]
+        if a == "out":
+            return wout_full.at[pl.ds(pl.multiple_of(zz * shard + c * (shard // 4), 16), shard // 4), pl.ds(pl.multiple_of(m * width, 128), width)]
+        return wq_full.at[zz, m * 2 + lax.div(c, 2), pl.ds(pl.multiple_of(lax.rem(c, 2) * piece, 16), piece), :]
+
+    def own_part(a, m, c):
+        if a == "in":
+            return win_ref.at[:, pl.ds(pl.multiple_of((m * 4 + c) * width, 128), width)]
+        if a == "back":
+            return wback_ref.at[pl.ds(pl.multiple_of((m * 4 + c) * bpiece, 16), bpiece), :]
+        if a == "out":
+            return wout_ref.at[pl.ds(pl.multiple_of(c * (shard // 4), 16), shard // 4), pl.ds(pl.multiple_of(m * width, 128), width)]
+        return wq_ref.at[m * 2 + lax.div(c, 2), pl.ds(pl.multiple_of(lax.rem(c, 2) * piece, 16), piece), :]
+
+    def side(a, zz, m):
+        if a == "in":
+            return win_full.at[pl.ds(pl.multiple_of(zz * shard, 16), shard), pl.ds(pl.multiple_of(m * 4 * width, 128), 4 * width)]
+        if a == "back":
+            return wback_full.at[pl.ds(pl.multiple_of(zz * back + m * 4 * bpiece, 16), 4 * bpiece), :]
+        if a == "out":
+            return wout_full.at[pl.ds(pl.multiple_of(zz * shard, 16), shard), pl.ds(pl.multiple_of(m * width, 128), width)]
+        return wq_full.at[zz, pl.ds(m * 2, 2)]
+
+    for dz in (1, 2, 3):
+        net.add(("wq", dz), lambda: wq_ref.at[chip, pl.ds(pl.multiple_of(core * piece, 16), piece), :],
+                lambda: wqv.at[pl.ds(pl.multiple_of(z * shard + core * piece, 16), piece), :], plane[dz])
+        net.add(("wqm", dz), lambda dz=dz: wqv.at[pl.ds(pl.multiple_of(zs[dz] * shard + core * piece, 16), piece), :],
+                lambda dz=dz: wqv.at[pl.ds(pl.multiple_of(zs[dz] * shard + core * piece, 16), piece), :], mate)
+        net.add(("small", dz), lambda: small_ref, lambda: small.at[z], plane[dz])
+    top, bottom = slice(0, half), slice(half, rows)
+    net.add("t1a", lambda: tok_ref.at[top], lambda: tok.at[1, top], peer[1])
+    net.add("t1b", lambda: tok_ref.at[bottom], lambda: tok.at[1, bottom], peer[1])
+    net.add("t2b", lambda: tok_ref.at[bottom], lambda: tok.at[2, bottom], peer[2])
+    net.add("t2a", lambda: tok_ref.at[top], lambda: tok.at[2, top], peer[2])
+    net.add("t3a", lambda: tok.at[1, top], lambda: tok.at[3, top], peer[2])
+    net.add("t3b", lambda: tok.at[2, bottom], lambda: tok.at[3, bottom], peer[1])
+    for j in range(4):
+        net.add(("kv", j), lambda j=j: kvs.at[j], lambda j=j: kvr.at[j], mate)
+    for j in (1, 2, 3):
+        net.add(("att0", j), lambda j=j: atts.at[j, :, 0:128], lambda: att.at[chip, :, 0:128], peer[j])
+        net.add(("att1", j), lambda j=j: atts.at[j, :, 128:256], lambda: att.at[chip, :, 128:256], peer[j])
+    for a in arrays:
+        via, last = (1, 2) if a in ("in", "qkv") else (2, 1)
+        for dz in (1, 2, 3):
+            net.add((a, "z", dz), lambda a=a: own_part(a, core, chip), lambda a=a: part(a, z, core, chip), plane[dz])
+            for j in (1, 2):
+                net.add((a, j, dz), lambda a=a, dz=dz: part(a, zs[dz], core, chip), lambda a=a, dz=dz: part(a, zs[dz], core, chip), peer[j])
+            net.add((a, 3, dz), lambda a=a, dz=dz, via=via: part(a, zs[dz], core, flip(chip, via)),
+                    lambda a=a, dz=dz, via=via: part(a, zs[dz], core, flip(chip, via)), peer[last])
+            net.add((a, "m", dz), lambda a=a, dz=dz: side(a, zs[dz], core), lambda a=a, dz=dz: side(a, zs[dz], core), mate)
+    loc.add("raw", lambda: wraw_ref, lambda: wraw)
+    loc.add("tok", lambda: tok_ref, lambda: tok.at[0])
+    loc.add("wq", lambda: wq_ref.at[chip], lambda: wqv.at[pl.ds(pl.multiple_of(z * shard, 16), shard), :])
+    loc.add("small", lambda: small_ref, lambda: small.at[z])
+    loc.add("in", lambda: win_ref, lambda: win_full.at[pl.ds(pl.multiple_of(z * shard, 16), shard), :])
+    loc.add("back", lambda: wback_ref, lambda: wback_full.at[pl.ds(pl.multiple_of(z * back, 16), back), :])
+    loc.add("out", lambda: wout_ref, lambda: wout_full.at[pl.ds(pl.multiple_of(z * shard, 16), shard), :])
+    loc.add("qkv", lambda: wq_ref, lambda: wq_full.at[z])
+    outs = (("k_o", k_s, k_out), ("v_o", v_s, v_out), ("q_o", q_s, q_out), ("o_o", o_s, o_out),
+            ("tok_o", tok, tok_out), ("att_o", att, att_out), ("small_o", small, small_out))
+    for name, src, dst in outs:
+        loc.add(name, lambda src=src: src, lambda dst=dst: dst)
+
+    loc.start("raw", "tok", "small")
+    hello(peer[1:] + [mate] + plane[1:])
+    lane = lanes_of()
+    loc.wait("raw")
+    for g in range(CHIPS):
+        for t in range(PACK // 128):
+            halves = []
+            for upper in (0, 1):
+                block = PACKED[2 * t + upper]
+                if block is None:
+                    halves.append(0.0)
+                    continue
+                block += GROUP_HEADS * g
+                tile_of = lambda i: wraw[:, i * 128 : (i + 1) * 128].astype(f32)
+                halves.append(half_tile(tile_of, block, upper))
+            wq_ref[g, :, t * 128 : (t + 1) * 128] = jnp.where(lane < 64, halves[0], halves[1]).astype(bf16)
+    loc.start("wq")
+    met(len(peer[1:] + [mate] + plane[1:]))
+    net.start(*[("wq", dz) for dz in (1, 2, 3)], *[("small", dz) for dz in (1, 2, 3)])
+    net.start("t1a", "t2b", "t1b", "t2a")
+    loc.start(*arrays)
+    for dz in (1, 2, 3):
+        net.recv(("wq", dz))
+        net.start(("wqm", dz))
+    for dz in (1, 2, 3):
+        net.start(*[(a, "z", dz) for a in arrays])
+    loc.wait("tok", "wq", "small")
+    for dz in (1, 2, 3):
+        net.recv(("small", dz), ("wqm", dz))
+
+    length = length_ref[0]
+    bias = small[chip, 7:8, 0:PACK].astype(f32)
+
+    def keep(tile, h, slot, block):
+        position = block * rows + lax.broadcasted_iota(jnp.int32, (rows, 1), 0)
+        mask = jnp.where(position < length, 0.0, -1e30).astype(f32)
+        ones = jnp.where((lane > 64) & (lane < 68), 1.0, 0.0)
+        k_s[h, slot * rows : (slot + 1) * rows, :] = jnp.where(
+            lane < 64, tile, jnp.where(lane == 64, mask, ones)
+        ).astype(bf16)
+        v_s[h, slot * rows : (slot + 1) * rows, :] = jnp.where(
+            lane < 64, pltpu.roll(tile, 64, 1), jnp.where(lane < 67, 1.0, 0.0)
+        ).astype(bf16)
+
+    def project(j):
+        proj = dot(tok[j], wqv[...]) + bias
+        for h in range(GROUP_HEADS):
+            tile = proj[:, KV_TILE[h] * 128 : (KV_TILE[h] + 1) * 128]
+            keep(tile.astype(bf16).astype(f32), h, j, flip(chip, j) * 2 + core)
+            kvs[j, :, h * 128 : (h + 1) * 128] = tile.astype(bf16)
+            first = 256 + (h // 2) * 128
+            tile = proj[:, first : first + 128].astype(bf16).astype(f32) * 0.125
+            if h == 1:
+                tile = pltpu.roll(tile, 64, 1)
+            q_s[h, j * rows : (j + 1) * rows, :] = jnp.where(
+                lane < 64, tile, jnp.where(lane == 64, 1.0, 0.0)
+            ).astype(bf16)
+        net.start(("kv", j))
+
+    def keep_other(j):
+        net.recv(("kv", j))
+        for h in range(GROUP_HEADS):
+            tile = kvr[j, :, h * 128 : (h + 1) * 128].astype(f32)
+            keep(tile, h, 4 + j, flip(chip, j) * 2 + other)
+
+    project(0)
+    net.recv("t1a")
+    net.start("t3a")
+    net.recv("t2b")
+    net.start("t3b")
+    net.recv("t1b")
+    project(1)
+    net.recv("t2a")
+    project(2)
+    keep_other(0)
+    keep_other(1)
+    keep_other(2)
+    net.recv("t3a", "t3b")
+    project(3)
+    keep_other(3)
+    loc.start("k_o", "v_o", "tok_o", "small_o")
+
+    query_tile, key_chunk = 512, 1024
+    tiles = 4 * rows // query_tile
+    chunks = 8 * rows // key_chunk
+
+    def first_hop(dz):
+        for a in arrays:
+            net.recv((a, "z", dz))
+            net.start((a, 1, dz), (a, 2, dz))
+
+    def second_hop(dz):
+        for a in arrays:
+            net.recv((a, 1, dz), (a, 2, dz))
+            net.start((a, 3, dz))
+
+    def third_hop(dz):
+        for a in arrays:
+            net.recv((a, 3, dz))
+            net.start((a, "m", dz))
+
+    def attended_tile(which):
+        for j in range(4):
+            r = slice(j * rows, (j + 1) * rows)
+            if which == 0:
+                upper = pltpu.roll(o_s[1, r, :].astype(f32), 64, 1)
+                value = jnp.where(lane < 64, o_s[0, r, :].astype(f32), upper)
+            else:
+                value = jnp.where(lane < 64, o_s[2, r, :].astype(f32), 0.0)
+            place = slice(which * 128, (which + 1) * 128)
+            if j == 0:
+                att[chip, :, place] = value.astype(bf16)
+            else:
+                atts[j, :, place] = value.astype(bf16)
+                net.start((f"att{which}", j))
+
+    def visit(t, carry):
+        h, i = lax.div(t, tiles), lax.rem(t, tiles)
+        qrows = pl.ds(pl.multiple_of(i * query_tile, query_tile), query_tile)
+        q = q_s[h, qrows, :]
+        top_score = jnp.full((query_tile, 1), -1e30, f32)
+        acc = jnp.zeros((query_tile, 128), f32)
+        for c in range(chunks):
+            krows = slice(c * key_chunk, (c + 1) * key_chunk)
+            scores = dot(q, k_s[h, krows, :], NT)
+            new_top = jnp.maximum(top_score, jnp.max(scores, axis=1, keepdims=True))
+            probs = jnp.exp2((scores - new_top) * LOG2E)
+            fade = jnp.exp2((top_score - new_top) * LOG2E)
+            acc = acc * fade + dot(probs.astype(bf16), v_s[h, krows, :])
+            top_score = new_top
+        total = acc[:, 64:65]
+        o_s[h, qrows, :] = (acc / total).astype(bf16)
+        hi, mid, low = split3(-(top_score + jnp.log(total)))
+        wide = q.astype(f32)
+        wide = jnp.where(lane == 65, hi, jnp.where(lane == 66, mid, jnp.where(lane == 67, low, wide)))
+        q_s[h, qrows, :] = wide.astype(bf16)
+
+        for at, work in enumerate((
+            lambda: first_hop(1), lambda: None, lambda: first_hop(2), lambda: second_hop(1),
+            lambda: first_hop(3), lambda: (second_hop(2), attended_tile(0)), lambda: third_hop(1), lambda: second_hop(3),
+            lambda: (attended_tile(1), third_hop(2)),
+        )):
+            pl.when(t == at)(lambda work=work: (work(), None)[1])
+        return carry
+
+    lax.fori_loop(0, GROUP_HEADS * tiles, visit, 0)
+    third_hop(3)
+    loc.start("q_o", "o_o")
+    for j in (1, 2, 3):
+        net.recv(("att0", j), ("att1", j))
+    loc.start("att_o")
+    for dz in (1, 2, 3):
+        for a in arrays:
+            net.recv((a, "m", dz))
+    for name in net.specs:
+        net.sent(name)
+    loc.wait(*arrays, *[name for name, _, _ in outs])
+
+
+def backward_kernel(
+    do_ref, q_ref, k_ref, v_ref, o_ref, tok_ref, grads_ref, sums_ref,
+    dproj_out, gw_out, fin_out, sums_out,
+    do_s, q_s, k_s, v_s, o_s, doa, tok, tokt, dqs, dq_keep, kv_own, kvs, kvr, dall, dproj,
+    gw, gwr, gz, gzr, gwf, acc, rb, rx, ry, rx2, ry2, rz, fin, sums, sums_r, sums_z, sums_f,
+    send_sems, recv_sems, local_sems,
+):
+    s, z, core, chip = coordinates()
+    other = 1 - core
+    rows = do_ref.shape[1]
+    peer = [None] + [(flip(chip, j) * 2 + core, z) for j in (1, 2, 3)]
+    mate = (chip * 2 + other, z)
+    plane = [None] + [(s, flip(z, dz)) for dz in (1, 2, 3)]
+    zs = [z] + [flip(z, dz) for dz in (1, 2, 3)]
+    ch = [chip] + [flip(chip, j) for j in (1, 2, 3)]
+    net, loc = Net(send_sems, recv_sems), Local(local_sems)
+    length = grads_ref.shape[3]
+    cut = length // 32 * 16
+    xs, ys = slice(0, cut), slice(cut, length)
+    shard = tok.shape[2] // PLANES
+    piece = shard // 2
+
+    for j in (1, 2, 3):
+        net.add(("do", j), lambda j=j: do_ref.at[ch[j]], lambda j=j: do_s.at[j], peer[j])
+    for h in range(GROUP_HEADS):
+        net.add(("kv", h), lambda h=h: kvs.at[h], lambda h=h: kvr.at[h], mate)
+        place = ((0, 128), (128, 384), (384, 640))[h]
+        for j in (1, 2, 3):
+            net.add(("dp", h, j), lambda j=j, place=place: dall.at[j, :, place[0] : place[1]],
+                    lambda place=place: dproj.at[chip, :, place[0] : place[1]], peer[j])
+    order = (3, 2, 1, 0)
+    for dz in order:
+        net.add(("r1", dz), lambda dz=dz: grads_ref.at[other, zs[dz]], lambda dz=dz: rb.at[zs[dz]], mate)
+        for n, j in enumerate((1, 3)):
+            net.add(("x1", n, dz), lambda dz=dz, j=j: acc.at[zs[dz], ch[j], xs], lambda dz=dz, n=n: rx.at[zs[dz], n], peer[1])
+        net.add(("x2", dz), lambda dz=dz: acc.at[zs[dz], ch[2], xs], lambda dz=dz: rx2.at[zs[dz]], peer[2])
+        for n, j in enumerate((2, 3)):
+            net.add(("y1", n, dz), lambda dz=dz, j=j: acc.at[zs[dz], ch[j], ys], lambda dz=dz, n=n: ry.at[zs[dz], n], peer[2])
+        net.add(("y2", dz), lambda dz=dz: acc.at[zs[dz], ch[1], ys], lambda dz=dz: ry2.at[zs[dz]], peer[1])
+        if dz:
+            net.add(("rz", dz), lambda dz=dz: acc.at[zs[dz], chip], lambda dz=dz: rz.at[dz - 1], plane[dz])
+    net.add("f1", lambda: fin.at[core, chip], lambda: fin.at[core, chip], peer[1])
+    net.add("f2", lambda: fin.at[core, chip], lambda: fin.at[core, chip], peer[2])
+    net.add("f3x", lambda: fin.at[core, ch[1], xs], lambda: fin.at[core, ch[1], xs], peer[2])
+    net.add("f3y", lambda: fin.at[core, ch[2], ys], lambda: fin.at[core, ch[2], ys], peer[1])
+    net.add("fm", lambda: fin.at[core], lambda: fin.at[core], mate)
+    net.add("s0", lambda: sums_ref, lambda: sums_r.at[0], mate)
+    net.add("s1", lambda: sums.at[1], lambda: sums_r.at[1], peer[1])
+    net.add("s2", lambda: sums.at[2], lambda: sums_r.at[2], peer[2])
+    for dz in (1, 2, 3):
+        net.add(("sz", dz), lambda dz=dz: sums.at[3, zs[dz]], lambda dz=dz: sums_z.at[dz - 1], plane[dz])
+    net.add("g0", lambda: gw.at[other], lambda: gwr, mate)
+    for dz in (1, 2, 3):
+        net.add(("gz", dz), lambda dz=dz: gz.at[zs[dz]], lambda dz=dz: gzr.at[dz - 1], plane[dz])
+    for j in (1, 2, 3):
+        net.add(("gf", j), lambda: gwf.at[core, chip], lambda: gwf.at[core, chip], peer[j])
+    net.add("gm", lambda: gwf.at[core], lambda: gwf.at[core], mate)
+
+    loads = (("do", lambda: do_ref.at[chip], lambda: do_s.at[0]), ("o", lambda: o_ref, lambda: o_s),
+             ("tok", lambda: tok_ref, lambda: tok), ("q", lambda: q_ref, lambda: q_s),
+             ("k", lambda: k_ref, lambda: k_s), ("v", lambda: v_ref, lambda: v_s),
+             ("sums", lambda: sums_ref, lambda: sums.at[0]), ("acc", lambda: grads_ref.at[core], lambda: acc))
+    for name, src, dst in loads:
+        loc.add(name, src, dst)
+    stores = (("dp_o", dproj, dproj_out), ("gw_o", gwf, gw_out), ("fin_o", fin, fin_out))
+    for name, src, dst in stores:
+        loc.add(name, lambda src=src: src, lambda dst=dst: dst)
+    loc.add("sums_o", lambda: sums_f, lambda: sums_out)
+
+    loc.start(*[name for name, _, _ in loads])
+    greet(peer[1:] + [mate] + plane[1:])
+    net.start(*[("do", j) for j in (1, 2, 3)])
+    net.start("s0", *[("r1", dz) for dz in order])
+    lane = lanes_of()
+    loc.wait("tok")
+    for j in range(4):
+        tokt[:, j * rows : (j + 1) * rows] = tok[j].T
+    loc.wait("do", "o", "q", "k", "v", "sums", "acc")
+    for j in range(4):
+        if j:
+            net.recv(("do", j))
+        for h in range(GROUP_HEADS):
+            tile = do_s[j, :, (h // 2) * 128 : (h // 2) * 128 + 128].astype(f32)
+            if h == 1:
+                tile = pltpu.roll(tile, 64, 1)
+            tile = jnp.where(lane < 64, tile, 0.0)
+            r = slice(j * rows, (j + 1) * rows)
+            delta = jnp.sum(tile * o_s[h, r, :].astype(f32), axis=1, keepdims=True)
+            hi, mid, low = split3(-delta)
+            tile = jnp.where(lane == 64, hi, jnp.where(lane == 65, mid, jnp.where(lane == 66, low, tile)))
+            doa[h, r, :] = tile.astype(bf16)
+
+    def add_into(ref, index, other_ref, other_index):
+        ref[index] = (ref[index].astype(f32) + other_ref[other_index].astype(f32)).astype(bf16)
+
+    def step_one(dz):
+        net.recv(("r1", dz))
+        def body(c, carry):
+            add_into(acc, (zs[dz], c), rb, (zs[dz], c))
+            return carry
+        lax.fori_loop(0, CHIPS, body, 0)
+        net.start(*[("x1", n, dz) for n in (0, 1)], *[("y1", n, dz) for n in (0, 1)])
+
+    def step_two(dz):
+        for n in range(2):
+            net.recv(("x1", 1 - n, dz), ("y1", 1 - n, dz))
+            jx, jy = (2, 1) if n == 0 else (0, 0)
+            add_into(acc, (zs[dz], ch[jx], xs), rx, (zs[dz], 1 - n))
+            add_into(acc, (zs[dz], ch[jy], ys), ry, (zs[dz], 1 - n))
+            if n == 0:
+                net.start(("x2", dz), ("y2", dz))
+
+    def step_three(dz):
+        net.recv(("x2", dz), ("y2", dz))
+        add_into(acc, (zs[dz], chip, xs), rx2, zs[dz])
+        add_into(acc, (zs[dz], chip, ys), ry2, zs[dz])
+        if dz:
+            net.start(("rz", dz))
+
+    def sums_step(n):
+        net.recv(f"s{n}")
+        sums[n + 1] = (sums[n].astype(f32) + sums_r[n].astype(f32)).astype(bf16)
+        if n < 2:
+            net.start(f"s{n + 1}")
+        else:
+            net.start(*[("sz", dz) for dz in (1, 2, 3)])
+
+    key_chunk, query_tile = 2 * rows, 256
+    per_head = 4
+
+    def head_end(h):
+        net.recv(("kv", h))
+        tile = KV_TILE[h]
+        dst = (0, 1, 4)[h] * 128
+        for j in range(4):
+            r = slice(j * rows, (j + 1) * rows)
+            both = kv_own[r, :] + kvr[h, r, :].astype(f32)
+            dall[j, :, dst : dst + 128] = both.astype(bf16)
+        dq = dqs[...].T * 0.125
+        for j in range(4):
+            r = slice(j * rows, (j + 1) * rows)
+            mine = dq[r, :]
+            if h == 0:
+                dq_keep[r, :] = mine
+            elif h == 1:
+                dall[j, :, 256:384] = jnp.where(lane < 64, dq_keep[r, :], pltpu.roll(mine, 64, 1)).astype(bf16)
+            else:
+                dall[j, :, 384:512] = jnp.where(lane < 64, mine, 0.0).astype(bf16)
+        for j in (1, 2, 3):
+            net.start(("dp", h, j))
+
+    stages = {
+        0: lambda: (step_one(3), sums_step(0)),
+        1: lambda: (step_one(2), sums_step(1)),
+        2: lambda: (step_two(3), sums_step(2)),
+        3: lambda: step_one(1),
+        4: lambda: (step_three(3), step_two(2)),
+        5: lambda: step_one(0),
+        6: lambda: (step_three(2), step_two(1)),
+        8: lambda: step_two(0),
+        9: lambda: step_three(1),
+        11: lambda: step_three(0),
+    }
+
+    def visit(t, carry):
+        h, part = lax.div(t, per_head), lax.rem(t, per_head)
+        start = pl.multiple_of(lax.rem(part + 2, 4) * key_chunk, key_chunk)
+        krows = pl.ds(start, key_chunk)
+        k, v = k_s[h, krows, :], v_s[h, krows, :]
+        kt = k.T
+
+        @pl.when(part == 0)
+        def _():
+            dqs[...] = jnp.zeros_like(dqs)
+
+        dk = jnp.zeros((key_chunk, 128), f32)
+        dv = jnp.zeros((key_chunk, 128), f32)
+        for i in range(4 * rows // query_tile):
+            r = slice(i * query_tile, (i + 1) * query_tile)
+            q, do = q_s[h, r, :], doa[h, r, :]
+            probs = jnp.exp2(dot(k, q, NT) * LOG2E)
+            dscores = (probs * dot(v, do, NT)).astype(bf16)
+            dv = dv + dot(probs.astype(bf16), do)
+            dk = dk + dot(dscores, q)
+            dqs[:, r] += dot(kt, dscores)
+        packed = jnp.where(lane < 64, dk, pltpu.roll(dv, 64, 1))
+
+        @pl.when(part < 2)
+        def _():
+            kvs[h, pl.ds(pl.multiple_of(part * key_chunk, key_chunk), key_chunk), :] = packed.astype(bf16)
+
+        @pl.when(part >= 2)
+        def _():
+            kv_own[pl.ds(pl.multiple_of((part - 2) * key_chunk, key_chunk), key_chunk), :] = packed
+
+        for hh in range(GROUP_HEADS):
+            @pl.when(t == hh * per_head + 1)
+            def _(hh=hh):
+                net.start(("kv", hh))
+
+            @pl.when(t == hh * per_head + 3)
+            def _(hh=hh):
+                head_end(hh)
+        for at, work in stages.items():
+            pl.when(t == at)(lambda work=work: (work(), None)[1])
+        return carry
+
+    lax.fori_loop(0, GROUP_HEADS * per_head, visit, 0)
+
+    dproj[chip] = dall[0]
+    d_cols = dall[...].reshape(4 * rows, PACK)
+    column_sums = jnp.sum(d_cols.astype(f32), axis=0, keepdims=True)
+    extra = jnp.where(lax.broadcasted_iota(jnp.int32, (16, 1), 0) == 0, column_sums, 0.0).astype(bf16)
+    for zz in range(PLANES):
+        part = dot(tokt[zz * shard : (zz + 1) * shard, :], d_cols)
+        for m in range(2):
+            gw[m, zz, 0:piece, :] = part[m * piece : (m + 1) * piece, :].astype(bf16)
+            gw[m, zz, piece : piece + 16, :] = extra
+    net.start("g0")
+
+    for dz in (1, 2, 3):
+        net.recv(("rz", dz), ("sz", dz))
+    total = acc[z, chip].astype(f32) + rz[0].astype(f32) + rz[1].astype(f32) + rz[2].astype(f32)
+    fin[core, chip] = total.astype(bf16)
+    net.start("f1", "f2")
+    total = sums[3, z].astype(f32)
+    for n in range(3):
+        total = total + sums_z[n].astype(f32)
+    sums_f[...] = total.astype(bf16)
+    loc.start("sums_o")
+
+    net.recv("g0")
+    for zz in range(PLANES):
+        gz[zz] = (gw[core, zz].astype(f32) + gwr[zz].astype(f32)).astype(bf16)
+    net.start(*[("gz", dz) for dz in (1, 2, 3)])
+    for h in range(GROUP_HEADS):
+        for j in (1, 2, 3):
+            net.recv(("dp", h, j))
+    loc.start("dp_o")
+    net.recv("f1")
+    net.start("f3x")
+    net.recv("f2")
+    net.start("f3y")
+    total = gz[z].astype(f32)
+    for dz in (1, 2, 3):
+        net.recv(("gz", dz))
+        total = total + gzr[dz - 1].astype(f32)
+    gwf[core, chip] = total.astype(bf16)
+    net.start(*[("gf", j) for j in (1, 2, 3)])
+    net.recv("f3x", "f3y")
+    net.start("fm")
+    net.recv(*[("gf", j) for j in (1, 2, 3)])
+    net.start("gm")
+    net.recv("fm", "gm")
+    loc.start("gw_o", "fin_o")
+    for name in net.specs:
+        net.sent(name)
+    loc.wait("dp_o", "gw_o", "fin_o", "sums_o")
+
+
+def gelu_parts(u):
+    x = jnp.abs(u) * (0.5 ** 0.5)
+    d = 1.0 + 0.3275911 * x
+    t = pl.reciprocal(d, approx=True)
+    t = t * (2.0 - d * t)
+    poly = t * (0.254829592 + t * (-0.284496736 + t * (1.421413741 + t * (-1.453152027 + t * 1.061405429))))
+    bell = jnp.exp2(u * u * (-0.5 * LOG2E))
+    tail = 0.5 * poly * bell
+    phi = jnp.where(u >= 0, 1.0 - tail, tail)
+    return u * phi, phi + u * bell * (1.0 / math.sqrt(2.0 * math.pi))
+
+
+def row_mean(a):
+    return jnp.mean(a, axis=1, keepdims=True)
+
+
+def wide_vectors(small):
+    total = small[0].astype(f32)[0:8]
+    step = small.shape[2] // PLANES
+    lane = lax.broadcasted_iota(jnp.int32, total.shape, 1)
+    total = jnp.where(lane < step, total, 0.0)
+    for zz in range(1, PLANES):
+        part = jnp.where(lane < step, small[zz].astype(f32)[0:8], 0.0)
+        total = total + pltpu.roll(part, zz * step, 1)
+    return total
+
+
+def ffn_kernel(
+    length_ref, att_ref, tok_ref, cot_ref, win_ref, wback_ref, wout_ref, small_ref,
+    out_ref, gh1_ref, do_ref, grads_ref, sums_ref,
+    winv, wbackv, woutv, act_s, gp_s, gi_s, acc, first_s, n1_s, low_s, lowt_s, gsec_s, gh2_s, isum, local_sems,
+):
+    s = lax.axis_index("seq")
+    rows, width = tok_ref.shape
+    step = width // PLANES
+    ch = winv.shape[1] // 8
+    loc = Local(local_sems)
+    loc.add("out", lambda: wout_ref, lambda: woutv)
+    for n in range(8):
+        loc.add(("in", n), lambda n=n: win_ref.at[:, n * ch : (n + 1) * ch], lambda n=n: winv.at[:, n * ch : (n + 1) * ch])
+        loc.add(("back", n), lambda n=n: wback_ref.at[n * ch : (n + 1) * ch, :], lambda n=n: wbackv.at[n * ch : (n + 1) * ch, :])
+    loc.start("out")
+    for n in range(8):
+        loc.start(("in", n), ("back", n))
+    vectors = wide_vectors(small_ref)
+    vec = lambda i: vectors[i : i + 1, :]
+    loc.wait("out")
+    branch = vec(0)
+    for g in range(4):
+        branch = branch + dot(att_ref[g, :, 0:step], woutv[g * step : (g + 1) * step, :])
+    hidden = tok_ref[...].astype(f32) + branch
+    centred = hidden - row_mean(hidden)
+    inverse1 = lax.rsqrt(row_mean(centred * centred) + 1e-5)
+    normed = centred * inverse1
+    n1_s[...] = normed
+    first = normed * vec(1) + vec(2)
+    first_s[...] = first
+    low_s[...] = first.astype(bf16)
+    lowt_s[...] = first.astype(bf16).T
+    acc[...] = jnp.zeros_like(acc)
+    for n in range(8):
+        loc.wait(("in", n), ("back", n))
+
+    def forward(n, carry):
+        cols = pl.ds(pl.multiple_of(n * ch, 128), ch)
+        bias = small_ref[lax.div(n, 2), 6:7, pl.ds(pl.multiple_of(lax.rem(n, 2) * ch, 128), ch)].astype(f32)
+        inner = dot(low_s[...], winv[:, cols]) + bias
+        value, slope = gelu_parts(inner)
+        value = value.astype(bf16)
+        act_s[n] = value
+        gp_s[n] = slope
+        acc[...] += dot(value, wbackv[cols, :])
+        return carry
+
+    lax.fori_loop(0, 8, forward, 0)
+    position = s * rows + lax.broadcasted_iota(jnp.int32, (rows, 1), 0)
+    valid = (position < length_ref[0]).astype(f32)
+    hidden = first_s[...] + acc[...] + vec(3)
+    centred = hidden - row_mean(hidden)
+    inverse = lax.rsqrt(row_mean(centred * centred) + 1e-5)
+    normed = centred * inverse
+    out_ref[...] = ((normed * vec(4) + vec(5)) * valid).astype(bf16)
+    grad = cot_ref[...].astype(f32) * valid
+    sum_rows = lambda a: jnp.sum(a, axis=0, keepdims=True)
+    g2_gain, g2_bias = sum_rows(grad * normed), sum_rows(grad)
+    scaled = grad * vec(4)
+    gh2 = inverse * (scaled - row_mean(scaled) - normed * row_mean(scaled * normed))
+    gh2_s[...] = gh2
+    second = gh2.astype(bf16)
+    gsec_s[...] = second
+    back_sum = sum_rows(second.astype(f32))
+    acc[...] = jnp.zeros_like(acc)
+
+    def backward(n, carry):
+        cols = pl.ds(pl.multiple_of(n * ch, 128), ch)
+        grad_inner = (dot(gsec_s[...], wbackv[cols, :], NT) * gp_s[n]).astype(bf16)
+        gi_s[n] = grad_inner
+        isum[n] = jnp.broadcast_to(sum_rows(grad_inner.astype(f32)), (8, ch))
+        acc[...] += dot(grad_inner, winv[:, cols], NT)
+        return carry
+
+    lax.fori_loop(0, 8, backward, 0)
+    grad = gh2_s[...] + acc[...]
+    normed = n1_s[...]
+    g1_gain, g1_bias = sum_rows(grad * normed), sum_rows(grad)
+    scaled = grad * vec(1)
+    gh1 = inverse1 * (scaled - row_mean(scaled) - normed * row_mean(scaled * normed))
+    gh1_ref[...] = gh1
+    gbranch = gh1.astype(bf16)
+    out_sum = sum_rows(gbranch.astype(f32))
+    for g in range(4):
+        w = woutv[g * step : (g + 1) * step, :]
+        do_ref[g, :, 0:step] = dot(gbranch, w, NT).astype(bf16)
+        do_ref[g, :, step:] = jnp.zeros((rows, do_ref.shape[2] - step), bf16)
+        gw = dot(att_ref[g, :, 0:step].T, gbranch).astype(bf16)
+        part = step // 4
+        for c in range(4):
+            for m in range(2):
+                grads_ref[m, g, c, step + 2 * 96 :, :] = gw[c * part : (c + 1) * part, m * ch : (m + 1) * ch]
+
+    def weights(n, carry):
+        gback = dot(act_s[n].T, gsec_s[...]).astype(bf16)
+        part = ch // 4
+        for k in range(4):
+            for x in range(2):
+                grads_ref[lax.rem(n, 2), lax.div(n, 2), k, step + x * part : step + (x + 1) * part, :] = gback[
+                    k * part : (k + 1) * part, x * ch : (x + 1) * ch
+                ]
+        for zz in range(PLANES):
+            gin = dot(lowt_s[zz * step : (zz + 1) * step, :], gi_s[n])
+            grads_ref[lax.div(n, 4), zz, lax.rem(n, 4), 0:step, :] = gin.astype(bf16)
+        return carry
+
+    lax.fori_loop(0, 8, weights, 0)
+    lane = lax.broadcasted_iota(jnp.int32, (8, width), 1)
+    place = lax.broadcasted_iota(jnp.int32, (8, width), 0)
+    total = jnp.zeros((8, width), f32)
+    for i, v in enumerate((out_sum, g1_gain, g1_bias, back_sum, g2_gain, g2_bias)):
+        total = jnp.where(place == i, v, total)
+    for zz in range(PLANES):
+        part = total if zz == 0 else pltpu.roll(total, width - zz * step, 1)
+        part = jnp.where(lane < step, part, 0.0)
+        both = jnp.concatenate([isum[2 * zz], isum[2 * zz + 1]], axis=1)
+        part = jnp.where(place == 6, both, part)
+        sums_ref[zz, 0:16, :] = jnp.concatenate([part, jnp.zeros((8, width), f32)], axis=0).astype(bf16)
+
+
+Q_PLACE, K_PLACE, V_PLACE = (4, 5, 6), (0, 2, 8), (1, 3, 9)
+
+
+def half_tile(tile_of, block, upper):
+    tile = tile_of(block // 2)
+    return tile if block % 2 == upper else pltpu.roll(tile, 64, 1)
+
+
+def final_kernel(
+    dproj_ref, wq_ref, gh1_ref, gw_ref, fin_ref, sums_ref,
+    gt_ref, gqkv_ref, gin_ref, gback_ref, gout_ref, qb_ref, vb_ref, o0, o1, o2, o3, o4, o5, ib_ref,
+    wv, local_sems,
+):
+    z = lax.axis_index("fsdp")
+    loc = Local(local_sems)
+    shard = wq_ref.shape[2]
+    for zz in range(PLANES):
+        loc.add(zz, lambda zz=zz: wq_ref.at[zz], lambda zz=zz: wv.at[:, zz * shard : (zz + 1) * shard, :])
+    loc.start(*range(PLANES))
+    lane = lanes_of()
+    up = lambda a: a.astype(f32)
+    ch = fin_ref.shape[3]
+    for m in range(2):
+        for c in range(4):
+            n = m * 4 + c
+            gin_ref[:, n * ch : (n + 1) * ch] = up(fin_ref[m, c, 0:shard, :])
+            part = ch // 4
+            for x in range(2):
+                gback_ref[n * part : (n + 1) * part, x * ch : (x + 1) * ch] = up(
+                    fin_ref[m, c, shard + x * part : shard + (x + 1) * part, :]
+                )
+            gout_ref[c * (shard // 4) : (c + 1) * (shard // 4), m * ch : (m + 1) * ch] = up(fin_ref[m, c, shard + 2 * part :, :])
+    piece = shard // 2
+    for m in range(2):
+        r = slice(m * piece, (m + 1) * piece)
+        for kind, places in enumerate((Q_PLACE, K_PLACE, V_PLACE)):
+            for i in range(HEADS // 2):
+                halves = []
+                for upper in (0, 1):
+                    g, h = divmod(2 * i + upper, GROUP_HEADS)
+                    tile_of = lambda t, g=g: up(gw_ref[m, g, 0:piece, t * 128 : (t + 1) * 128])
+                    halves.append(half_tile(tile_of, places[h], upper))
+                at = kind * HEADS * 64 + i * 128
+                gqkv_ref[r, at : at + 128] = jnp.where(lane < 64, halves[0], halves[1])
+    tile_of = lambda t: up(gw_ref[0, z, piece : piece + 16, t * 128 : (t + 1) * 128])
+    for ref, places in ((qb_ref, Q_PLACE), (vb_ref, V_PLACE)):
+        first = jnp.where(lane < 64, half_tile(tile_of, places[0], 0), half_tile(tile_of, places[1], 1))
+        ref[:, 0:128] = first[0:1]
+        ref[:, 128:192] = half_tile(tile_of, places[2], 0)[0:1, 0:64]
+    for i, ref in enumerate((o0, o1, o2, o3, o4, o5)):
+        ref[...] = up(sums_ref[...])[i : i + 1, 0:shard]
+    ib_ref[...] = up(sums_ref[...])[6:7, :]
+    loc.wait(*range(PLANES))
+    total = gh1_ref[...]
+    for g in range(4):
+        total = total + dot(dproj_ref[g], wv[g], NT)
+    gt_ref[...] = total.astype(bf16)
+
+
+def vmem(shape, dtype=bf16):
+    return pltpu.VMEM(shape, dtype)
+
+
+ANY = pl.BlockSpec(memory_space=pl.ANY)
+SMEM = pl.BlockSpec(memory_space=pltpu.SMEM)
+VMEM = pl.BlockSpec(memory_space=pltpu.VMEM)
+VMEM_BYTES = 60 * 2**20
+SEMS = 96
+
+
+def semaphores():
+    return [pltpu.SemaphoreType.DMA((SEMS,)), pltpu.SemaphoreType.DMA((SEMS,)), pltpu.SemaphoreType.DMA((16,))]
+
+
+def params(collective_id):
+    return pltpu.CompilerParams(
+        collective_id=collective_id, has_side_effects=True, vmem_limit_bytes=VMEM_BYTES
+    )
+
+
+def run_forward(lengths, tokens, w_qkv, w_in, w_back, w_out, small):
+    rows, width = tokens.shape
+    shard = w_qkv.shape[0]
+    hidden = w_in.shape[1]
+    S = jax.ShapeDtypeStruct
+    q_shape, kv_shape = (GROUP_HEADS, 4 * rows, 128), (GROUP_HEADS, 8 * rows, 128)
+    return pl.pallas_call(
+        forward_kernel,
+        out_shape=(
+            S(q_shape, bf16), S(kv_shape, bf16), S(kv_shape, bf16), S(q_shape, bf16),
+            S((4, rows, width), bf16), S((4, rows, 256), bf16), S((PLANES, 16, width), bf16),
+            S((PLANES * shard, hidden), bf16), S((hidden, width), bf16), S((width, width), bf16),
+            S((PLANES, CHIPS, shard, PACK), bf16),
+        ),
+        in_specs=[SMEM] + [ANY] * 6,
+        out_specs=[ANY] * 11,
+        scratch_shapes=[
+            vmem((4, rows, width)), vmem((width, PACK)), vmem(q_shape), vmem(kv_shape), vmem(kv_shape), vmem(q_shape),
+            vmem((4, rows, 256)), vmem((4, rows, 256)), vmem((4, rows, 384)), vmem((4, rows, 384)),
+            vmem((PLANES, 16, width)), vmem((shard, w_qkv.shape[1])), vmem((CHIPS, shard, PACK)),
+        ] + semaphores(),
+        compiler_params=params(1),
+    )(lengths, tokens, w_qkv, w_in, w_back, w_out, small)
+
+
+def run_backward(do, q, k, v, o, tok, grads, sums):
+    rows = do.shape[1]
+    width = tok.shape[2]
+    shard = width // PLANES
+    length, cols = grads.shape[3:]
+    cut = length // 32 * 16
+    S = jax.ShapeDtypeStruct
+    ext = shard // 2 + 16
+    return pl.pallas_call(
+        backward_kernel,
+        out_shape=(
+            S((4, rows, PACK), bf16), S((2, 4, ext, PACK), bf16), S((2, 4, length, cols), bf16), S((16, width), bf16),
+        ),
+        in_specs=[ANY] * 8,
+        out_specs=[ANY] * 4,
+        scratch_shapes=[
+            vmem((4, rows, 256)), vmem(q.shape), vmem(k.shape), vmem(v.shape), vmem(o.shape), vmem(q.shape),
+            vmem(tok.shape), vmem((width, 4 * rows)), vmem((128, 4 * rows), f32), vmem((4 * rows, 128), f32),
+            vmem((4 * rows, 128), f32), vmem((3, 4 * rows, 128)), vmem((3, 4 * rows, 128)),
+            vmem((4, rows, PACK)), vmem((4, rows, PACK)),
+            vmem((2, 4, ext, PACK)), vmem((4, ext, PACK)), vmem((4, ext, PACK)), vmem((3, ext, PACK)), vmem((2, 4, ext, PACK)),
+            vmem((4, 4, length, cols)), vmem((4, 4, length, cols)),
+            vmem((4, 2, cut, cols)), vmem((4, 2, length - cut, cols)), vmem((4, cut, cols)), vmem((4, length - cut, cols)),
+            vmem((3, length, cols)), vmem((2, 4, length, cols)),
+            vmem((4, 4, 16, width)), vmem((3, 4, 16, width)), vmem((3, 16, width)), vmem((16, width)),
+        ] + semaphores(),
+        compiler_params=params(2),
+    )(do, q, k, v, o, tok, grads, sums)
+
+
+def run_ffn(lengths, att, tokens, cotangent, w_in, w_back, w_out, small):
+    rows, width = tokens.shape
+    hidden = w_in.shape[1]
+    ch = hidden // 8
+    S = jax.ShapeDtypeStruct
+    one = S((rows, width), bf16)
+    return pl.pallas_call(
+        ffn_kernel,
+        out_shape=(one, S((rows, width), f32), S((4, rows, 256), bf16), S((2, 4, 4, width // 4 + 192 + 48, ch), bf16), S((4, 16, width), bf16)),
+        in_specs=[SMEM] + [VMEM] * 3 + [ANY] * 3 + [VMEM],
+        out_specs=[VMEM] * 5,
+        scratch_shapes=[
+            vmem((width, hidden)), vmem((hidden, width)), vmem((width, width)),
+            vmem((8, rows, ch)), vmem((8, rows, ch), f32), vmem((8, rows, ch)),
+            vmem((rows, width), f32), vmem((rows, width), f32), vmem((rows, width), f32),
+            vmem((rows, width)), vmem((width, rows)), vmem((rows, width)), vmem((rows, width), f32), vmem((8, 8, ch), f32),
+            pltpu.SemaphoreType.DMA((24,)),
+        ],
+        compiler_params=pltpu.CompilerParams(vmem_limit_bytes=VMEM_BYTES),
+    )(lengths, att, tokens, cotangent, w_in, w_back, w_out, small)
+
+
+def run_final(dproj, wq_full, gh1, gw, fin, sums):
+    rows, width = gh1.shape
+    shard = width // PLANES
+    S = jax.ShapeDtypeStruct
+    one = S((1, shard), f32)
+    return pl.pallas_call(
+        final_kernel,
+        out_shape=(
+            S((rows, width), bf16), S((shard, 3 * width), f32), S((shard, 8 * fin.shape[3]), f32),
+            S((2 * fin.shape[3], width), f32), S((shard, width), f32), one, one, one, one, one, one, one, one, S((1, width), f32),
+        ),
+        in_specs=[VMEM, ANY] + [VMEM] * 4,
+        out_specs=[VMEM] * 14,
+        scratch_shapes=[vmem((4, width, PACK)), pltpu.SemaphoreType.DMA((4,))],
+        compiler_params=pltpu.CompilerParams(vmem_limit_bytes=VMEM_BYTES),
+    )(dproj, wq_full, gh1, gw, fin, sums)
+
+
+def planned(
+    tokens, lengths, w_qkv, q_bias, v_bias, w_out, out_bias, ln1_gain, ln1_bias,
+    w_in, in_bias, w_back, back_bias, ln2_gain, ln2_bias, cotangent,
+):
+    width = tokens.shape[2]
+    shard = q_bias.shape[0]
+    gap, half = jnp.zeros((width - shard,), bf16), jnp.zeros((64,), bf16)
+    vectors = []
+    for a in (out_bias, ln1_gain, ln1_bias, back_bias, ln2_gain, ln2_bias):
+        vectors += [a, gap]
+    vectors += [in_bias, half, v_bias[0:64], half, v_bias[64:128], q_bias, half, half, v_bias[128:192]]
+    vectors += [jnp.zeros((width - PACK + 8 * width,), bf16)]
+    small = jnp.concatenate(vectors).reshape(16, width)
+    q, k, v, o, tok_all, att, small_all, full_in, full_back, full_out, wq_full = run_forward(
+        lengths, tokens[0], w_qkv, w_in, w_back, w_out, small
+    )
+    output, gh1, do, grads, sums = run_ffn(
+        lengths, att, tokens[0], cotangent[0], full_in, full_back, full_out, small_all
+    )
+    dproj, gw, fin, sums_f = run_backward(do, q, k, v, o, tok_all, grads, sums)
+    gt, gqkv, gin, gback, gout, qb, vb, ob, g1, b1, bb, g2, b2, ib = run_final(dproj, wq_full, gh1, gw, fin, sums_f)
+    flat = lambda a: a.reshape(a.shape[1])
+    return (
+        output[None], gt[None], gqkv, flat(qb), flat(vb), gout, flat(ob), flat(g1), flat(b1), gin, flat(ib),
+        gback, flat(bb), flat(g2), flat(b2),
+    )
 
 
 masked_score = -1e30
@@ -327,8 +1300,9 @@
 
 
 def solution(mesh):
+    fits = mesh.shape["seq"] == 2 * CHIPS and mesh.shape["fsdp"] == PLANES
     return jax.shard_map(
-        on_device,
+        planned if fits else on_device,
         mesh=mesh,
         in_specs=(
             P("fsdp", "seq", None),

time: 1100 us -> 260 us (0.24)
  waiting for transfers between devices: 597 us -> 0 us
  Pallas kernels: 0 us -> 250 us
  matrix products: 187 us -> 0 us
  local copies, waits for them, and re-layouts: 127 us -> 6.96 us
  other arithmetic: 75.6 us -> 1.28 us
  blocking collectives: 58.3 us -> 0 us
  starting transfers between devices: 28.6 us -> 0 us
  between operations: 17.7 us -> 1.33 us
    pallas_call x0 -> x4, Pallas kernels: none -> 250 us  [the longest x1 110 us: run_backward(): pl.pallas_call(backward_kernel, out_shape=(S((4, rows, PACK), bf16), S((2...]
    reduce_scatter x3 -> x0, waiting for transfers between devices: 204 us -> none  [the longest x1 88.1 us: on_device(): lax.psum_scatter(local_grads[7].astype(jnp.bfloat16), 'fsdp', scatter_dim...]
    dot_general x54 -> x0, matrix products: 187 us -> none  [the longest x8 28.4 us: backward_tile(): jnp.einsum('qhd,khd->hqk', grad_heads, value_heads, preferred_element_typ...]
    all_gather x5 -> x0, waiting for transfers between devices: 153 us -> none  [the longest x1 65.9 us: on_device(): lax.all_gather(w_back, 'fsdp', axis=0, tiled=True)]
    ppermute x15 -> x0, waiting for transfers between devices: 146 us -> none  [passed_along(): return lax.ppermute(block, axis, route)]
    slice x15 -> x1, local copies, waits for them, and re-layouts: 76 us -> 0.84 us  [planned(): v_bias[128:192]]
    unnamed x11 -> x0, waiting for transfers between devices: 56.2 us -> none
    convert_element_type x38 -> x0, other arithmetic: 43.5 us -> none  [the longest x7 19.8 us: return_key_grads(): passed_along(grad_pair.astype(jnp.bfloat16), 'seq', 1)]
  transfers between devices with their start and end apart: 25 -> 0, of which waited for: 23 -> 0; matrix products, arithmetic and copies ran while one was open for 21% -> 0% of each run, Pallas kernels for 0% -> 0%
where the time goes in v1:
time: 260 us; the launch traced here: 259 us
  Pallas kernels  250 us (96%)
  local copies, waits for them, and re-layouts  6.96 us (3%)
    pallas_call x1, Pallas kernels, run_backward(): pl.pallas_call(backward_kernel, out_shape=(S((4, rows, PACK), bf16), S((2...  110 us
    pallas_call x1, Pallas kernels, run_forward(): pl.pallas_call(forward_kernel, out_shape=(S(q_shape, bf16), S(kv_shape, b...  93.9 us
    pallas_call x1, Pallas kernels, run_ffn(): pl.pallas_call(ffn_kernel, out_shape=(one, S((rows, width), f32), S((4, r...  37.4 us
    pallas_call x1, Pallas kernels, run_final(): pl.pallas_call(final_kernel, out_shape=(S((rows, width), bf16), S((shard,...  8.48 us
    concatenate x2, local copies, waits for them, and re-layouts, planned(): small = jnp.concatenate(vectors).reshape(16, width)  5.45 us

profile of v1, /device:TPU:1, one launch (start us, length us, event | category | flops | bytes accessed | tf_op | source)
XLA Modules:
  0.0 259.5 jit_solution(12936771480042578924)
XLA Ops:
  1.3 0.8 fusion
  2.2 5.4 %concatenate.7 = bf16[12288]{0:T(1024)(128)(2,1)S(1)} concatenate(bf16[192]{0:T(256)(128)(2,1)} %param.22, bf16[576]{0:T(1024)(128)(2,1)S(1)} %broadcast_in_dim.15, bf16[192]{0:T(256)(128)(2,1)} %param.23, bf16[576]{0:T(1024)(128)(2,1)S(1)} %broadcast_in_dim.15, bf16[192]{0:T(256)(128)(2,1)} %param.24, bf16[576]{0:T(1024)(128)(2,1)S(1)} %broadcast_in_dim.15, ...), dimensions={0} | concatenate | bytes 49152 | tf_op jit(solution)/shard_map/concatenate | solution.py:966
  7.6 0.7 reshape.60.small_ref
  8.3 93.9 %shard_map.271 = (bf16[3,1536,128]{2,1,0:T(8,128)(2,1)}, bf16[3,3072,128]{2,1,0:T(8,128)(2,1)}, bf16[3,3072,128]{2,1,0:T(8,128)(2,1)}, bf16[3,1536,128]{2,1,0:T(...) custom-call(s32[1]{0:T(128)S(6)} %copy.31.length_ref, ...), custom_call_target="tpu_custom_call" | custom-call | tf_op jit(solution)/shard_map/pallas_call | solution.py:865
  102.2 37.4 %shard_map.272 = (bf16[384,768]{1,0:T(8,128)(2,1)}, f32[384,768]{1,0:T(8,128)}, bf16[4,384,256]{2,1,0:T(8,128)(2,1)}, bf16[2,4,4,432,384]{4,3,2,1,0:T(8,128)(2,1)}, bf16[4,16,768]{2,1,0:T(8,128)(2,1)}) custom-call(s32[1]{0:T(128)S(6)} %copy.31.length_ref, bf16[4,384,256]{2,1,0:T(8,128)(2,1)} %get-tuple-element.49.att_ref, bf16[384,768]{1,0:T(8,128)(2,1)} %bitcast.13, ...), custom_call_target="tpu_custom_call" | custom-call | tf_op jit(solution)/shard_map/pallas_call | solution.py:920
  139.6 110.1 %shard_map.273 = (bf16[4,384,640]{2,1,0:T(8,128)(2,1)}, bf16[2,4,112,640]{3,2,1,0:T(8,128)(2,1)}, bf16[2,4,432,384]{3,2,1,0:T(8,128)(2,1)}, bf16[16,768]{1,0:T(8,128)(2,1)}) custom-call(bf16[4,384,256]{2,1,0:T(8,128)(2,1)} %get-tuple-element.55.do_ref, bf16[3,1536,128]{2,1,0:T(8,128)(2,1)} %get-tuple-element.56.q_ref, ...), custom_call_target="tpu_custom_call" | custom-call | tf_op jit(solution)/shard_map/pallas_call | solution.py:892
  249.7 8.5 %shard_map.274 = (bf16[384,768]{1,0:T(8,128)(2,1)}, f32[192,2304]{1,0:T(8,128)}, f32[192,3072]{1,0:T(8,128)}, f32[768,768]{1,0:T(8,128)}, f32[192,768]{1,0:T(8,1...) custom-call(bf16[4,384,640]{2,1,0:T(8,128)(2,1)} %get-tuple-element., ...), custom_call_target="tpu_custom_call" | custom-call | tf_op jit(solution)/shard_map/pallas_call | solution.py:941
  258.2 1.3 reduce
  (4 shorter events, 0.0 us)

commit v2 on v1

--- a/solution.py
+++ b/solution.py
@@ -124,7 +124,7 @@
 
 def forward_kernel(
     length_ref, tok_ref, wraw_ref, win_ref, wback_ref, wout_ref, small_ref,
-    q_out, k_out, v_out, o_out, tok_out, att_out, small_out, win_full, wback_full, wout_full, wq_full,
+    q_out, k_out, v_out, o_out, tok_out, att_out, small_out, win_full, wout_full, wq_out, wback_full, wq_full,
     tok, wqv, q_s, k_s, v_s, o_s, att, atts, kvs, kvr, small, wraw, wq_ref, send_sems, recv_sems, local_sems,
 ):
     s, z, core, chip = coordinates()
@@ -139,36 +139,31 @@
     zs = [z] + [flip(z, dz) for dz in (1, 2, 3)]
     net, loc = Net(send_sems, recv_sems), Local(local_sems)
     width = win_full.shape[1] // 8
-    back = wback_full.shape[0] // PLANES
+    back = wback_ref.shape[0]
     bpiece = back // 8
-    arrays = ("out", "in", "back", "qkv")
+    arrays = ("out", "in", "back")
+    at = lambda start, size, unit=16: pl.ds(pl.multiple_of(start, unit), size)
 
     def part(a, zz, m, c):
         if a == "in":
-            return win_full.at[pl.ds(pl.multiple_of(zz * shard, 16), shard), pl.ds(pl.multiple_of((m * 4 + c) * width, 128), width)]
+            return win_full.at[at(zz * shard, shard), at((m * 4 + c) * width, width, 128)]
         if a == "back":
-            return wback_full.at[pl.ds(pl.multiple_of(zz * back + (m * 4 + c) * bpiece, 16), bpiece), :]
-        if a == "out":
-            return wout_full.at[pl.ds(pl.multiple_of(zz * shard + c * (shard // 4), 16), shard // 4), pl.ds(pl.multiple_of(m * width, 128), width)]
-        return wq_full.at[zz, m * 2 + lax.div(c, 2), pl.ds(pl.multiple_of(lax.rem(c, 2) * piece, 16), piece), :]
+            return wback_full.at[at(zz * back + (m * 4 + c) * bpiece, bpiece), :]
+        return wout_full.at[at(zz * shard + c * (shard // 4), shard // 4), at(m * width, width, 128)]
 
     def own_part(a, m, c):
         if a == "in":
-            return win_ref.at[:, pl.ds(pl.multiple_of((m * 4 + c) * width, 128), width)]
+            return win_ref.at[:, at((m * 4 + c) * width, width, 128)]
         if a == "back":
-            return wback_ref.at[pl.ds(pl.multiple_of((m * 4 + c) * bpiece, 16), bpiece), :]
-        if a == "out":
-            return wout_ref.at[pl.ds(pl.multiple_of(c * (shard // 4), 16), shard // 4), pl.ds(pl.multiple_of(m * width, 128), width)]
-        return wq_ref.at[m * 2 + lax.div(c, 2), pl.ds(pl.multiple_of(lax.rem(c, 2) * piece, 16), piece), :]
+            return wback_ref.at[at((m * 4 + c) * bpiece, bpiece), :]
+        return wout_ref.at[at(c * (shard // 4), shard // 4), at(m * width, width, 128)]
 
     def side(a, zz, m):
         if a == "in":
-            return win_full.at[pl.ds(pl.multiple_of(zz * shard, 16), shard), pl.ds(pl.multiple_of(m * 4 * width, 128), 4 * width)]
+            return win_full.at[at(zz * shard, shard), at(m * 4 * width, 4 * width, 128)]
         if a == "back":
-            return wback_full.at[pl.ds(pl.multiple_of(zz * back + m * 4 * bpiece, 16), 4 * bpiece), :]
-        if a == "out":
-            return wout_full.at[pl.ds(pl.multiple_of(zz * shard, 16), shard), pl.ds(pl.multiple_of(m * width, 128), width)]
-        return wq_full.at[zz, pl.ds(m * 2, 2)]
+            return wback_full.at[at(zz * back + m * 4 * bpiece, 4 * bpiece), :]
+        return wout_full.at[at(zz * shard, shard), at(m * width, width, 128)]
 
     for dz in (1, 2, 3):
         net.add(("wq", dz), lambda: wq_ref.at[chip, pl.ds(pl.multiple_of(core * piece, 16), piece), :],
@@ -189,7 +184,7 @@
         net.add(("att0", j), lambda j=j: atts.at[j, :, 0:128], lambda: att.at[chip, :, 0:128], peer[j])
         net.add(("att1", j), lambda j=j: atts.at[j, :, 128:256], lambda: att.at[chip, :, 128:256], peer[j])
     for a in arrays:
-        via, last = (1, 2) if a in ("in", "qkv") else (2, 1)
+        via, last = (1, 2) if a == "in" else (2, 1)
         for dz in (1, 2, 3):
             net.add((a, "z", dz), lambda a=a: own_part(a, core, chip), lambda a=a: part(a, z, core, chip), plane[dz])
             for j in (1, 2):
@@ -197,15 +192,14 @@
             net.add((a, 3, dz), lambda a=a, dz=dz, via=via: part(a, zs[dz], core, flip(chip, via)),
                     lambda a=a, dz=dz, via=via: part(a, zs[dz], core, flip(chip, via)), peer[last])
             net.add((a, "m", dz), lambda a=a, dz=dz: side(a, zs[dz], core), lambda a=a, dz=dz: side(a, zs[dz], core), mate)
+    for dz in (1, 2, 3):
+        net.add(("qkv", "z", dz), lambda: wq_ref.at[core * 2 + lax.div(chip, 2), pl.ds(pl.multiple_of(lax.rem(chip, 2) * piece, 16), piece), :],
+                lambda: wq_full.at[z, core * 2 + lax.div(chip, 2), pl.ds(pl.multiple_of(lax.rem(chip, 2) * piece, 16), piece), :], plane[dz])
     loc.add("raw", lambda: wraw_ref, lambda: wraw)
     loc.add("tok", lambda: tok_ref, lambda: tok.at[0])
     loc.add("wq", lambda: wq_ref.at[chip], lambda: wqv.at[pl.ds(pl.multiple_of(z * shard, 16), shard), :])
     loc.add("small", lambda: small_ref, lambda: small.at[z])
-    loc.add("in", lambda: win_ref, lambda: win_full.at[pl.ds(pl.multiple_of(z * shard, 16), shard), :])
-    loc.add("back", lambda: wback_ref, lambda: wback_full.at[pl.ds(pl.multiple_of(z * back, 16), back), :])
-    loc.add("out", lambda: wout_ref, lambda: wout_full.at[pl.ds(pl.multiple_of(z * shard, 16), shard), :])
-    loc.add("qkv", lambda: wq_ref, lambda: wq_full.at[z])
-    outs = (("k_o", k_s, k_out), ("v_o", v_s, v_out), ("q_o", q_s, q_out), ("o_o", o_s, o_out),
+    outs = (("wq_o", wq_ref, wq_out), ("k_o", k_s, k_out), ("v_o", v_s, v_out), ("q_o", q_s, q_out), ("o_o", o_s, o_out),
             ("tok_o", tok, tok_out), ("att_o", att, att_out), ("small_o", small, small_out))
     for name, src, dst in outs:
         loc.add(name, lambda src=src: src, lambda dst=dst: dst)
@@ -226,11 +220,10 @@
                 tile_of = lambda i: wraw[:, i * 128 : (i + 1) * 128].astype(f32)
                 halves.append(half_tile(tile_of, block, upper))
             wq_ref[g, :, t * 128 : (t + 1) * 128] = jnp.where(lane < 64, halves[0], halves[1]).astype(bf16)
-    loc.start("wq")
+    loc.start("wq", "wq_o")
     met(len(peer[1:] + [mate] + plane[1:]))
     net.start(*[("wq", dz) for dz in (1, 2, 3)], *[("small", dz) for dz in (1, 2, 3)])
     net.start("t1a", "t2b", "t1b", "t2a")
-    loc.start(*arrays)
     for dz in (1, 2, 3):
         net.recv(("wq", dz))
         net.start(("wqm", dz))
@@ -241,7 +234,7 @@
         net.recv(("small", dz), ("wqm", dz))
 
     length = length_ref[0]
-    bias = small[chip, 7:8, 0:PACK].astype(f32)
+    bias = small[chip, 3:4, 0:PACK].astype(f32)
 
     def keep(tile, h, slot, block):
         position = block * rows + lax.broadcasted_iota(jnp.int32, (rows, 1), 0)
@@ -292,7 +285,7 @@
     keep_other(3)
     loc.start("k_o", "v_o", "tok_o", "small_o")
 
-    query_tile, key_chunk = 512, 1024
+    query_tile, key_chunk = 2 * rows, 4 * rows
     tiles = 4 * rows // query_tile
     chunks = 8 * rows // key_chunk
 
@@ -348,9 +341,12 @@
         q_s[h, qrows, :] = wide.astype(bf16)
 
         for at, work in enumerate((
-            lambda: first_hop(1), lambda: None, lambda: first_hop(2), lambda: second_hop(1),
-            lambda: first_hop(3), lambda: (second_hop(2), attended_tile(0)), lambda: third_hop(1), lambda: second_hop(3),
-            lambda: (attended_tile(1), third_hop(2)),
+            lambda: first_hop(1),
+            lambda: (first_hop(2), second_hop(1)),
+            lambda: (first_hop(3), net.start(*[("qkv", "z", dz) for dz in (1, 2, 3)]), second_hop(2), third_hop(1)),
+            lambda: (attended_tile(0), second_hop(3)),
+            lambda: third_hop(2),
+            lambda: attended_tile(1),
         )):
             pl.when(t == at)(lambda work=work: (work(), None)[1])
         return carry
@@ -364,16 +360,17 @@
     for dz in (1, 2, 3):
         for a in arrays:
             net.recv((a, "m", dz))
+        net.recv(("qkv", "z", dz))
     for name in net.specs:
         net.sent(name)
-    loc.wait(*arrays, *[name for name, _, _ in outs])
+    loc.wait(*[name for name, _, _ in outs])
 
 
 def backward_kernel(
-    do_ref, q_ref, k_ref, v_ref, o_ref, tok_ref, grads_ref, sums_ref,
-    dproj_out, gw_out, fin_out, sums_out,
+    do_ref, q_ref, k_ref, v_ref, o_ref, tok_ref, grads_ref, sums_ref, back_ref,
+    dproj_out, gw_out, hw_out, fin_out, finb_out, sums_out,
     do_s, q_s, k_s, v_s, o_s, doa, tok, tokt, dqs, dq_keep, kv_own, kvs, kvr, dall, dproj,
-    gw, gwr, gz, gzr, gwf, acc, rb, rx, ry, rx2, ry2, rz, fin, sums, sums_r, sums_z, sums_f,
+    gw, gwr, gz, gzr, gwf, hw, hwr, hz, hzr, hwf, acc, rb, rx, ry, rx2, ry2, rz, rzb, fin, finb, sums, sums_r, sums_z, sums_f,
     send_sems, recv_sems, local_sems,
 ):
     s, z, core, chip = coordinates()
@@ -391,8 +388,6 @@
     shard = tok.shape[2] // PLANES
     piece = shard // 2
 
-    for j in (1, 2, 3):
-        net.add(("do", j), lambda j=j: do_ref.at[ch[j]], lambda j=j: do_s.at[j], peer[j])
     for h in range(GROUP_HEADS):
         net.add(("kv", h), lambda h=h: kvs.at[h], lambda h=h: kvr.at[h], mate)
         place = ((0, 128), (128, 384), (384, 640))[h]
@@ -410,6 +405,15 @@
         net.add(("y2", dz), lambda dz=dz: acc.at[zs[dz], ch[1], ys], lambda dz=dz: ry2.at[zs[dz]], peer[1])
         if dz:
             net.add(("rz", dz), lambda dz=dz: acc.at[zs[dz], chip], lambda dz=dz: rz.at[dz - 1], plane[dz])
+    for dz in (1, 2, 3):
+        net.add(("rzb", dz), lambda dz=dz: back_ref.at[zs[dz]], lambda dz=dz: rzb.at[dz], plane[dz])
+    bh = finb.shape[2] // 2
+    bx, by = slice(0, bh), slice(bh, 2 * bh)
+    net.add("b1", lambda: finb.at[core, chip], lambda: finb.at[core, chip], peer[1])
+    net.add("b2", lambda: finb.at[core, chip], lambda: finb.at[core, chip], peer[2])
+    net.add("b3x", lambda: finb.at[core, ch[1], bx], lambda: finb.at[core, ch[1], bx], peer[2])
+    net.add("b3y", lambda: finb.at[core, ch[2], by], lambda: finb.at[core, ch[2], by], peer[1])
+    net.add("bm", lambda: finb.at[core], lambda: finb.at[core], mate)
     net.add("f1", lambda: fin.at[core, chip], lambda: fin.at[core, chip], peer[1])
     net.add("f2", lambda: fin.at[core, chip], lambda: fin.at[core, chip], peer[2])
     net.add("f3x", lambda: fin.at[core, ch[1], xs], lambda: fin.at[core, ch[1], xs], peer[2])
@@ -420,36 +424,35 @@
     net.add("s2", lambda: sums.at[2], lambda: sums_r.at[2], peer[2])
     for dz in (1, 2, 3):
         net.add(("sz", dz), lambda dz=dz: sums.at[3, zs[dz]], lambda dz=dz: sums_z.at[dz - 1], plane[dz])
-    net.add("g0", lambda: gw.at[other], lambda: gwr, mate)
-    for dz in (1, 2, 3):
-        net.add(("gz", dz), lambda dz=dz: gz.at[zs[dz]], lambda dz=dz: gzr.at[dz - 1], plane[dz])
-    for j in (1, 2, 3):
-        net.add(("gf", j), lambda: gwf.at[core, chip], lambda: gwf.at[core, chip], peer[j])
-    net.add("gm", lambda: gwf.at[core], lambda: gwf.at[core], mate)
-
-    loads = (("do", lambda: do_ref.at[chip], lambda: do_s.at[0]), ("o", lambda: o_ref, lambda: o_s),
+    for a, w, wr, g, gr, f in (("g", gw, gwr, gz, gzr, gwf), ("h", hw, hwr, hz, hzr, hwf)):
+        net.add((a, 0), lambda w=w: w.at[other], lambda wr=wr: wr, mate)
+        for dz in (1, 2, 3):
+            net.add((a, "z", dz), lambda g=g, dz=dz: g.at[zs[dz]], lambda gr=gr, dz=dz: gr.at[dz - 1], plane[dz])
+        for j in (1, 2, 3):
+            net.add((a, "f", j), lambda f=f: f.at[core, chip], lambda f=f: f.at[core, chip], peer[j])
+        net.add((a, "m"), lambda f=f: f.at[core], lambda f=f: f.at[core], mate)
+
+    loads = (("do", lambda: do_ref, lambda: do_s), ("o", lambda: o_ref, lambda: o_s),
              ("tok", lambda: tok_ref, lambda: tok), ("q", lambda: q_ref, lambda: q_s),
              ("k", lambda: k_ref, lambda: k_s), ("v", lambda: v_ref, lambda: v_s),
-             ("sums", lambda: sums_ref, lambda: sums.at[0]), ("acc", lambda: grads_ref.at[core], lambda: acc))
+             ("sums", lambda: sums_ref, lambda: sums.at[0]), ("back", lambda: back_ref.at[z], lambda: rzb.at[0]), ("acc", lambda: grads_ref.at[core], lambda: acc))
     for name, src, dst in loads:
         loc.add(name, src, dst)
-    stores = (("dp_o", dproj, dproj_out), ("gw_o", gwf, gw_out), ("fin_o", fin, fin_out))
+    stores = (("dp_o", dproj, dproj_out), ("gw_o", gwf, gw_out), ("hw_o", hwf, hw_out), ("fin_o", fin, fin_out), ("finb_o", finb, finb_out))
     for name, src, dst in stores:
         loc.add(name, lambda src=src: src, lambda dst=dst: dst)
     loc.add("sums_o", lambda: sums_f, lambda: sums_out)
 
     loc.start(*[name for name, _, _ in loads])
     greet(peer[1:] + [mate] + plane[1:])
-    net.start(*[("do", j) for j in (1, 2, 3)])
     net.start("s0", *[("r1", dz) for dz in order])
+    net.start(*[("rzb", dz) for dz in (1, 2, 3)])
     lane = lanes_of()
     loc.wait("tok")
     for j in range(4):
         tokt[:, j * rows : (j + 1) * rows] = tok[j].T
-    loc.wait("do", "o", "q", "k", "v", "sums", "acc")
+    loc.wait("do", "o", "q", "k", "v", "sums", "back", "acc")
     for j in range(4):
-        if j:
-            net.recv(("do", j))
         for h in range(GROUP_HEADS):
             tile = do_s[j, :, (h // 2) * 128 : (h // 2) * 128 + 128].astype(f32)
             if h == 1:
@@ -495,6 +498,69 @@
             net.start(f"s{n + 1}")
         else:
             net.start(*[("sz", dz) for dz in (1, 2, 3)])
+
+    def back_total():
+        net.recv(*[("rzb", dz) for dz in (1, 2, 3)])
+        total = rzb[0].astype(f32) + rzb[1].astype(f32) + rzb[2].astype(f32) + rzb[3].astype(f32)
+        finb[core, chip] = total.astype(bf16)
+        net.start("b1", "b2")
+
+    def back_forward():
+        net.recv("b1")
+        net.start("b3x")
+        net.recv("b2")
+        net.start("b3y")
+
+    def back_mate():
+        net.recv("b3x", "b3y")
+        net.start("bm")
+
+    def fin_total():
+        for dz in (1, 2, 3):
+            net.recv(("rz", dz), ("sz", dz))
+        total = acc[z, chip].astype(f32) + rz[0].astype(f32) + rz[1].astype(f32) + rz[2].astype(f32)
+        fin[core, chip] = total.astype(bf16)
+        net.start("f1", "f2")
+        total = sums[3, z].astype(f32)
+        for n in range(3):
+            total = total + sums_z[n].astype(f32)
+        sums_f[...] = total.astype(bf16)
+        loc.start("sums_o")
+
+    def fin_forward():
+        net.recv("f1")
+        net.start("f3x")
+        net.recv("f2")
+        net.start("f3y")
+
+    def weight_part(a, w, first, last):
+        cols = dall[:, :, first:last].reshape(4 * rows, last - first)
+        column_sums = jnp.sum(cols.astype(f32), axis=0, keepdims=True)
+        extra = jnp.where(lax.broadcasted_iota(jnp.int32, (16, 1), 0) == 0, column_sums, 0.0).astype(bf16)
+        for zz in range(PLANES):
+            part = dot(tokt[zz * shard : (zz + 1) * shard, :], cols)
+            for m in range(2):
+                w[m, zz, 0:piece, :] = part[m * piece : (m + 1) * piece, :].astype(bf16)
+                w[m, zz, piece : piece + 16, :] = extra
+        net.start((a, 0))
+
+    def weight_pair(a, w, wr, g):
+        net.recv((a, 0))
+        for zz in range(PLANES):
+            g[zz] = (w[core, zz].astype(f32) + wr[zz].astype(f32)).astype(bf16)
+        net.start(*[(a, "z", dz) for dz in (1, 2, 3)])
+
+    def weight_total(a, g, gr, f):
+        total = g[z].astype(f32)
+        for dz in (1, 2, 3):
+            net.recv((a, "z", dz))
+            total = total + gr[dz - 1].astype(f32)
+        f[core, chip] = total.astype(bf16)
+        net.start(*[(a, "f", j) for j in (1, 2, 3)])
+
+    def weight_mate(a):
+        net.recv(*[(a, "f", j) for j in (1, 2, 3)])
+        net.start((a, "m"))
 
     key_chunk, query_tile = 2 * rows, 256
     per_head = 4
@@ -523,14 +589,15 @@
     stages = {
         0: lambda: (step_one(3), sums_step(0)),
         1: lambda: (step_one(2), sums_step(1)),
-        2: lambda: (step_two(3), sums_step(2)),
-        3: lambda: step_one(1),
-        4: lambda: (step_three(3), step_two(2)),
-        5: lambda: step_one(0),
-        6: lambda: (step_three(2), step_two(1)),
-        8: lambda: step_two(0),
-        9: lambda: step_three(1),
-        11: lambda: step_three(0),
+        2: lambda: (step_two(3), step_one(1), sums_step(2)),
+        3: lambda: (step_three(3), step_two(2)),
+        4: lambda: (step_one(0), back_total()),
+        5: lambda: (step_three(2), step_two(1)),
+        6: lambda: (step_two(0), back_forward()),
+        7: lambda: (step_three(1), weight_part("g", gw, 0, 384)),
+        8: lambda: (step_three(0), back_mate()),
+        9: lambda: (fin_total(), weight_pair("g", gw, gwr, gz)),
+        11: lambda: (fin_forward(), weight_total("g", gz, gzr, gwf)),
     }
 
     def visit(t, carry):
@@ -578,55 +645,24 @@
 
     lax.fori_loop(0, GROUP_HEADS * per_head, visit, 0)
 
+    weight_part("h", hw, 384, PACK)
     dproj[chip] = dall[0]
-    d_cols = dall[...].reshape(4 * rows, PACK)
-    column_sums = jnp.sum(d_cols.astype(f32), axis=0, keepdims=True)
-    extra = jnp.where(lax.broadcasted_iota(jnp.int32, (16, 1), 0) == 0, column_sums, 0.0).astype(bf16)
-    for zz in range(PLANES):
-        part = dot(tokt[zz * shard : (zz + 1) * shard, :], d_cols)
-        for m in range(2):
-            gw[m, zz, 0:piece, :] = part[m * piece : (m + 1) * piece, :].astype(bf16)
-            gw[m, zz, piece : piece + 16, :] = extra
-    net.start("g0")
-
-    for dz in (1, 2, 3):
-        net.recv(("rz", dz), ("sz", dz))
-    total = acc[z, chip].astype(f32) + rz[0].astype(f32) + rz[1].astype(f32) + rz[2].astype(f32)
-    fin[core, chip] = total.astype(bf16)
-    net.start("f1", "f2")
-    total = sums[3, z].astype(f32)
-    for n in range(3):
-        total = total + sums_z[n].astype(f32)
-    sums_f[...] = total.astype(bf16)
-    loc.start("sums_o")
-
-    net.recv("g0")
-    for zz in range(PLANES):
-        gz[zz] = (gw[core, zz].astype(f32) + gwr[zz].astype(f32)).astype(bf16)
-    net.start(*[("gz", dz) for dz in (1, 2, 3)])
+    weight_pair("h", hw, hwr, hz)
+    weight_mate("g")
+    net.recv("f3x", "f3y")
+    net.start("fm")
+    weight_total("h", hz, hzr, hwf)
     for h in range(GROUP_HEADS):
         for j in (1, 2, 3):
             net.recv(("dp", h, j))
-    loc.start("dp_o")
-    net.recv("f1")
-    net.start("f3x")
-    net.recv("f2")
-    net.start("f3y")
-    total = gz[z].astype(f32)
-    for dz in (1, 2, 3):
-        net.recv(("gz", dz))
-        total = total + gzr[dz - 1].astype(f32)
-    gwf[core, chip] = total.astype(bf16)
-    net.start(*[("gf", j) for j in (1, 2, 3)])
-    net.recv("f3x", "f3y")
-    net.start("fm")
-    net.recv(*[("gf", j) for j in (1, 2, 3)])
-    net.start("gm")
-    net.recv("fm", "gm")
-    loc.start("gw_o", "fin_o")
+    net.recv("fm", "bm", ("g", "m"))
+    loc.start("dp_o", "gw_o", "fin_o", "finb_o")
+    weight_mate("h")
+    net.recv(("h", "m"))
+    loc.start("hw_o")
     for name in net.specs:
         net.sent(name)
-    loc.wait("dp_o", "gw_o", "fin_o", "sums_o")
+    loc.wait("dp_o", "gw_o", "hw_o", "fin_o", "finb_o", "sums_o")
 
 
 def gelu_parts(u):
@@ -646,36 +682,109 @@
 
 
 def wide_vectors(small):
-    total = small[0].astype(f32)[0:8]
     step = small.shape[2] // PLANES
-    lane = lax.broadcasted_iota(jnp.int32, total.shape, 1)
-    total = jnp.where(lane < step, total, 0.0)
-    for zz in range(1, PLANES):
-        part = jnp.where(lane < step, small[zz].astype(f32)[0:8], 0.0)
-        total = total + pltpu.roll(part, zz * step, 1)
+    lane = lax.broadcasted_iota(jnp.int32, (8, small.shape[2]), 1)
+    total = [0.0] * PLANES
+    for zz in range(PLANES):
+        value = small[zz].astype(f32)[0:8]
+        for k in range(PLANES):
+            part = jnp.where((lane >= k * step) & (lane < (k + 1) * step), value, 0.0)
+            turn = (zz - k) % PLANES * step
+            total[k] = total[k] + (pltpu.roll(part, turn, 1) if turn else part)
     return total
 
 
 def ffn_kernel(
-    length_ref, att_ref, tok_ref, cot_ref, win_ref, wback_ref, wout_ref, small_ref,
-    out_ref, gh1_ref, do_ref, grads_ref, sums_ref,
-    winv, wbackv, woutv, act_s, gp_s, gi_s, acc, first_s, n1_s, low_s, lowt_s, gsec_s, gh2_s, isum, local_sems,
+    length_ref, att_ref, tok_ref, cot_ref, win_ref, win_own, wout_ref, wout_own, small_ref, wback_ref, wback_own, wq_in,
+    out_ref, gh1_ref, do_out, grads_ref, sums_ref, wq_full, back_out,
+    winv, wbackv, woutv, act_s, gp_s, gi_s, acc, first_s, n1_s, low_s, lowt_s, gsec_s, gh2_s, isum,
+    gb, rb, rx, ry, rx2, ry2, do_ref, do_in, send_sems, recv_sems, local_sems,
 ):
-    s = lax.axis_index("seq")
+    s, z, core, chip = coordinates()
+    other = 1 - core
     rows, width = tok_ref.shape
     step = width // PLANES
     ch = winv.shape[1] // 8
-    loc = Local(local_sems)
-    loc.add("out", lambda: wout_ref, lambda: woutv)
-    for n in range(8):
-        loc.add(("in", n), lambda n=n: win_ref.at[:, n * ch : (n + 1) * ch], lambda n=n: winv.at[:, n * ch : (n + 1) * ch])
-        loc.add(("back", n), lambda n=n: wback_ref.at[n * ch : (n + 1) * ch, :], lambda n=n: wbackv.at[n * ch : (n + 1) * ch, :])
-    loc.start("out")
-    for n in range(8):
-        loc.start(("in", n), ("back", n))
+    wide = 2 * ch
+    back = wback_own.shape[0]
+    shard = win_own.shape[0]
+    piece = shard // 2
+    peer = [None] + [(flip(chip, j) * 2 + core, z) for j in (1, 2, 3)]
+    mate = (chip * 2 + other, z)
+    zs = [z] + [flip(z, dz) for dz in (1, 2, 3)]
+    ch_of = [chip] + [flip(chip, j) for j in (1, 2, 3)]
+    net, loc = Net(send_sems, recv_sems), Local(local_sems)
+
+    def region(zz, m, c):
+        return wq_full.at[zz, m * 2 + lax.div(c, 2), pl.ds(pl.multiple_of(lax.rem(c, 2) * piece, 16), piece), :]
+
+    for dz in (1, 2, 3):
+        for j in (1, 2):
+            net.add((j, dz), lambda dz=dz: region(zs[dz], core, chip), lambda dz=dz: region(zs[dz], core, chip), peer[j])
+        net.add((3, dz), lambda dz=dz: region(zs[dz], core, ch_of[2]), lambda dz=dz: region(zs[dz], core, ch_of[2]), peer[1])
+        net.add(("m", dz), lambda dz=dz: wq_full.at[zs[dz], pl.ds(core * 2, 2)], lambda dz=dz: wq_full.at[zs[dz], pl.ds(core * 2, 2)], mate)
+    half = gb.shape[3] // 2
+    xs, ys = slice(0, half), slice(half, 2 * half)
+    for zz in range(PLANES):
+        net.add(("r1", zz), lambda zz=zz: gb.at[other, zz], lambda zz=zz: rb.at[zz], mate)
+        for n, j in enumerate((1, 3)):
+            net.add(("x1", n, zz), lambda zz=zz, j=j: gb.at[core, zz, ch_of[j], xs], lambda zz=zz, n=n: rx.at[zz, n], peer[1])
+        net.add(("x2", zz), lambda zz=zz: gb.at[core, zz, ch_of[2], xs], lambda zz=zz: rx2.at[zz], peer[2])
+        for n, j in enumerate((2, 3)):
+            net.add(("y1", n, zz), lambda zz=zz, j=j: gb.at[core, zz, ch_of[j], ys], lambda zz=zz, n=n: ry.at[zz, n], peer[2])
+        net.add(("y2", zz), lambda zz=zz: gb.at[core, zz, ch_of[1], ys], lambda zz=zz: ry2.at[zz], peer[1])
+    for j in (1, 2, 3):
+        net.add(("do", j), lambda j=j: do_ref.at[ch_of[j]], lambda j=j: do_in.at[j], peer[j])
+    loc.add("do_o", lambda: do_in, lambda: do_out)
+    loc.add("back_o", lambda: gb.at[core, :, chip], lambda: back_out)
+    for dz in range(4):
+        for name, own, full, dst in (("out", wout_own, wout_ref, woutv), ("in", win_own, win_ref, winv), ("back", wback_own, wback_ref, wbackv)):
+            n = own.shape[0]
+            place = lambda dz=dz, n=n: pl.ds(pl.multiple_of(zs[dz] * n, 16), n)
+            loc.add((name, dz), lambda own=own, full=full, dz=dz, place=place: own if dz == 0 else full.at[place(), :],
+                    lambda dst=dst, place=place: dst.at[place(), :])
+    for name in ("out", "in", "back"):
+        loc.start(*[(name, dz) for dz in range(4)])
+    hello(peer[1:] + [mate])
+
+    def hop_two(dz):
+        net.recv((1, dz), (2, dz))
+        net.start((3, dz))
+
+    def hop_three(dz):
+        net.recv((3, dz))
+        net.start(("m", dz))
+
+    def add_into(ref, index, other_ref, other_index):
+        ref[index] = (ref[index].astype(f32) + other_ref[other_index].astype(f32)).astype(bf16)
+
+    def step_one(zz):
+        net.recv(("r1", zz))
+        for c in range(CHIPS):
+            add_into(gb, (core, zz, c), rb, (zz, c))
+        net.start(*[("x1", n, zz) for n in (0, 1)], *[("y1", n, zz) for n in (0, 1)])
+
+    def step_two(zz):
+        net.recv(("x1", 1, zz), ("y1", 1, zz))
+        add_into(gb, (core, zz, ch_of[2], xs), rx, (zz, 1))
+        add_into(gb, (core, zz, ch_of[1], ys), ry, (zz, 1))
+        net.start(("x2", zz), ("y2", zz))
+        net.recv(("x1", 0, zz), ("y1", 0, zz))
+        add_into(gb, (core, zz, chip, xs), rx, (zz, 0))
+        add_into(gb, (core, zz, chip, ys), ry, (zz, 0))
+
+    def step_three(zz):
+        net.recv(("x2", zz), ("y2", zz))
+        add_into(gb, (core, zz, chip, xs), rx2, zz)
+        add_into(gb, (core, zz, chip, ys), ry2, zz)
+
+    def during(n, works):
+        for at, work in works.items():
+            pl.when(n == at)(lambda work=work: (work(), None)[1])
+
     vectors = wide_vectors(small_ref)
-    vec = lambda i: vectors[i : i + 1, :]
-    loc.wait("out")
+    vec = lambda i: vectors[i % 4][i // 4 : i // 4 + 1, :]
+    loc.wait(*[("out", dz) for dz in range(4)])
     branch = vec(0)
     for g in range(4):
         branch = branch + dot(att_ref[g, :, 0:step], woutv[g * step : (g + 1) * step, :])
@@ -689,13 +798,15 @@
     low_s[...] = first.astype(bf16)
     lowt_s[...] = first.astype(bf16).T
     acc[...] = jnp.zeros_like(acc)
-    for n in range(8):
-        loc.wait(("in", n), ("back", n))
+    met(4)
+    for dz in (1, 2, 3):
+        net.start((1, dz), (2, dz))
+    loc.wait(*[("in", dz) for dz in range(4)])
+    loc.wait(*[("back", dz) for dz in range(4)])
 
     def forward(n, carry):
-        cols = pl.ds(pl.multiple_of(n * ch, 128), ch)
-        bias = small_ref[lax.div(n, 2), 6:7, pl.ds(pl.multiple_of(lax.rem(n, 2) * ch, 128), ch)].astype(f32)
-        inner = dot(low_s[...], winv[:, cols]) + bias
+        cols = pl.ds(pl.multiple_of(n * wide, 128), wide)
+        inner = dot(low_s[...], winv[:, cols]) + small_ref[n, 2:3, :].astype(f32)
         value, slope = gelu_parts(inner)
         value = value.astype(bf16)
         act_s[n] = value
@@ -703,7 +814,9 @@
         acc[...] += dot(value, wbackv[cols, :])
         return carry
 
-    lax.fori_loop(0, 8, forward, 0)
+    lax.fori_loop(0, PLANES, forward, 0)
+    for dz in (1, 2, 3):
+        hop_two(dz)
     position = s * rows + lax.broadcasted_iota(jnp.int32, (rows, 1), 0)
     valid = (position < length_ref[0]).astype(f32)
     hidden = first_s[...] + acc[...] + vec(3)
@@ -722,15 +835,36 @@
     back_sum = sum_rows(second.astype(f32))
     acc[...] = jnp.zeros_like(acc)
 
+    def back_weights(n, carry):
+        gback = dot(act_s[n].T, gsec_s[...]).astype(bf16)
+        part = wide // 8
+        for m in range(2):
+            for k in range(4):
+                for x in range(2):
+                    gb[m, n, k, x * part : (x + 1) * part, :] = gback[
+                        (m * 4 + k) * part : (m * 4 + k + 1) * part, x * ch : (x + 1) * ch
+                    ]
+        during(n, {
+            0: lambda: net.start(("r1", 0)), 1: lambda: (net.start(("r1", 1)), hop_three(1)),
+            2: lambda: (net.start(("r1", 2)), hop_three(2)), 3: lambda: (net.start(("r1", 3)), hop_three(3)),
+        })
+        return carry
+
+    lax.fori_loop(0, PLANES, back_weights, 0)
+
     def backward(n, carry):
-        cols = pl.ds(pl.multiple_of(n * ch, 128), ch)
+        cols = pl.ds(pl.multiple_of(n * wide, 128), wide)
         grad_inner = (dot(gsec_s[...], wbackv[cols, :], NT) * gp_s[n]).astype(bf16)
         gi_s[n] = grad_inner
-        isum[n] = jnp.broadcast_to(sum_rows(grad_inner.astype(f32)), (8, ch))
+        isum[n] = jnp.broadcast_to(sum_rows(grad_inner.astype(f32)), (8, wide))
         acc[...] += dot(grad_inner, winv[:, cols], NT)
+        during(n, {
+            0: lambda: step_one(0), 1: lambda: step_one(1),
+            2: lambda: (step_one(2), step_two(0)), 3: lambda: step_one(3),
+        })
         return carry
 
-    lax.fori_loop(0, 8, backward, 0)
+    lax.fori_loop(0, PLANES, backward, 0)
     grad = gh2_s[...] + acc[...]
     normed = n1_s[...]
     g1_gain, g1_bias = sum_rows(grad * normed), sum_rows(grad)
@@ -743,26 +877,27 @@
         w = woutv[g * step : (g + 1) * step, :]
         do_ref[g, :, 0:step] = dot(gbranch, w, NT).astype(bf16)
         do_ref[g, :, step:] = jnp.zeros((rows, do_ref.shape[2] - step), bf16)
+    net.start(*[("do", j) for j in (1, 2, 3)])
+    do_in[0] = do_ref[chip]
+    for g in range(4):
         gw = dot(att_ref[g, :, 0:step].T, gbranch).astype(bf16)
         part = step // 4
         for c in range(4):
             for m in range(2):
-                grads_ref[m, g, c, step + 2 * 96 :, :] = gw[c * part : (c + 1) * part, m * ch : (m + 1) * ch]
+                grads_ref[m, g, c, step:, :] = gw[c * part : (c + 1) * part, m * ch : (m + 1) * ch]
 
     def weights(n, carry):
-        gback = dot(act_s[n].T, gsec_s[...]).astype(bf16)
-        part = ch // 4
-        for k in range(4):
+        for zz in range(PLANES):
+            gin = dot(lowt_s[zz * step : (zz + 1) * step, :], gi_s[n]).astype(bf16)
             for x in range(2):
-                grads_ref[lax.rem(n, 2), lax.div(n, 2), k, step + x * part : step + (x + 1) * part, :] = gback[
-                    k * part : (k + 1) * part, x * ch : (x + 1) * ch
-                ]
-        for zz in range(PLANES):
-            gin = dot(lowt_s[zz * step : (zz + 1) * step, :], gi_s[n])
-            grads_ref[lax.div(n, 4), zz, lax.rem(n, 4), 0:step, :] = gin.astype(bf16)
+                grads_ref[lax.div(n, 2), zz, lax.rem(n, 2) * 2 + x, 0:step, :] = gin[:, x * ch : (x + 1) * ch]
+        during(n, {
+            0: lambda: (step_two(1), step_three(0)), 1: lambda: step_two(2),
+            2: lambda: (step_two(3), step_three(1)), 3: lambda: step_three(2),
+        })
         return carry
 
-    lax.fori_loop(0, 8, weights, 0)
+    lax.fori_loop(0, PLANES, weights, 0)
     lane = lax.broadcasted_iota(jnp.int32, (8, width), 1)
     place = lax.broadcasted_iota(jnp.int32, (8, width), 0)
     total = jnp.zeros((8, width), f32)
@@ -771,9 +906,15 @@
     for zz in range(PLANES):
         part = total if zz == 0 else pltpu.roll(total, width - zz * step, 1)
         part = jnp.where(lane < step, part, 0.0)
-        both = jnp.concatenate([isum[2 * zz], isum[2 * zz + 1]], axis=1)
-        part = jnp.where(place == 6, both, part)
+        part = jnp.where(place == 6, isum[zz], part)
         sums_ref[zz, 0:16, :] = jnp.concatenate([part, jnp.zeros((8, width), f32)], axis=0).astype(bf16)
+    step_three(3)
+    net.recv(*[("do", j) for j in (1, 2, 3)])
+    loc.start("back_o", "do_o")
+    net.recv(*[("m", dz) for dz in (1, 2, 3)])
+    for name in net.specs:
+        net.sent(name)
+    loc.wait("back_o", "do_o")
 
 
 Q_PLACE, K_PLACE, V_PLACE = (4, 5, 6), (0, 2, 8), (1, 3, 9)
@@ -785,15 +926,17 @@
 
 
 def final_kernel(
-    dproj_ref, wq_ref, gh1_ref, gw_ref, fin_ref, sums_ref,
+    dproj_ref, wq_ref, wq_own, gh1_ref, gw_ref, hw_ref, fin_ref, finb_ref, sums_ref,
     gt_ref, gqkv_ref, gin_ref, gback_ref, gout_ref, qb_ref, vb_ref, o0, o1, o2, o3, o4, o5, ib_ref,
     wv, local_sems,
 ):
     z = lax.axis_index("fsdp")
     loc = Local(local_sems)
     shard = wq_ref.shape[2]
-    for zz in range(PLANES):
-        loc.add(zz, lambda zz=zz: wq_ref.at[zz], lambda zz=zz: wv.at[:, zz * shard : (zz + 1) * shard, :])
+    for dz in range(PLANES):
+        zz = flip(z, dz)
+        loc.add(dz, lambda zz=zz, dz=dz: wq_own if dz == 0 else wq_ref.at[zz],
+                lambda zz=zz: wv.at[:, pl.ds(pl.multiple_of(zz * shard, 16), shard), :])
     loc.start(*range(PLANES))
     lane = lanes_of()
     up = lambda a: a.astype(f32)
@@ -805,10 +948,16 @@
             part = ch // 4
             for x in range(2):
                 gback_ref[n * part : (n + 1) * part, x * ch : (x + 1) * ch] = up(
-                    fin_ref[m, c, shard + x * part : shard + (x + 1) * part, :]
+                    finb_ref[m, c, x * part : (x + 1) * part, :]
                 )
-            gout_ref[c * (shard // 4) : (c + 1) * (shard // 4), m * ch : (m + 1) * ch] = up(fin_ref[m, c, shard + 2 * part :, :])
+            gout_ref[c * (shard // 4) : (c + 1) * (shard // 4), m * ch : (m + 1) * ch] = up(fin_ref[m, c, shard:, :])
     piece = shard // 2
+
+    def packed_tile(m, g, r, t):
+        if t < 3:
+            return up(gw_ref[m, g, r, t * 128 : (t + 1) * 128])
+        return up(hw_ref[m, g, r, (t - 3) * 128 : (t - 2) * 128])
+
     for m in range(2):
         r = slice(m * piece, (m + 1) * piece)
         for kind, places in enumerate((Q_PLACE, K_PLACE, V_PLACE)):
@@ -816,11 +965,11 @@
                 halves = []
                 for upper in (0, 1):
                     g, h = divmod(2 * i + upper, GROUP_HEADS)
-                    tile_of = lambda t, g=g: up(gw_ref[m, g, 0:piece, t * 128 : (t + 1) * 128])
+                    tile_of = lambda t, g=g: packed_tile(m, g, slice(0, piece), t)
                     halves.append(half_tile(tile_of, places[h], upper))
                 at = kind * HEADS * 64 + i * 128
                 gqkv_ref[r, at : at + 128] = jnp.where(lane < 64, halves[0], halves[1])
-    tile_of = lambda t: up(gw_ref[0, z, piece : piece + 16, t * 128 : (t + 1) * 128])
+    tile_of = lambda t: packed_tile(0, z, slice(piece, piece + 16), t)
     for ref, places in ((qb_ref, Q_PLACE), (vb_ref, V_PLACE)):
         first = jnp.where(lane < 64, half_tile(tile_of, places[0], 0), half_tile(tile_of, places[1], 1))
         ref[:, 0:128] = first[0:1]
@@ -867,11 +1016,11 @@
         out_shape=(
             S(q_shape, bf16), S(kv_shape, bf16), S(kv_shape, bf16), S(q_shape, bf16),
             S((4, rows, width), bf16), S((4, rows, 256), bf16), S((PLANES, 16, width), bf16),
-            S((PLANES * shard, hidden), bf16), S((hidden, width), bf16), S((width, width), bf16),
-            S((PLANES, CHIPS, shard, PACK), bf16),
+            S((PLANES * shard, hidden), bf16), S((width, width), bf16),
+            S((CHIPS, shard, PACK), bf16), S((hidden, width), bf16), S((PLANES, CHIPS, shard, PACK), bf16),
         ),
         in_specs=[SMEM] + [ANY] * 6,
-        out_specs=[ANY] * 11,
+        out_specs=[ANY] * 12,
         scratch_shapes=[
             vmem((4, rows, width)), vmem((width, PACK)), vmem(q_shape), vmem(kv_shape), vmem(kv_shape), vmem(q_shape),
             vmem((4, rows, 256)), vmem((4, rows, 256)), vmem((4, rows, 384)), vmem((4, rows, 384)),
@@ -881,7 +1030,7 @@
     )(lengths, tokens, w_qkv, w_in, w_back, w_out, small)
 
 
-def run_backward(do, q, k, v, o, tok, grads, sums):
+def run_backward(do, q, k, v, o, tok, grads, sums, back):
     rows = do.shape[1]
     width = tok.shape[2]
     shard = width // PLANES
@@ -892,48 +1041,55 @@
     return pl.pallas_call(
         backward_kernel,
         out_shape=(
-            S((4, rows, PACK), bf16), S((2, 4, ext, PACK), bf16), S((2, 4, length, cols), bf16), S((16, width), bf16),
+            S((4, rows, PACK), bf16), S((2, 4, ext, 384), bf16), S((2, 4, ext, 256), bf16), S((2, 4, length, cols), bf16), S((2, 4) + back.shape[1:], bf16), S((16, width), bf16),
         ),
-        in_specs=[ANY] * 8,
-        out_specs=[ANY] * 4,
+        in_specs=[ANY] * 9,
+        out_specs=[ANY] * 6,
         scratch_shapes=[
             vmem((4, rows, 256)), vmem(q.shape), vmem(k.shape), vmem(v.shape), vmem(o.shape), vmem(q.shape),
             vmem(tok.shape), vmem((width, 4 * rows)), vmem((128, 4 * rows), f32), vmem((4 * rows, 128), f32),
             vmem((4 * rows, 128), f32), vmem((3, 4 * rows, 128)), vmem((3, 4 * rows, 128)),
             vmem((4, rows, PACK)), vmem((4, rows, PACK)),
-            vmem((2, 4, ext, PACK)), vmem((4, ext, PACK)), vmem((4, ext, PACK)), vmem((3, ext, PACK)), vmem((2, 4, ext, PACK)),
+            *[vmem(lead + (ext, n)) for n in (384, 256) for lead in ((2, 4), (4,), (4,), (3,), (2, 4))],
             vmem((4, 4, length, cols)), vmem((4, 4, length, cols)),
             vmem((4, 2, cut, cols)), vmem((4, 2, length - cut, cols)), vmem((4, cut, cols)), vmem((4, length - cut, cols)),
-            vmem((3, length, cols)), vmem((2, 4, length, cols)),
+            vmem((3, length, cols)), vmem((4,) + back.shape[1:]), vmem((2, 4, length, cols)), vmem((2, 4) + back.shape[1:]),
             vmem((4, 4, 16, width)), vmem((3, 4, 16, width)), vmem((3, 16, width)), vmem((16, width)),
         ] + semaphores(),
         compiler_params=params(2),
-    )(do, q, k, v, o, tok, grads, sums)
-
-
-def run_ffn(lengths, att, tokens, cotangent, w_in, w_back, w_out, small):
+    )(do, q, k, v, o, tok, grads, sums, back)
+
+
+def run_ffn(lengths, att, tokens, cotangent, full_in, w_in, full_out, w_out, small, full_back, w_back, wq_full):
     rows, width = tokens.shape
     hidden = w_in.shape[1]
     ch = hidden // 8
     S = jax.ShapeDtypeStruct
     one = S((rows, width), bf16)
+    bp = w_back.shape[0] // 8
     return pl.pallas_call(
         ffn_kernel,
-        out_shape=(one, S((rows, width), f32), S((4, rows, 256), bf16), S((2, 4, 4, width // 4 + 192 + 48, ch), bf16), S((4, 16, width), bf16)),
-        in_specs=[SMEM] + [VMEM] * 3 + [ANY] * 3 + [VMEM],
-        out_specs=[VMEM] * 5,
+        out_shape=(
+            one, S((rows, width), f32), S((4, rows, 256), bf16), S((2, 4, 4, width // 4 + 48, ch), bf16), S((4, 16, width), bf16),
+            S(wq_full.shape, bf16), S((4, 2 * bp, ch), bf16),
+        ),
+        in_specs=[SMEM] + [VMEM] * 3 + [ANY] * 4 + [VMEM] + [ANY] * 3,
+        input_output_aliases={11: 5},
+        out_specs=[VMEM] * 2 + [ANY] + [VMEM] * 2 + [ANY] * 2,
         scratch_shapes=[
             vmem((width, hidden)), vmem((hidden, width)), vmem((width, width)),
-            vmem((8, rows, ch)), vmem((8, rows, ch), f32), vmem((8, rows, ch)),
+            vmem((4, rows, 2 * ch)), vmem((4, rows, 2 * ch), f32), vmem((4, rows, 2 * ch)),
             vmem((rows, width), f32), vmem((rows, width), f32), vmem((rows, width), f32),
-            vmem((rows, width)), vmem((width, rows)), vmem((rows, width)), vmem((rows, width), f32), vmem((8, 8, ch), f32),
-            pltpu.SemaphoreType.DMA((24,)),
+            vmem((rows, width)), vmem((width, rows)), vmem((rows, width)), vmem((rows, width), f32), vmem((4, 8, 2 * ch), f32),
+            vmem((2, 4, 4, 2 * bp, ch)), vmem((4, 4, 2 * bp, ch)), vmem((4, 2, bp, ch)), vmem((4, 2, bp, ch)), vmem((4, bp, ch)), vmem((4, bp, ch)),
+            vmem((4, rows, 256)), vmem((4, rows, 256)),
+            pltpu.SemaphoreType.DMA((SEMS,)), pltpu.SemaphoreType.DMA((SEMS,)), pltpu.SemaphoreType.DMA((24,)),
         ],
-        compiler_params=pltpu.CompilerParams(vmem_limit_bytes=VMEM_BYTES),
-    )(lengths, att, tokens, cotangent, w_in, w_back, w_out, small)
-
-
-def run_final(dproj, wq_full, gh1, gw, fin, sums):
+        compiler_params=params(3),
+    )(lengths, att, tokens, cotangent, full_in, w_in, full_out, w_out, small, full_back, w_back, wq_full)
+
+
+def run_final(dproj, wq_full, wq, gh1, gw, hw, fin, finb, sums):
     rows, width = gh1.shape
     shard = width // PLANES
     S = jax.ShapeDtypeStruct
@@ -944,11 +1100,11 @@
             S((rows, width), bf16), S((shard, 3 * width), f32), S((shard, 8 * fin.shape[3]), f32),
             S((2 * fin.shape[3], width), f32), S((shard, width), f32), one, one, one, one, one, one, one, one, S((1, width), f32),
         ),
-        in_specs=[VMEM, ANY] + [VMEM] * 4,
+        in_specs=[VMEM, ANY, ANY] + [VMEM] * 6,
         out_specs=[VMEM] * 14,
         scratch_shapes=[vmem((4, width, PACK)), pltpu.SemaphoreType.DMA((4,))],
         compiler_params=pltpu.CompilerParams(vmem_limit_bytes=VMEM_BYTES),
-    )(dproj, wq_full, gh1, gw, fin, sums)
+    )(dproj, wq_full, wq, gh1, gw, hw, fin, finb, sums)
 
 
 def planned(
@@ -956,22 +1112,20 @@
     w_in, in_bias, w_back, back_bias, ln2_gain, ln2_bias, cotangent,
 ):
     width = tokens.shape[2]
-    shard = q_bias.shape[0]
-    gap, half = jnp.zeros((width - shard,), bf16), jnp.zeros((64,), bf16)
-    vectors = []
-    for a in (out_bias, ln1_gain, ln1_bias, back_bias, ln2_gain, ln2_bias):
-        vectors += [a, gap]
-    vectors += [in_bias, half, v_bias[0:64], half, v_bias[64:128], q_bias, half, half, v_bias[128:192]]
-    vectors += [jnp.zeros((width - PACK + 8 * width,), bf16)]
-    small = jnp.concatenate(vectors).reshape(16, width)
-    q, k, v, o, tok_all, att, small_all, full_in, full_back, full_out, wq_full = run_forward(
+    line = lambda *a: jnp.concatenate(a + (jnp.zeros((width - sum(x.shape[0] for x in a),), bf16),))
+    gap = jnp.zeros((64,), bf16)
+    small = jnp.stack([
+        jnp.concatenate([out_bias, ln1_gain, ln1_bias, back_bias]), line(ln2_gain, ln2_bias), in_bias,
+        line(gap, v_bias[0:64], gap, v_bias[64:128], q_bias, gap, gap, v_bias[128:192]),
+    ] + [jnp.zeros((width,), bf16)] * 12)
+    q, k, v, o, tok_all, att, small_all, full_in, full_out, wq, full_back, wq_full = run_forward(
         lengths, tokens[0], w_qkv, w_in, w_back, w_out, small
     )
-    output, gh1, do, grads, sums = run_ffn(
-        lengths, att, tokens[0], cotangent[0], full_in, full_back, full_out, small_all
-    )
-    dproj, gw, fin, sums_f = run_backward(do, q, k, v, o, tok_all, grads, sums)
-    gt, gqkv, gin, gback, gout, qb, vb, ob, g1, b1, bb, g2, b2, ib = run_final(dproj, wq_full, gh1, gw, fin, sums_f)
+    output, gh1, do, grads, sums, wq_full, back = run_ffn(
+        lengths, att, tokens[0], cotangent[0], full_in, w_in, full_out, w_out, small_all, full_back, w_back, wq_full
+    )
+    dproj, gw, hw, fin, finb, sums_f = run_backward(do, q, k, v, o, tok_all, grads, sums, back)
+    gt, gqkv, gin, gback, gout, qb, vb, ob, g1, b1, bb, g2, b2, ib = run_final(dproj, wq_full, wq, gh1, gw, hw, fin, finb, sums_f)
     flat = lambda a: a.reshape(a.shape[1])
     return (
         output[None], gt[None], gqkv, flat(qb), flat(vb), gout, flat(ob), flat(g1), flat(b1), gin, flat(ib),

time: 260 us -> 241 us (0.927)
  Pallas kernels: 250 us -> 230 us
    pallas_call x1, Pallas kernels: 110 us -> 84.2 us  [run_backward(): pl.pallas_call(backward_kernel, out_shape=(S((4, rows, PACK), bf16), S((2...]
    pallas_call x1, Pallas kernels: 37.4 us -> 59.6 us  [run_ffn(): pl.pallas_call(ffn_kernel, out_shape=(one, S((rows, width), f32), S((4, r...]
    pallas_call x1, Pallas kernels: 93.9 us -> 76.7 us  [run_forward(): pl.pallas_call(forward_kernel, out_shape=(S(q_shape, bf16), S(kv_shape, b...]
    concatenate x2 -> x1, local copies, waits for them, and re-layouts: 5.45 us -> 0.76 us  [planned(): jnp.concatenate(a + (jnp.zeros((width - sum((x.shape[0] for x in a)),), b...]
where the time goes in v2:
time: 241 us; the launch traced here: 238 us
  Pallas kernels  230 us (95%)
  local copies, waits for them, and re-layouts  4.38 us (2%)
  other arithmetic  2.82 us (1%)
    pallas_call x1, Pallas kernels, run_backward(): pl.pallas_call(backward_kernel, out_shape=(S((4, rows, PACK), bf16), S((2...  84.2 us
    pallas_call x1, Pallas kernels, run_forward(): pl.pallas_call(forward_kernel, out_shape=(S(q_shape, bf16), S(kv_shape, b...  76.7 us
    pallas_call x1, Pallas kernels, run_ffn(): pl.pallas_call(ffn_kernel, out_shape=(one, S((rows, width), f32), S((4, r...  59.6 us
    pallas_call x1, Pallas kernels, run_final(): pl.pallas_call(final_kernel, out_shape=(S((rows, width), bf16), S((shard,...  8.98 us

profile of v2, /device:TPU:1, one launch (start us, length us, event | category | flops | bytes accessed | tf_op | source)
XLA Modules:
  0.0 238.1 jit_solution(17637832231213909201)
XLA Ops:
  1.3 0.8 pad_maximum_fusion.1
  2.1 0.8 fusion
  2.9 0.8 concatenate.11
  3.7 0.8 pad_maximum_fusion
  4.5 0.7 stack.23
  5.2 1.2 stack.27.small_ref
  6.4 76.7 %shard_map.271 = (bf16[3,1536,128]{2,1,0:T(8,128)(2,1)}, bf16[3,3072,128]{2,1,0:T(8,128)(2,1)}, bf16[3,3072,128]{2,1,0:T(8,128)(2,1)}, bf16[3,1536,128]{2,1,0:T(...) custom-call(s32[1]{0:T(128)S(6)} %copy.34.length_ref, ...), custom_call_target="tpu_custom_call" | custom-call | tf_op jit(solution)/shard_map/pallas_call | solution.py:1014
  83.1 59.6 %shard_map.272 = (bf16[384,768]{1,0:T(8,128)(2,1)}, f32[384,768]{1,0:T(8,128)}, bf16[4,384,256]{2,1,0:T(8,128)(2,1)}, bf16[2,4,4,240,384]{4,3,2,1,0:T(8,128)(2,1...) custom-call(s32[1]{0:T(128)S(6)} %copy.34.length_ref, ...), custom_call_target="tpu_custom_call", output_to_operand_aliasing={{5}: (11, {})} | custom-call | tf_op jit(solution)/shard_map/pallas_call | solution.py:1070
  142.8 84.2 %shard_map.273 = (bf16[4,384,640]{2,1,0:T(8,128)(2,1)}, bf16[2,4,112,384]{3,2,1,0:T(8,128)(2,1)}, bf16[2,4,112,256]{3,2,1,0:T(8,128)(2,1)}, bf16[2,4,240,384]{3,...) custom-call(bf16[4,384,256]{2,1,0:T(8,128)(2,1)} %get-tuple-element.61.do_ref, ...), custom_call_target="tpu_custom_call" | custom-call | tf_op jit(solution)/shard_map/pallas_call | solution.py:1041
  227.0 0.0 copy-start
  227.0 9.0 %shard_map.274 = (bf16[384,768]{1,0:T(8,128)(2,1)}, f32[192,2304]{1,0:T(8,128)}, f32[192,3072]{1,0:T(8,128)}, f32[768,768]{1,0:T(8,128)}, f32[192,768]{1,0:T(8,1...) custom-call(bf16[4,384,640]{2,1,0:T(8,128)(2,1)} %get-tuple-element., ...), custom_call_target="tpu_custom_call" | custom-call | tf_op jit(solution)/shard_map/pallas_call | solution.py:1097
  236.0 1.3 reduce
  237.3 0.0 copy-done
  237.3 0.8 copy.35
  (8 shorter events, 0.0 us)
Async XLA Ops:
  227.0 10.3 %copy-start = (bf16[384,768]{1,0:T(8,128)(2,1)S(1)}, bf16[384,768]{1,0:T(8,128)(2,1)}, u32[]{:S(2)}) copy-start(bf16[384,768]{1,0:T(8,128)(2,1)} %get-tuple-element.60) | copy-start | bytes 1769476

commit v3 on v2

--- a/solution.py
+++ b/solution.py
@@ -22,6 +22,15 @@
 PACKED = (12, 24, 13, 25, 0, 1, 2, None, 14, 26)
 KV_TILE = (0, 1, 4)
 PACK = 640
+
+
+(
+    K_ACC, K_ATT0, K_ATT1, K_ATT_O, K_B1, K_B2, K_B3X, K_B3Y, K_BACK, K_BACK_O, K_BM, K_DO, K_DO_O, K_DP,
+    K_DP_O, K_F, K_F1, K_F2, K_F3X, K_F3Y, K_FINB_O, K_FIN_O, K_FM, K_G, K_GW_O, K_H, K_HW_O, K_IN, K_K, K_KV,
+    K_K_O, K_M, K_O, K_OUT, K_O_O, K_Q, K_QKV, K_Q_O, K_R1, K_RAW, K_RZ, K_RZB, K_S0, K_S1, K_S2, K_SMALL,
+    K_SMALL_O, K_SUMS, K_SUMS_O, K_SZ, K_T1A, K_T1B, K_T2A, K_T2B, K_T3A, K_T3B, K_TOK, K_TOK_O, K_V, K_V_O,
+    K_WQ, K_WQM, K_WQ_O, K_X1, K_X2, K_Y1, K_Y2, K_Z,
+) = range(100, 168)
 
 
 def dot(a, b, dims=NN):
@@ -81,6 +90,72 @@
             self.get(name).wait()
 
 
+class Line:
+    def __init__(self, s, z, send_sems, recv_sems):
+        high = lax.div(z, 2)
+        self.s, self.z = s, z
+        self.order = [z, 1 - z + 4 * high, 2 - high, 3 - 3 * high]
+        self.has_right, self.has_left = z < PLANES - 1, z > 0
+        self.right, self.left = jnp.minimum(z + 1, PLANES - 1), jnp.maximum(z - 1, 0)
+        self.middle = jnp.logical_and(self.has_right, self.has_left)
+        self.end = jnp.logical_not(self.middle)
+        self.send_sems, self.recv_sems = send_sems, recv_sems
+        self.specs = {}
+
+    def add(self, name, own, place):
+        self.specs[name] = (len(self.specs), own, place)
+
+    def copy(self, name, i, to_right=False):
+        n, own, place = self.specs[name]
+        zz = self.order[i]
+        if i:
+            target = jnp.where(zz < self.z, self.right, self.left)
+        else:
+            target = self.right if to_right else self.left
+        return pltpu.make_async_remote_copy(
+            src_ref=place(zz) if i else own(),
+            dst_ref=place(zz),
+            send_sem=self.send_sems.at[n * 5 + (i + 1 if i else int(to_right))],
+            recv_sem=self.recv_sems.at[n * PLANES + zz],
+            device_id=(self.s, target),
+            device_id_type=MESH,
+        )
+
+    def start(self, *names):
+        for name in names:
+            pl.when(self.has_right)(lambda: self.copy(name, 0, True).start())
+            pl.when(self.has_left)(lambda: self.copy(name, 0).start())
+
+    def pass_on(self, name, i):
+        self.copy(name, i).wait_recv()
+        self.copy(name, i).start()
+
+    def step(self, n, *names):
+        for name in names:
+            if n == 1:
+                @pl.when(self.middle)
+                def _():
+                    self.pass_on(name, 1)
+                    self.pass_on(name, 2)
+
+                pl.when(self.end)(lambda: self.copy(name, 1).wait_recv())
+            elif n == 2:
+                pl.when(self.middle)(lambda: self.pass_on(name, 3))
+                pl.when(self.end)(lambda: self.copy(name, 2).wait_recv())
+            else:
+                pl.when(self.end)(lambda: self.copy(name, 3).wait_recv())
+
+    def sent(self):
+        for name in self.specs:
+            pl.when(self.has_right)(lambda: self.copy(name, 0, True).wait_send())
+            pl.when(self.has_left)(lambda: self.copy(name, 0).wait_send())
+
+            @pl.when(self.middle)
+            def _():
+                for i in (1, 2, 3):
+                    self.copy(name, i).wait_send()
+
+
 def coordinates():
     s, z = lax.axis_index("seq"), lax.axis_index("fsdp")
     core = lax.rem(s, 2)
@@ -124,8 +199,8 @@
 
 def forward_kernel(
     length_ref, tok_ref, wraw_ref, win_ref, wback_ref, wout_ref, small_ref,
-    q_out, k_out, v_out, o_out, tok_out, att_out, small_out, win_full, wout_full, wq_out, wback_full, wq_full,
-    tok, wqv, q_s, k_s, v_s, o_s, att, atts, kvs, kvr, small, wraw, wq_ref, send_sems, recv_sems, local_sems,
+    q_out, k_out, v_out, o_out, tok_out, att_out, small_out, win_full, wout_full, wq_out, wback_full,
+    tok, wqv, q_s, k_s, v_s, o_s, att, atts, kvs, kvr, small, wraw, wq_ref, send_sems, recv_sems, line_send, line_recv, local_sems,
 ):
     s, z, core, chip = coordinates()
     other = 1 - core
@@ -141,73 +216,77 @@
     width = win_full.shape[1] // 8
     back = wback_ref.shape[0]
     bpiece = back // 8
-    arrays = ("out", "in", "back")
+    hops = [(K_IN, 1), (K_IN, 2), (K_IN, 3), (K_BACK, 1)]
     at = lambda start, size, unit=16: pl.ds(pl.multiple_of(start, unit), size)
 
     def part(a, zz, m, c):
-        if a == "in":
+        if a == K_IN:
             return win_full.at[at(zz * shard, shard), at((m * 4 + c) * width, width, 128)]
-        if a == "back":
+        if a == K_BACK:
             return wback_full.at[at(zz * back + (m * 4 + c) * bpiece, bpiece), :]
         return wout_full.at[at(zz * shard + c * (shard // 4), shard // 4), at(m * width, width, 128)]
 
     def own_part(a, m, c):
-        if a == "in":
+        if a == K_IN:
             return win_ref.at[:, at((m * 4 + c) * width, width, 128)]
-        if a == "back":
+        if a == K_BACK:
             return wback_ref.at[at((m * 4 + c) * bpiece, bpiece), :]
         return wout_ref.at[at(c * (shard // 4), shard // 4), at(m * width, width, 128)]
 
     def side(a, zz, m):
-        if a == "in":
+        if a == K_IN:
             return win_full.at[at(zz * shard, shard), at(m * 4 * width, 4 * width, 128)]
-        if a == "back":
+        if a == K_BACK:
             return wback_full.at[at(zz * back + m * 4 * bpiece, 4 * bpiece), :]
         return wout_full.at[at(zz * shard, shard), at(m * width, width, 128)]
 
+    line = Line(s, z, line_send, line_recv)
+    lines = line.order
+    for a in (K_IN, K_BACK):
+        line.add(a, lambda a=a: own_part(a, core, chip), lambda zz, a=a: part(a, zz, core, chip))
+    line.add(K_OUT, lambda: wout_ref.at[:, at(core * width, width, 128)], lambda zz: side(K_OUT, zz, core))
+
     for dz in (1, 2, 3):
-        net.add(("wq", dz), lambda: wq_ref.at[chip, pl.ds(pl.multiple_of(core * piece, 16), piece), :],
+        net.add((K_WQ, dz), lambda: wq_ref.at[chip, pl.ds(pl.multiple_of(core * piece, 16), piece), :],
                 lambda: wqv.at[pl.ds(pl.multiple_of(z * shard + core * piece, 16), piece), :], plane[dz])
-        net.add(("wqm", dz), lambda dz=dz: wqv.at[pl.ds(pl.multiple_of(zs[dz] * shard + core * piece, 16), piece), :],
+        net.add((K_WQM, dz), lambda dz=dz: wqv.at[pl.ds(pl.multiple_of(zs[dz] * shard + core * piece, 16), piece), :],
                 lambda dz=dz: wqv.at[pl.ds(pl.multiple_of(zs[dz] * shard + core * piece, 16), piece), :], mate)
-        net.add(("small", dz), lambda: small_ref, lambda: small.at[z], plane[dz])
+        net.add((K_SMALL, dz), lambda: small_ref, lambda: small.at[z], plane[dz])
     top, bottom = slice(0, half), slice(half, rows)
-    net.add("t1a", lambda: tok_ref.at[top], lambda: tok.at[1, top], peer[1])
-    net.add("t1b", lambda: tok_ref.at[bottom], lambda: tok.at[1, bottom], peer[1])
-    net.add("t2b", lambda: tok_ref.at[bottom], lambda: tok.at[2, bottom], peer[2])
-    net.add("t2a", lambda: tok_ref.at[top], lambda: tok.at[2, top], peer[2])
-    net.add("t3a", lambda: tok.at[1, top], lambda: tok.at[3, top], peer[2])
-    net.add("t3b", lambda: tok.at[2, bottom], lambda: tok.at[3, bottom], peer[1])
+    net.add(K_T1A, lambda: tok_ref.at[top], lambda: tok.at[1, top], peer[1])
+    net.add(K_T1B, lambda: tok_ref.at[bottom], lambda: tok.at[1, bottom], peer[1])
+    net.add(K_T2B, lambda: tok_ref.at[bottom], lambda: tok.at[2, bottom], peer[2])
+    net.add(K_T2A, lambda: tok_ref.at[top], lambda: tok.at[2, top], peer[2])
+    net.add(K_T3A, lambda: tok.at[1, top], lambda: tok.at[3, top], peer[2])
+    net.add(K_T3B, lambda: tok.at[2, bottom], lambda: tok.at[3, bottom], peer[1])
     for j in range(4):
-        net.add(("kv", j), lambda j=j: kvs.at[j], lambda j=j: kvr.at[j], mate)
+        net.add((K_KV, j), lambda j=j: kvs.at[j], lambda j=j: kvr.at[j], mate)
     for j in (1, 2, 3):
-        net.add(("att0", j), lambda j=j: atts.at[j, :, 0:128], lambda: att.at[chip, :, 0:128], peer[j])
-        net.add(("att1", j), lambda j=j: atts.at[j, :, 128:256], lambda: att.at[chip, :, 128:256], peer[j])
-    for a in arrays:
-        via, last = (1, 2) if a == "in" else (2, 1)
-        for dz in (1, 2, 3):
-            net.add((a, "z", dz), lambda a=a: own_part(a, core, chip), lambda a=a: part(a, z, core, chip), plane[dz])
-            for j in (1, 2):
-                net.add((a, j, dz), lambda a=a, dz=dz: part(a, zs[dz], core, chip), lambda a=a, dz=dz: part(a, zs[dz], core, chip), peer[j])
-            net.add((a, 3, dz), lambda a=a, dz=dz, via=via: part(a, zs[dz], core, flip(chip, via)),
-                    lambda a=a, dz=dz, via=via: part(a, zs[dz], core, flip(chip, via)), peer[last])
-            net.add((a, "m", dz), lambda a=a, dz=dz: side(a, zs[dz], core), lambda a=a, dz=dz: side(a, zs[dz], core), mate)
-    for dz in (1, 2, 3):
-        net.add(("qkv", "z", dz), lambda: wq_ref.at[core * 2 + lax.div(chip, 2), pl.ds(pl.multiple_of(lax.rem(chip, 2) * piece, 16), piece), :],
-                lambda: wq_full.at[z, core * 2 + lax.div(chip, 2), pl.ds(pl.multiple_of(lax.rem(chip, 2) * piece, 16), piece), :], plane[dz])
-    loc.add("raw", lambda: wraw_ref, lambda: wraw)
-    loc.add("tok", lambda: tok_ref, lambda: tok.at[0])
-    loc.add("wq", lambda: wq_ref.at[chip], lambda: wqv.at[pl.ds(pl.multiple_of(z * shard, 16), shard), :])
-    loc.add("small", lambda: small_ref, lambda: small.at[z])
-    outs = (("wq_o", wq_ref, wq_out), ("k_o", k_s, k_out), ("v_o", v_s, v_out), ("q_o", q_s, q_out), ("o_o", o_s, o_out),
-            ("tok_o", tok, tok_out), ("att_o", att, att_out), ("small_o", small, small_out))
+        net.add((K_ATT0, j), lambda j=j: atts.at[j, :, 0:128], lambda: att.at[chip, :, 0:128], peer[j])
+        net.add((K_ATT1, j), lambda j=j: atts.at[j, :, 128:256], lambda: att.at[chip, :, 128:256], peer[j])
+    for a, dz in hops:
+        via, last = (1, 2) if a == K_IN else (2, 1)
+        for j in (1, 2):
+            net.add((a, j, dz), lambda a=a, dz=dz: part(a, lines[dz], core, chip), lambda a=a, dz=dz: part(a, lines[dz], core, chip), peer[j])
+        net.add((a, 3, dz), lambda a=a, dz=dz, via=via: part(a, lines[dz], core, flip(chip, via)),
+                lambda a=a, dz=dz, via=via: part(a, lines[dz], core, flip(chip, via)), peer[last])
+    mates = hops + [(K_OUT, dz) for dz in (1, 2, 3)]
+    for a, dz in mates:
+        net.add((a, K_M, dz), lambda a=a, dz=dz: side(a, lines[dz], core), lambda a=a, dz=dz: side(a, lines[dz], core), mate)
+    loc.add(K_RAW, lambda: wraw_ref, lambda: wraw)
+    loc.add(K_TOK, lambda: tok_ref, lambda: tok.at[0])
+    loc.add(K_WQ, lambda: wq_ref.at[chip], lambda: wqv.at[pl.ds(pl.multiple_of(z * shard, 16), shard), :])
+    loc.add(K_SMALL, lambda: small_ref, lambda: small.at[z])
+    outs = ((K_WQ_O, wq_ref, wq_out), (K_K_O, k_s, k_out), (K_V_O, v_s, v_out), (K_Q_O, q_s, q_out), (K_O_O, o_s, o_out),
+            (K_TOK_O, tok, tok_out), (K_ATT_O, att, att_out), (K_SMALL_O, small, small_out))
     for name, src, dst in outs:
         loc.add(name, lambda src=src: src, lambda dst=dst: dst)
 
-    loc.start("raw", "tok", "small")
-    hello(peer[1:] + [mate] + plane[1:])
+    loc.start(K_RAW, K_TOK, K_SMALL)
+    greet(peer[1:] + [mate] + plane[1:])
+    net.start(K_T1A, K_T2B, K_T1B, K_T2A)
     lane = lanes_of()
-    loc.wait("raw")
+    loc.wait(K_RAW)
     for g in range(CHIPS):
         for t in range(PACK // 128):
             halves = []
@@ -220,18 +299,15 @@
                 tile_of = lambda i: wraw[:, i * 128 : (i + 1) * 128].astype(f32)
                 halves.append(half_tile(tile_of, block, upper))
             wq_ref[g, :, t * 128 : (t + 1) * 128] = jnp.where(lane < 64, halves[0], halves[1]).astype(bf16)
-    loc.start("wq", "wq_o")
-    met(len(peer[1:] + [mate] + plane[1:]))
-    net.start(*[("wq", dz) for dz in (1, 2, 3)], *[("small", dz) for dz in (1, 2, 3)])
-    net.start("t1a", "t2b", "t1b", "t2a")
+    loc.start(K_WQ, K_WQ_O)
+    net.start(*[(K_WQ, dz) for dz in (1, 2, 3)], *[(K_SMALL, dz) for dz in (1, 2, 3)])
     for dz in (1, 2, 3):
-        net.recv(("wq", dz))
-        net.start(("wqm", dz))
+        net.recv((K_WQ, dz))
+        net.start((K_WQM, dz))
+    line.start(K_OUT, K_IN)
+    loc.wait(K_TOK, K_WQ, K_SMALL)
     for dz in (1, 2, 3):
-        net.start(*[(a, "z", dz) for a in arrays])
-    loc.wait("tok", "wq", "small")
-    for dz in (1, 2, 3):
-        net.recv(("small", dz), ("wqm", dz))
+        net.recv((K_SMALL, dz), (K_WQM, dz))
 
     length = length_ref[0]
     bias = small[chip, 3:4, 0:PACK].astype(f32)
@@ -260,49 +336,48 @@
             q_s[h, j * rows : (j + 1) * rows, :] = jnp.where(
                 lane < 64, tile, jnp.where(lane == 64, 1.0, 0.0)
             ).astype(bf16)
-        net.start(("kv", j))
+        net.start((K_KV, j))
 
     def keep_other(j):
-        net.recv(("kv", j))
+        net.recv((K_KV, j))
         for h in range(GROUP_HEADS):
             tile = kvr[j, :, h * 128 : (h + 1) * 128].astype(f32)
             keep(tile, h, 4 + j, flip(chip, j) * 2 + other)
 
+    def first_hop(a, dz):
+        net.start((a, 1, dz), (a, 2, dz))
+
+    def second_hop(a, dz):
+        net.recv((a, 1, dz), (a, 2, dz))
+        net.start((a, 3, dz))
+
+    def third_hop(a, dz):
+        net.recv((a, 3, dz))
+        net.start((a, K_M, dz))
+
     project(0)
-    net.recv("t1a")
-    net.start("t3a")
-    net.recv("t2b")
-    net.start("t3b")
-    net.recv("t1b")
+    net.recv(K_T1A)
+    net.start(K_T3A)
+    net.recv(K_T2B)
+    net.start(K_T3B)
+    net.recv(K_T1B)
     project(1)
-    net.recv("t2a")
+    net.recv(K_T2A)
     project(2)
     keep_other(0)
     keep_other(1)
     keep_other(2)
-    net.recv("t3a", "t3b")
+    line.step(1, K_OUT, K_IN)
+    line.start(K_BACK)
+    first_hop(K_IN, 1)
+    net.recv(K_T3A, K_T3B)
     project(3)
     keep_other(3)
-    loc.start("k_o", "v_o", "tok_o", "small_o")
+    loc.start(K_K_O, K_V_O, K_TOK_O, K_SMALL_O)
 
     query_tile, key_chunk = 2 * rows, 4 * rows
     tiles = 4 * rows // query_tile
     chunks = 8 * rows // key_chunk
-
-    def first_hop(dz):
-        for a in arrays:
-            net.recv((a, "z", dz))
-            net.start((a, 1, dz), (a, 2, dz))
-
-    def second_hop(dz):
-        for a in arrays:
-            net.recv((a, 1, dz), (a, 2, dz))
-            net.start((a, 3, dz))
-
-    def third_hop(dz):
-        for a in arrays:
-            net.recv((a, 3, dz))
-            net.start((a, "m", dz))
 
     def attended_tile(which):
         for j in range(4):
@@ -317,7 +392,25 @@
                 att[chip, :, place] = value.astype(bf16)
             else:
                 atts[j, :, place] = value.astype(bf16)
-                net.start((f"att{which}", j))
+                net.start(((K_ATT0, K_ATT1)[which], j))
+
+    stages = {
+        0: lambda: (line.step(2, K_OUT, K_IN), first_hop(K_IN, 2), line.step(1, K_BACK)),
+        2: lambda: second_hop(K_IN, 1),
+        3: lambda: (line.step(3, K_OUT, K_IN), first_hop(K_IN, 3), [net.start((K_OUT, K_M, dz)) for dz in (1, 2, 3)]),
+        4: lambda: (line.step(2, K_BACK), second_hop(K_IN, 2), first_hop(K_BACK, 1)),
+        5: lambda: third_hop(K_IN, 1),
+        6: lambda: third_hop(K_IN, 2),
+        7: lambda: attended_tile(0),
+        8: lambda: (second_hop(K_IN, 3), line.step(3, K_BACK)),
+        9: lambda: second_hop(K_BACK, 1),
+        10: lambda: third_hop(K_IN, 3),
+        11: lambda: (attended_tile(1), third_hop(K_BACK, 1)),
+    }
+
+    def progress(n):
+        for at, work in stages.items():
+            pl.when(n == at)(lambda work=work: (work(), None)[1])
 
     def visit(t, carry):
         h, i = lax.div(t, tiles), lax.rem(t, tiles)
@@ -333,36 +426,26 @@
             fade = jnp.exp2((top_score - new_top) * LOG2E)
             acc = acc * fade + dot(probs.astype(bf16), v_s[h, krows, :])
             top_score = new_top
+            if c < chunks - 1:
+                progress(t * chunks + c)
         total = acc[:, 64:65]
         o_s[h, qrows, :] = (acc / total).astype(bf16)
         hi, mid, low = split3(-(top_score + jnp.log(total)))
         wide = q.astype(f32)
         wide = jnp.where(lane == 65, hi, jnp.where(lane == 66, mid, jnp.where(lane == 67, low, wide)))
         q_s[h, qrows, :] = wide.astype(bf16)
-
-        for at, work in enumerate((
-            lambda: first_hop(1),
-            lambda: (first_hop(2), second_hop(1)),
-            lambda: (first_hop(3), net.start(*[("qkv", "z", dz) for dz in (1, 2, 3)]), second_hop(2), third_hop(1)),
-            lambda: (attended_tile(0), second_hop(3)),
-            lambda: third_hop(2),
-            lambda: attended_tile(1),
-        )):
-            pl.when(t == at)(lambda work=work: (work(), None)[1])
+        progress(t * chunks + chunks - 1)
         return carry
 
     lax.fori_loop(0, GROUP_HEADS * tiles, visit, 0)
-    third_hop(3)
-    loc.start("q_o", "o_o")
+    loc.start(K_Q_O, K_O_O)
     for j in (1, 2, 3):
-        net.recv(("att0", j), ("att1", j))
-    loc.start("att_o")
-    for dz in (1, 2, 3):
-        for a in arrays:
-            net.recv((a, "m", dz))
-        net.recv(("qkv", "z", dz))
+        net.recv((K_ATT0, j), (K_ATT1, j))
+    loc.start(K_ATT_O)
+    net.recv(*[(a, K_M, dz) for a, dz in mates])
     for name in net.specs:
         net.sent(name)
+    line.sent()
     loc.wait(*[name for name, _, _ in outs])
 
 
@@ -389,69 +472,69 @@
     piece = shard // 2
 
     for h in range(GROUP_HEADS):
-        net.add(("kv", h), lambda h=h: kvs.at[h], lambda h=h: kvr.at[h], mate)
+        net.add((K_KV, h), lambda h=h: kvs.at[h], lambda h=h: kvr.at[h], mate)
         place = ((0, 128), (128, 384), (384, 640))[h]
         for j in (1, 2, 3):
-            net.add(("dp", h, j), lambda j=j, place=place: dall.at[j, :, place[0] : place[1]],
+            net.add((K_DP, h, j), lambda j=j, place=place: dall.at[j, :, place[0] : place[1]],
                     lambda place=place: dproj.at[chip, :, place[0] : place[1]], peer[j])
     order = (3, 2, 1, 0)
     for dz in order:
-        net.add(("r1", dz), lambda dz=dz: grads_ref.at[other, zs[dz]], lambda dz=dz: rb.at[zs[dz]], mate)
+        net.add((K_R1, dz), lambda dz=dz: grads_ref.at[other, zs[dz]], lambda dz=dz: rb.at[zs[dz]], mate)
         for n, j in enumerate((1, 3)):
-            net.add(("x1", n, dz), lambda dz=dz, j=j: acc.at[zs[dz], ch[j], xs], lambda dz=dz, n=n: rx.at[zs[dz], n], peer[1])
-        net.add(("x2", dz), lambda dz=dz: acc.at[zs[dz], ch[2], xs], lambda dz=dz: rx2.at[zs[dz]], peer[2])
+            net.add((K_X1, n, dz), lambda dz=dz, j=j: acc.at[zs[dz], ch[j], xs], lambda dz=dz, n=n: rx.at[zs[dz], n], peer[1])
+        net.add((K_X2, dz), lambda dz=dz: acc.at[zs[dz], ch[2], xs], lambda dz=dz: rx2.at[zs[dz]], peer[2])
         for n, j in enumerate((2, 3)):
-            net.add(("y1", n, dz), lambda dz=dz, j=j: acc.at[zs[dz], ch[j], ys], lambda dz=dz, n=n: ry.at[zs[dz], n], peer[2])
-        net.add(("y2", dz), lambda dz=dz: acc.at[zs[dz], ch[1], ys], lambda dz=dz: ry2.at[zs[dz]], peer[1])
+            net.add((K_Y1, n, dz), lambda dz=dz, j=j: acc.at[zs[dz], ch[j], ys], lambda dz=dz, n=n: ry.at[zs[dz], n], peer[2])
+        net.add((K_Y2, dz), lambda dz=dz: acc.at[zs[dz], ch[1], ys], lambda dz=dz: ry2.at[zs[dz]], peer[1])
         if dz:
-            net.add(("rz", dz), lambda dz=dz: acc.at[zs[dz], chip], lambda dz=dz: rz.at[dz - 1], plane[dz])
+            net.add((K_RZ, dz), lambda dz=dz: acc.at[zs[dz], chip], lambda dz=dz: rz.at[dz - 1], plane[dz])
     for dz in (1, 2, 3):
-        net.add(("rzb", dz), lambda dz=dz: back_ref.at[zs[dz]], lambda dz=dz: rzb.at[dz], plane[dz])
+        net.add((K_RZB, dz), lambda dz=dz: back_ref.at[zs[dz]], lambda dz=dz: rzb.at[dz], plane[dz])
     bh = finb.shape[2] // 2
     bx, by = slice(0, bh), slice(bh, 2 * bh)
-    net.add("b1", lambda: finb.at[core, chip], lambda: finb.at[core, chip], peer[1])
-    net.add("b2", lambda: finb.at[core, chip], lambda: finb.at[core, chip], peer[2])
-    net.add("b3x", lambda: finb.at[core, ch[1], bx], lambda: finb.at[core, ch[1], bx], peer[2])
-    net.add("b3y", lambda: finb.at[core, ch[2], by], lambda: finb.at[core, ch[2], by], peer[1])
-    net.add("bm", lambda: finb.at[core], lambda: finb.at[core], mate)
-    net.add("f1", lambda: fin.at[core, chip], lambda: fin.at[core, chip], peer[1])
-    net.add("f2", lambda: fin.at[core, chip], lambda: fin.at[core, chip], peer[2])
-    net.add("f3x", lambda: fin.at[core, ch[1], xs], lambda: fin.at[core, ch[1], xs], peer[2])
-    net.add("f3y", lambda: fin.at[core, ch[2], ys], lambda: fin.at[core, ch[2], ys], peer[1])
-    net.add("fm", lambda: fin.at[core], lambda: fin.at[core], mate)
-    net.add("s0", lambda: sums_ref, lambda: sums_r.at[0], mate)
-    net.add("s1", lambda: sums.at[1], lambda: sums_r.at[1], peer[1])
-    net.add("s2", lambda: sums.at[2], lambda: sums_r.at[2], peer[2])
+    net.add(K_B1, lambda: finb.at[core, chip], lambda: finb.at[core, chip], peer[1])
+    net.add(K_B2, lambda: finb.at[core, chip], lambda: finb.at[core, chip], peer[2])
+    net.add(K_B3X, lambda: finb.at[core, ch[1], bx], lambda: finb.at[core, ch[1], bx], peer[2])
+    net.add(K_B3Y, lambda: finb.at[core, ch[2], by], lambda: finb.at[core, ch[2], by], peer[1])
+    net.add(K_BM, lambda: finb.at[core], lambda: finb.at[core], mate)
+    net.add(K_F1, lambda: fin.at[core, chip], lambda: fin.at[core, chip], peer[1])
+    net.add(K_F2, lambda: fin.at[core, chip], lambda: fin.at[core, chip], peer[2])
+    net.add(K_F3X, lambda: fin.at[core, ch[1], xs], lambda: fin.at[core, ch[1], xs], peer[2])
+    net.add(K_F3Y, lambda: fin.at[core, ch[2], ys], lambda: fin.at[core, ch[2], ys], peer[1])
+    net.add(K_FM, lambda: fin.at[core], lambda: fin.at[core], mate)
+    net.add(K_S0, lambda: sums_ref, lambda: sums_r.at[0], mate)
+    net.add(K_S1, lambda: sums.at[1], lambda: sums_r.at[1], peer[1])
+    net.add(K_S2, lambda: sums.at[2], lambda: sums_r.at[2], peer[2])
     for dz in (1, 2, 3):
-        net.add(("sz", dz), lambda dz=dz: sums.at[3, zs[dz]], lambda dz=dz: sums_z.at[dz - 1], plane[dz])
-    for a, w, wr, g, gr, f in (("g", gw, gwr, gz, gzr, gwf), ("h", hw, hwr, hz, hzr, hwf)):
+        net.add((K_SZ, dz), lambda dz=dz: sums.at[3, zs[dz]], lambda dz=dz: sums_z.at[dz - 1], plane[dz])
+    for a, w, wr, g, gr, f in ((K_G, gw, gwr, gz, gzr, gwf), (K_H, hw, hwr, hz, hzr, hwf)):
         net.add((a, 0), lambda w=w: w.at[other], lambda wr=wr: wr, mate)
         for dz in (1, 2, 3):
-            net.add((a, "z", dz), lambda g=g, dz=dz: g.at[zs[dz]], lambda gr=gr, dz=dz: gr.at[dz - 1], plane[dz])
+            net.add((a, K_Z, dz), lambda g=g, dz=dz: g.at[zs[dz]], lambda gr=gr, dz=dz: gr.at[dz - 1], plane[dz])
         for j in (1, 2, 3):
-            net.add((a, "f", j), lambda f=f: f.at[core, chip], lambda f=f: f.at[core, chip], peer[j])
-        net.add((a, "m"), lambda f=f: f.at[core], lambda f=f: f.at[core], mate)
-
-    loads = (("do", lambda: do_ref, lambda: do_s), ("o", lambda: o_ref, lambda: o_s),
-             ("tok", lambda: tok_ref, lambda: tok), ("q", lambda: q_ref, lambda: q_s),
-             ("k", lambda: k_ref, lambda: k_s), ("v", lambda: v_ref, lambda: v_s),
-             ("sums", lambda: sums_ref, lambda: sums.at[0]), ("back", lambda: back_ref.at[z], lambda: rzb.at[0]), ("acc", lambda: grads_ref.at[core], lambda: acc))
+            net.add((a, K_F, j), lambda f=f: f.at[core, chip], lambda f=f: f.at[core, chip], peer[j])
+        net.add((a, K_M), lambda f=f: f.at[core], lambda f=f: f.at[core], mate)
+
+    loads = ((K_DO, lambda: do_ref, lambda: do_s), (K_O, lambda: o_ref, lambda: o_s),
+             (K_TOK, lambda: tok_ref, lambda: tok), (K_Q, lambda: q_ref, lambda: q_s),
+             (K_K, lambda: k_ref, lambda: k_s), (K_V, lambda: v_ref, lambda: v_s),
+             (K_SUMS, lambda: sums_ref, lambda: sums.at[0]), (K_BACK, lambda: back_ref.at[z], lambda: rzb.at[0]), (K_ACC, lambda: grads_ref.at[core], lambda: acc))
     for name, src, dst in loads:
         loc.add(name, src, dst)
-    stores = (("dp_o", dproj, dproj_out), ("gw_o", gwf, gw_out), ("hw_o", hwf, hw_out), ("fin_o", fin, fin_out), ("finb_o", finb, finb_out))
+    stores = ((K_DP_O, dproj, dproj_out), (K_GW_O, gwf, gw_out), (K_HW_O, hwf, hw_out), (K_FIN_O, fin, fin_out), (K_FINB_O, finb, finb_out))
     for name, src, dst in stores:
         loc.add(name, lambda src=src: src, lambda dst=dst: dst)
-    loc.add("sums_o", lambda: sums_f, lambda: sums_out)
+    loc.add(K_SUMS_O, lambda: sums_f, lambda: sums_out)
 
     loc.start(*[name for name, _, _ in loads])
     greet(peer[1:] + [mate] + plane[1:])
-    net.start("s0", *[("r1", dz) for dz in order])
-    net.start(*[("rzb", dz) for dz in (1, 2, 3)])
+    net.start(K_S0, *[(K_R1, dz) for dz in order])
+    net.start(*[(K_RZB, dz) for dz in (1, 2, 3)])
     lane = lanes_of()
-    loc.wait("tok")
+    loc.wait(K_TOK)
     for j in range(4):
         tokt[:, j * rows : (j + 1) * rows] = tok[j].T
-    loc.wait("do", "o", "q", "k", "v", "sums", "back", "acc")
+    loc.wait(K_DO, K_O, K_Q, K_K, K_V, K_SUMS, K_BACK, K_ACC)
     for j in range(4):
         for h in range(GROUP_HEADS):
             tile = do_s[j, :, (h // 2) * 128 : (h // 2) * 128 + 128].astype(f32)
@@ -468,70 +551,70 @@
         ref[index] = (ref[index].astype(f32) + other_ref[other_index].astype(f32)).astype(bf16)
 
     def step_one(dz):
-        net.recv(("r1", dz))
+        net.recv((K_R1, dz))
         def body(c, carry):
             add_into(acc, (zs[dz], c), rb, (zs[dz], c))
             return carry
         lax.fori_loop(0, CHIPS, body, 0)
-        net.start(*[("x1", n, dz) for n in (0, 1)], *[("y1", n, dz) for n in (0, 1)])
+        net.start(*[(K_X1, n, dz) for n in (0, 1)], *[(K_Y1, n, dz) for n in (0, 1)])
 
     def step_two(dz):
         for n in range(2):
-            net.recv(("x1", 1 - n, dz), ("y1", 1 - n, dz))
+            net.recv((K_X1, 1 - n, dz), (K_Y1, 1 - n, dz))
             jx, jy = (2, 1) if n == 0 else (0, 0)
             add_into(acc, (zs[dz], ch[jx], xs), rx, (zs[dz], 1 - n))
             add_into(acc, (zs[dz], ch[jy], ys), ry, (zs[dz], 1 - n))
             if n == 0:
-                net.start(("x2", dz), ("y2", dz))
+                net.start((K_X2, dz), (K_Y2, dz))
 
     def step_three(dz):
-        net.recv(("x2", dz), ("y2", dz))
+        net.recv((K_X2, dz), (K_Y2, dz))
         add_into(acc, (zs[dz], chip, xs), rx2, zs[dz])
         add_into(acc, (zs[dz], chip, ys), ry2, zs[dz])
         if dz:
-            net.start(("rz", dz))
+            net.start((K_RZ, dz))
 
     def sums_step(n):
-        net.recv(f"s{n}")
+        net.recv((K_S0, K_S1, K_S2)[n])
         sums[n + 1] = (sums[n].astype(f32) + sums_r[n].astype(f32)).astype(bf16)
         if n < 2:
-            net.start(f"s{n + 1}")
+            net.start((K_S1, K_S2)[n])
         else:
-            net.start(*[("sz", dz) for dz in (1, 2, 3)])
+            net.start(*[(K_SZ, dz) for dz in (1, 2, 3)])
 
     def back_total():
-        net.recv(*[("rzb", dz) for dz in (1, 2, 3)])
+        net.recv(*[(K_RZB, dz) for dz in (1, 2, 3)])
         total = rzb[0].astype(f32) + rzb[1].astype(f32) + rzb[2].astype(f32) + rzb[3].astype(f32)
         finb[core, chip] = total.astype(bf16)
-        net.start("b1", "b2")
+        net.start(K_B1, K_B2)
 
     def back_forward():
-        net.recv("b1")
-        net.start("b3x")
-        net.recv("b2")
-        net.start("b3y")
+        net.recv(K_B1)
+        net.start(K_B3X)
+        net.recv(K_B2)
+        net.start(K_B3Y)
 
     def back_mate():
-        net.recv("b3x", "b3y")
-        net.start("bm")
+        net.recv(K_B3X, K_B3Y)
+        net.start(K_BM)
 
     def fin_total():
         for dz in (1, 2, 3):
-            net.recv(("rz", dz), ("sz", dz))
+            net.recv((K_RZ, dz), (K_SZ, dz))
         total = acc[z, chip].astype(f32) + rz[0].astype(f32) + rz[1].astype(f32) + rz[2].astype(f32)
         fin[core, chip] = total.astype(bf16)
-        net.start("f1", "f2")
+        net.start(K_F1, K_F2)
         total = sums[3, z].astype(f32)
         for n in range(3):
             total = total + sums_z[n].astype(f32)
         sums_f[...] = total.astype(bf16)
-        loc.start("sums_o")
+        loc.start(K_SUMS_O)
 
     def fin_forward():
-        net.recv("f1")
-        net.start("f3x")
-        net.recv("f2")
-        net.start("f3y")
+        net.recv(K_F1)
+        net.start(K_F3X)
+        net.recv(K_F2)
+        net.start(K_F3Y)
 
     def weight_part(a, w, first, last):
         cols = dall[:, :, first:last].reshape(4 * rows, last - first)
@@ -548,25 +631,25 @@
         net.recv((a, 0))
         for zz in range(PLANES):
             g[zz] = (w[core, zz].astype(f32) + wr[zz].astype(f32)).astype(bf16)
-        net.start(*[(a, "z", dz) for dz in (1, 2, 3)])
+        net.start(*[(a, K_Z, dz) for dz in (1, 2, 3)])
 
     def weight_total(a, g, gr, f):
         total = g[z].astype(f32)
         for dz in (1, 2, 3):
-            net.recv((a, "z", dz))
+            net.recv((a, K_Z, dz))
             total = total + gr[dz - 1].astype(f32)
         f[core, chip] = total.astype(bf16)
-        net.start(*[(a, "f", j) for j in (1, 2, 3)])
+        net.start(*[(a, K_F, j) for j in (1, 2, 3)])
 
     def weight_mate(a):
-        net.recv(*[(a, "f", j) for j in (1, 2, 3)])
-        net.start((a, "m"))
+        net.recv(*[(a, K_F, j) for j in (1, 2, 3)])
+        net.start((a, K_M))
 
     key_chunk, query_tile = 2 * rows, 256
     per_head = 4
 
     def head_end(h):
-        net.recv(("kv", h))
+        net.recv((K_KV, h))
         tile = KV_TILE[h]
         dst = (0, 1, 4)[h] * 128
         for j in range(4):
@@ -584,7 +667,7 @@
             else:
                 dall[j, :, 384:512] = jnp.where(lane < 64, mine, 0.0).astype(bf16)
         for j in (1, 2, 3):
-            net.start(("dp", h, j))
+            net.start((K_DP, h, j))
 
     stages = {
         0: lambda: (step_one(3), sums_step(0)),
@@ -594,10 +677,10 @@
         4: lambda: (step_one(0), back_total()),
         5: lambda: (step_three(2), step_two(1)),
         6: lambda: (step_two(0), back_forward()),
-        7: lambda: (step_three(1), weight_part("g", gw, 0, 384)),
+        7: lambda: (step_three(1), weight_part(K_G, gw, 0, 384)),
         8: lambda: (step_three(0), back_mate()),
-        9: lambda: (fin_total(), weight_pair("g", gw, gwr, gz)),
-        11: lambda: (fin_forward(), weight_total("g", gz, gzr, gwf)),
+        9: lambda: (fin_total(), weight_pair(K_G, gw, gwr, gz)),
+        11: lambda: (fin_forward(), weight_total(K_G, gz, gzr, gwf)),
     }
 
     def visit(t, carry):
@@ -634,7 +717,7 @@
         for hh in range(GROUP_HEADS):
             @pl.when(t == hh * per_head + 1)
             def _(hh=hh):
-                net.start(("kv", hh))
+                net.start((K_KV, hh))
 
             @pl.when(t == hh * per_head + 3)
             def _(hh=hh):
@@ -645,24 +728,24 @@
 
     lax.fori_loop(0, GROUP_HEADS * per_head, visit, 0)
 
-    weight_part("h", hw, 384, PACK)
+    weight_part(K_H, hw, 384, PACK)
     dproj[chip] = dall[0]
-    weight_pair("h", hw, hwr, hz)
-    weight_mate("g")
-    net.recv("f3x", "f3y")
-    net.start("fm")
-    weight_total("h", hz, hzr, hwf)
+    weight_pair(K_H, hw, hwr, hz)
+    weight_mate(K_G)
+    net.recv(K_F3X, K_F3Y)
+    net.start(K_FM)
+    weight_total(K_H, hz, hzr, hwf)
     for h in range(GROUP_HEADS):
         for j in (1, 2, 3):
-            net.recv(("dp", h, j))
-    net.recv("fm", "bm", ("g", "m"))
-    loc.start("dp_o", "gw_o", "fin_o", "finb_o")
-    weight_mate("h")
-    net.recv(("h", "m"))
-    loc.start("hw_o")
+            net.recv((K_DP, h, j))
+    net.recv(K_FM, K_BM, (K_G, K_M))
+    loc.start(K_DP_O, K_GW_O, K_FIN_O, K_FINB_O)
+    weight_mate(K_H)
+    net.recv((K_H, K_M))
+    loc.start(K_HW_O)
     for name in net.specs:
         net.sent(name)
-    loc.wait("dp_o", "gw_o", "hw_o", "fin_o", "finb_o", "sums_o")
+    loc.wait(K_DP_O, K_GW_O, K_HW_O, K_FIN_O, K_FINB_O, K_SUMS_O)
 
 
 def gelu_parts(u):
@@ -695,10 +778,10 @@
 
 
 def ffn_kernel(
-    length_ref, att_ref, tok_ref, cot_ref, win_ref, win_own, wout_ref, wout_own, small_ref, wback_ref, wback_own, wq_in,
+    length_ref, att_ref, tok_ref, cot_ref, win_ref, win_own, wout_ref, wout_own, small_ref, wback_ref, wback_own, wq_own,
     out_ref, gh1_ref, do_out, grads_ref, sums_ref, wq_full, back_out,
     winv, wbackv, woutv, act_s, gp_s, gi_s, acc, first_s, n1_s, low_s, lowt_s, gsec_s, gh2_s, isum,
-    gb, rb, rx, ry, rx2, ry2, do_ref, do_in, send_sems, recv_sems, local_sems,
+    gb, rb, rx, ry, rx2, ry2, do_ref, do_in, send_sems, recv_sems, line_send, line_recv, local_sems,
 ):
     s, z, core, chip = coordinates()
     other = 1 - core
@@ -711,41 +794,56 @@
     piece = shard // 2
     peer = [None] + [(flip(chip, j) * 2 + core, z) for j in (1, 2, 3)]
     mate = (chip * 2 + other, z)
-    zs = [z] + [flip(z, dz) for dz in (1, 2, 3)]
+    plane = [(s, flip(z, dz)) for dz in (1, 2, 3)]
     ch_of = [chip] + [flip(chip, j) for j in (1, 2, 3)]
     net, loc = Net(send_sems, recv_sems), Local(local_sems)
 
-    def region(zz, m, c):
-        return wq_full.at[zz, m * 2 + lax.div(c, 2), pl.ds(pl.multiple_of(lax.rem(c, 2) * piece, 16), piece), :]
-
+    bpiece = back // 8
+    line = Line(s, z, line_send, line_recv)
+    lines = line.order
+    line.add(K_QKV, lambda: wq_own.at[pl.ds(core * 2, 2)], lambda zz: wq_full.at[zz, pl.ds(core * 2, 2)])
     for dz in (1, 2, 3):
+        net.add((K_QKV, dz), lambda dz=dz: wq_full.at[lines[dz], pl.ds(core * 2, 2)], lambda dz=dz: wq_full.at[lines[dz], pl.ds(core * 2, 2)], mate)
+
+    def region(ref, zz, c):
+        return ref.at[pl.ds(pl.multiple_of(zz * back + (core * 4 + c) * bpiece, 16), bpiece), :]
+
+    def side(zz):
+        return wbackv.at[pl.ds(pl.multiple_of(zz * back + core * 4 * bpiece, 16), 4 * bpiece), :]
+
+    for dz in (2, 3):
         for j in (1, 2):
-            net.add((j, dz), lambda dz=dz: region(zs[dz], core, chip), lambda dz=dz: region(zs[dz], core, chip), peer[j])
-        net.add((3, dz), lambda dz=dz: region(zs[dz], core, ch_of[2]), lambda dz=dz: region(zs[dz], core, ch_of[2]), peer[1])
-        net.add(("m", dz), lambda dz=dz: wq_full.at[zs[dz], pl.ds(core * 2, 2)], lambda dz=dz: wq_full.at[zs[dz], pl.ds(core * 2, 2)], mate)
+            net.add((j, dz), lambda dz=dz: region(wback_ref, lines[dz], chip), lambda dz=dz: region(wbackv, lines[dz], chip), peer[j])
+        via, last = ((1, 2), (2, 1))[dz - 2]
+        net.add((3, dz), lambda dz=dz, via=via: region(wbackv, lines[dz], ch_of[via]), lambda dz=dz, via=via: region(wbackv, lines[dz], ch_of[via]), peer[last])
+        net.add((K_M, dz), lambda dz=dz: side(lines[dz]), lambda dz=dz: side(lines[dz]), mate)
+        loc.add((K_M, dz), lambda dz=dz: region(wback_ref, lines[dz], chip), lambda dz=dz: region(wbackv, lines[dz], chip))
     half = gb.shape[3] // 2
     xs, ys = slice(0, half), slice(half, 2 * half)
     for zz in range(PLANES):
-        net.add(("r1", zz), lambda zz=zz: gb.at[other, zz], lambda zz=zz: rb.at[zz], mate)
+        net.add((K_R1, zz), lambda zz=zz: gb.at[other, zz], lambda zz=zz: rb.at[zz], mate)
         for n, j in enumerate((1, 3)):
-            net.add(("x1", n, zz), lambda zz=zz, j=j: gb.at[core, zz, ch_of[j], xs], lambda zz=zz, n=n: rx.at[zz, n], peer[1])
-        net.add(("x2", zz), lambda zz=zz: gb.at[core, zz, ch_of[2], xs], lambda zz=zz: rx2.at[zz], peer[2])
+            net.add((K_X1, n, zz), lambda zz=zz, j=j: gb.at[core, zz, ch_of[j], xs], lambda zz=zz, n=n: rx.at[zz, n], peer[1])
+        net.add((K_X2, zz), lambda zz=zz: gb.at[core, zz, ch_of[2], xs], lambda zz=zz: rx2.at[zz], peer[2])
         for n, j in enumerate((2, 3)):
-            net.add(("y1", n, zz), lambda zz=zz, j=j: gb.at[core, zz, ch_of[j], ys], lambda zz=zz, n=n: ry.at[zz, n], peer[2])
-        net.add(("y2", zz), lambda zz=zz: gb.at[core, zz, ch_of[1], ys], lambda zz=zz: ry2.at[zz], peer[1])
+            net.add((K_Y1, n, zz), lambda zz=zz, j=j: gb.at[core, zz, ch_of[j], ys], lambda zz=zz, n=n: ry.at[zz, n], peer[2])
+        net.add((K_Y2, zz), lambda zz=zz: gb.at[core, zz, ch_of[1], ys], lambda zz=zz: ry2.at[zz], peer[1])
     for j in (1, 2, 3):
-        net.add(("do", j), lambda j=j: do_ref.at[ch_of[j]], lambda j=j: do_in.at[j], peer[j])
-    loc.add("do_o", lambda: do_in, lambda: do_out)
-    loc.add("back_o", lambda: gb.at[core, :, chip], lambda: back_out)
-    for dz in range(4):
-        for name, own, full, dst in (("out", wout_own, wout_ref, woutv), ("in", win_own, win_ref, winv), ("back", wback_own, wback_ref, wbackv)):
-            n = own.shape[0]
-            place = lambda dz=dz, n=n: pl.ds(pl.multiple_of(zs[dz] * n, 16), n)
-            loc.add((name, dz), lambda own=own, full=full, dz=dz, place=place: own if dz == 0 else full.at[place(), :],
-                    lambda dst=dst, place=place: dst.at[place(), :])
-    for name in ("out", "in", "back"):
-        loc.start(*[(name, dz) for dz in range(4)])
-    hello(peer[1:] + [mate])
+        net.add((K_DO, j), lambda j=j: do_ref.at[ch_of[j]], lambda j=j: do_in.at[j], peer[j])
+    loc.add(K_DO_O, lambda: do_in, lambda: do_out)
+    loc.add(K_BACK_O, lambda: gb.at[core, :, chip], lambda: back_out)
+    shards = {K_OUT: (wout_own, wout_ref, woutv), K_IN: (win_own, win_ref, winv), K_BACK: (wback_own, wback_ref, wbackv)}
+    loads = [(name, i) for name in shards for i in range(4) if name != K_BACK or i < 2]
+    for name, i in loads:
+        own, full, dst = shards[name]
+        n = own.shape[0]
+        place = lambda i=i, n=n: pl.ds(pl.multiple_of(lines[i] * n, 16), n)
+        loc.add((name, i), lambda own=own, full=full, i=i, place=place: full.at[place(), :] if i else own,
+                lambda dst=dst, place=place: dst.at[place(), :])
+    loc.start(*loads, (K_M, 2), (K_M, 3))
+    greet(peer[1:] + [mate] + plane)
+    net.start((1, 2), (2, 2), (1, 3), (2, 3))
+    line.start(K_QKV)
 
     def hop_two(dz):
         net.recv((1, dz), (2, dz))
@@ -753,28 +851,29 @@
 
     def hop_three(dz):
         net.recv((3, dz))
-        net.start(("m", dz))
+        loc.wait((K_M, dz))
+        net.start((K_M, dz))
 
     def add_into(ref, index, other_ref, other_index):
         ref[index] = (ref[index].astype(f32) + other_ref[other_index].astype(f32)).astype(bf16)
 
     def step_one(zz):
-        net.recv(("r1", zz))
+        net.recv((K_R1, zz))
         for c in range(CHIPS):
             add_into(gb, (core, zz, c), rb, (zz, c))
-        net.start(*[("x1", n, zz) for n in (0, 1)], *[("y1", n, zz) for n in (0, 1)])
+        net.start(*[(K_X1, n, zz) for n in (0, 1)], *[(K_Y1, n, zz) for n in (0, 1)])
 
     def step_two(zz):
-        net.recv(("x1", 1, zz), ("y1", 1, zz))
+        net.recv((K_X1, 1, zz), (K_Y1, 1, zz))
         add_into(gb, (core, zz, ch_of[2], xs), rx, (zz, 1))
         add_into(gb, (core, zz, ch_of[1], ys), ry, (zz, 1))
-        net.start(("x2", zz), ("y2", zz))
-        net.recv(("x1", 0, zz), ("y1", 0, zz))
+        net.start((K_X2, zz), (K_Y2, zz))
+        net.recv((K_X1, 0, zz), (K_Y1, 0, zz))
         add_into(gb, (core, zz, chip, xs), rx, (zz, 0))
         add_into(gb, (core, zz, chip, ys), ry, (zz, 0))
 
     def step_three(zz):
-        net.recv(("x2", zz), ("y2", zz))
+        net.recv((K_X2, zz), (K_Y2, zz))
         add_into(gb, (core, zz, chip, xs), rx2, zz)
         add_into(gb, (core, zz, chip, ys), ry2, zz)
 
@@ -784,7 +883,7 @@
 
     vectors = wide_vectors(small_ref)
     vec = lambda i: vectors[i % 4][i // 4 : i // 4 + 1, :]
-    loc.wait(*[("out", dz) for dz in range(4)])
+    loc.wait(*[(K_OUT, dz) for dz in range(4)])
     branch = vec(0)
     for g in range(4):
         branch = branch + dot(att_ref[g, :, 0:step], woutv[g * step : (g + 1) * step, :])
@@ -797,12 +896,7 @@
     first_s[...] = first
     low_s[...] = first.astype(bf16)
     lowt_s[...] = first.astype(bf16).T
-    acc[...] = jnp.zeros_like(acc)
-    met(4)
-    for dz in (1, 2, 3):
-        net.start((1, dz), (2, dz))
-    loc.wait(*[("in", dz) for dz in range(4)])
-    loc.wait(*[("back", dz) for dz in range(4)])
+    loc.wait(*[(name, i) for name, i in loads if name != K_OUT])
 
     def forward(n, carry):
         cols = pl.ds(pl.multiple_of(n * wide, 128), wide)
@@ -811,12 +905,24 @@
         value = value.astype(bf16)
         act_s[n] = value
         gp_s[n] = slope
-        acc[...] += dot(value, wbackv[cols, :])
+        during(n, {2: lambda: hop_two(2), 3: lambda: hop_two(3)})
         return carry
 
     lax.fori_loop(0, PLANES, forward, 0)
-    for dz in (1, 2, 3):
-        hop_two(dz)
+
+    def second_layer(i):
+        zz = lines[i]
+        return dot(act_s[zz], wbackv[pl.ds(pl.multiple_of(zz * back, 16), back), :])
+
+    acc[...] = second_layer(0)
+    acc[...] += second_layer(1)
+    hop_three(2)
+    hop_three(3)
+    line.step(1, K_QKV)
+    net.recv((K_M, 2))
+    acc[...] += second_layer(2)
+    net.recv((K_M, 3))
+    acc[...] += second_layer(3)
     position = s * rows + lax.broadcasted_iota(jnp.int32, (rows, 1), 0)
     valid = (position < length_ref[0]).astype(f32)
     hidden = first_s[...] + acc[...] + vec(3)
@@ -845,8 +951,8 @@
                         (m * 4 + k) * part : (m * 4 + k + 1) * part, x * ch : (x + 1) * ch
                     ]
         during(n, {
-            0: lambda: net.start(("r1", 0)), 1: lambda: (net.start(("r1", 1)), hop_three(1)),
-            2: lambda: (net.start(("r1", 2)), hop_three(2)), 3: lambda: (net.start(("r1", 3)), hop_three(3)),
+            0: lambda: net.start((K_R1, 0)), 1: lambda: net.start((K_R1, 1)),
+            2: lambda: net.start((K_R1, 2)), 3: lambda: net.start((K_R1, 3)),
         })
         return carry
 
@@ -877,7 +983,9 @@
         w = woutv[g * step : (g + 1) * step, :]
         do_ref[g, :, 0:step] = dot(gbranch, w, NT).astype(bf16)
         do_ref[g, :, step:] = jnp.zeros((rows, do_ref.shape[2] - step), bf16)
-    net.start(*[("do", j) for j in (1, 2, 3)])
+    net.start(*[(K_DO, j) for j in (1, 2, 3)])
+    line.step(2, K_QKV)
+    net.start((K_QKV, 1), (K_QKV, 2))
     do_in[0] = do_ref[chip]
     for g in range(4):
         gw = dot(att_ref[g, :, 0:step].T, gbranch).astype(bf16)
@@ -909,12 +1017,15 @@
         part = jnp.where(place == 6, isum[zz], part)
         sums_ref[zz, 0:16, :] = jnp.concatenate([part, jnp.zeros((8, width), f32)], axis=0).astype(bf16)
     step_three(3)
-    net.recv(*[("do", j) for j in (1, 2, 3)])
-    loc.start("back_o", "do_o")
-    net.recv(*[("m", dz) for dz in (1, 2, 3)])
+    net.recv(*[(K_DO, j) for j in (1, 2, 3)])
+    loc.start(K_BACK_O, K_DO_O)
+    line.step(3, K_QKV)
+    net.start((K_QKV, 3))
+    net.recv(*[(K_QKV, dz) for dz in (1, 2, 3)])
     for name in net.specs:
         net.sent(name)
-    loc.wait("back_o", "do_o")
+    line.sent()
+    loc.wait(K_BACK_O, K_DO_O)
 
 
 Q_PLACE, K_PLACE, V_PLACE = (4, 5, 6), (0, 2, 8), (1, 3, 9)
@@ -995,8 +1106,9 @@
 SEMS = 96
 
 
-def semaphores():
-    return [pltpu.SemaphoreType.DMA((SEMS,)), pltpu.SemaphoreType.DMA((SEMS,)), pltpu.SemaphoreType.DMA((16,))]
+def semaphores(line=False):
+    counts = (SEMS, SEMS) + ((5 * 3, PLANES * 3) if line else ()) + (16,)
+    return [pltpu.SemaphoreType.DMA((n,)) for n in counts]
 
 
 def params(collective_id):
@@ -1017,15 +1129,15 @@
             S(q_shape, bf16), S(kv_shape, bf16), S(kv_shape, bf16), S(q_shape, bf16),
             S((4, rows, width), bf16), S((4, rows, 256), bf16), S((PLANES, 16, width), bf16),
             S((PLANES * shard, hidden), bf16), S((width, width), bf16),
-            S((CHIPS, shard, PACK), bf16), S((hidden, width), bf16), S((PLANES, CHIPS, shard, PACK), bf16),
+            S((CHIPS, shard, PACK), bf16), S((hidden, width), bf16),
         ),
         in_specs=[SMEM] + [ANY] * 6,
-        out_specs=[ANY] * 12,
+        out_specs=[ANY] * 11,
         scratch_shapes=[
             vmem((4, rows, width)), vmem((width, PACK)), vmem(q_shape), vmem(kv_shape), vmem(kv_shape), vmem(q_shape),
             vmem((4, rows, 256)), vmem((4, rows, 256)), vmem((4, rows, 384)), vmem((4, rows, 384)),
             vmem((PLANES, 16, width)), vmem((shard, w_qkv.shape[1])), vmem((CHIPS, shard, PACK)),
-        ] + semaphores(),
+        ] + semaphores(line=True),
         compiler_params=params(1),
     )(lengths, tokens, w_qkv, w_in, w_back, w_out, small)
 
@@ -1060,7 +1172,7 @@
     )(do, q, k, v, o, tok, grads, sums, back)
 
 
-def run_ffn(lengths, att, tokens, cotangent, full_in, w_in, full_out, w_out, small, full_back, w_back, wq_full):
+def run_ffn(lengths, att, tokens, cotangent, full_in, w_in, full_out, w_out, small, full_back, w_back, wq):
     rows, width = tokens.shape
     hidden = w_in.shape[1]
     ch = hidden // 8
@@ -1071,10 +1183,9 @@
         ffn_kernel,
         out_shape=(
             one, S((rows, width), f32), S((4, rows, 256), bf16), S((2, 4, 4, width // 4 + 48, ch), bf16), S((4, 16, width), bf16),
-            S(wq_full.shape, bf16), S((4, 2 * bp, ch), bf16),
+            S((PLANES,) + wq.shape, bf16), S((4, 2 * bp, ch), bf16),
         ),
         in_specs=[SMEM] + [VMEM] * 3 + [ANY] * 4 + [VMEM] + [ANY] * 3,
-        input_output_aliases={11: 5},
         out_specs=[VMEM] * 2 + [ANY] + [VMEM] * 2 + [ANY] * 2,
         scratch_shapes=[
             vmem((width, hidden)), vmem((hidden, width)), vmem((width, width)),
@@ -1083,10 +1194,11 @@
             vmem((rows, width)), vmem((width, rows)), vmem((rows, width)), vmem((rows, width), f32), vmem((4, 8, 2 * ch), f32),
             vmem((2, 4, 4, 2 * bp, ch)), vmem((4, 4, 2 * bp, ch)), vmem((4, 2, bp, ch)), vmem((4, 2, bp, ch)), vmem((4, bp, ch)), vmem((4, bp, ch)),
             vmem((4, rows, 256)), vmem((4, rows, 256)),
-            pltpu.SemaphoreType.DMA((SEMS,)), pltpu.SemaphoreType.DMA((SEMS,)), pltpu.SemaphoreType.DMA((24,)),
+            pltpu.SemaphoreType.DMA((SEMS,)), pltpu.SemaphoreType.DMA((SEMS,)),
+            pltpu.SemaphoreType.DMA((5,)), pltpu.SemaphoreType.DMA((PLANES,)), pltpu.SemaphoreType.DMA((24,)),
         ],
         compiler_params=params(3),
-    )(lengths, att, tokens, cotangent, full_in, w_in, full_out, w_out, small, full_back, w_back, wq_full)
+    )(lengths, att, tokens, cotangent, full_in, w_in, full_out, w_out, small, full_back, w_back, wq)
 
 
 def run_final(dproj, wq_full, wq, gh1, gw, hw, fin, finb, sums):
@@ -1118,11 +1230,11 @@
         jnp.concatenate([out_bias, ln1_gain, ln1_bias, back_bias]), line(ln2_gain, ln2_bias), in_bias,
         line(gap, v_bias[0:64], gap, v_bias[64:128], q_bias, gap, gap, v_bias[128:192]),
     ] + [jnp.zeros((width,), bf16)] * 12)
-    q, k, v, o, tok_all, att, small_all, full_in, full_out, wq, full_back, wq_full = run_forward(
+    q, k, v, o, tok_all, att, small_all, full_in, full_out, wq, full_back = run_forward(
         lengths, tokens[0], w_qkv, w_in, w_back, w_out, small
     )
     output, gh1, do, grads, sums, wq_full, back = run_ffn(
-        lengths, att, tokens[0], cotangent[0], full_in, w_in, full_out, w_out, small_all, full_back, w_back, wq_full
+        lengths, att, tokens[0], cotangent[0], full_in, w_in, full_out, w_out, small_all, full_back, w_back, wq
     )
     dproj, gw, hw, fin, finb, sums_f = run_backward(do, q, k, v, o, tok_all, grads, sums, back)
     gt, gqkv, gin, gback, gout, qb, vb, ob, g1, b1, bb, g2, b2, ib = run_final(dproj, wq_full, wq, gh1, gw, hw, fin, finb, sums_f)
@@ -1242,20 +1354,11 @@
     ln2_bias,
     cotangent,
 ):
-    gathered = (
-        lax.all_gather(w_qkv, "fsdp", axis=0, tiled=True),
-        lax.all_gather(q_bias, "fsdp", axis=0, tiled=True),
-        lax.all_gather(v_bias, "fsdp", axis=0, tiled=True),
-        lax.all_gather(w_out, "fsdp", axis=0, tiled=True),
-        lax.all_gather(out_bias, "fsdp", axis=0, tiled=True),
-        lax.all_gather(ln1_gain, "fsdp", axis=0, tiled=True),
-        lax.all_gather(ln1_bias, "fsdp", axis=0, tiled=True),
-        lax.all_gather(w_in, "fsdp", axis=0, tiled=True),
-        lax.all_gather(in_bias, "fsdp", axis=0, tiled=True),
-        lax.all_gather(w_back, "fsdp", axis=0, tiled=True),
-        lax.all_gather(back_bias, "fsdp", axis=0, tiled=True),
-        lax.all_gather(ln2_gain, "fsdp", axis=0, tiled=True),
-        lax.all_gather(ln2_bias, "fsdp", axis=0, tiled=True),
+    gathered = tuple(
+        lax.all_gather(a, "fsdp", axis=0, tiled=True)
+        for a in (
+            w_qkv, q_bias, v_bias, w_out, out_bias, ln1_gain, ln1_bias, w_in, in_bias, w_back, back_bias, ln2_gain, ln2_bias
+        )
     )
     (
         full_qkv,
@@ -1394,104 +1497,23 @@
         g_ln2_gain,
         g_ln2_bias,
     )
-    owned = (
-        lax.psum_scatter(
-            local_grads[0].astype(jnp.bfloat16), "fsdp", scatter_dimension=0, tiled=True
-        ).astype(jnp.float32),
-        lax.psum_scatter(
-            local_grads[1].astype(jnp.bfloat16), "fsdp", scatter_dimension=0, tiled=True
-        ).astype(jnp.float32),
-        lax.psum_scatter(
-            local_grads[2].astype(jnp.bfloat16), "fsdp", scatter_dimension=0, tiled=True
-        ).astype(jnp.float32),
-        lax.psum_scatter(
-            local_grads[3].astype(jnp.bfloat16), "fsdp", scatter_dimension=0, tiled=True
-        ).astype(jnp.float32),
-        lax.psum_scatter(
-            local_grads[4].astype(jnp.bfloat16), "fsdp", scatter_dimension=0, tiled=True
-        ).astype(jnp.float32),
-        lax.psum_scatter(
-            local_grads[5].astype(jnp.bfloat16), "fsdp", scatter_dimension=0, tiled=True
-        ).astype(jnp.float32),
-        lax.psum_scatter(
-            local_grads[6].astype(jnp.bfloat16), "fsdp", scatter_dimension=0, tiled=True
-        ).astype(jnp.float32),
-        lax.psum_scatter(
-            local_grads[7].astype(jnp.bfloat16), "fsdp", scatter_dimension=0, tiled=True
-        ).astype(jnp.float32),
-        lax.psum_scatter(
-            local_grads[8].astype(jnp.bfloat16), "fsdp", scatter_dimension=0, tiled=True
-        ).astype(jnp.float32),
-        lax.psum_scatter(
-            local_grads[9].astype(jnp.bfloat16), "fsdp", scatter_dimension=0, tiled=True
-        ).astype(jnp.float32),
-        lax.psum_scatter(
-            local_grads[10].astype(jnp.bfloat16), "fsdp", scatter_dimension=0, tiled=True
-        ).astype(jnp.float32),
-        lax.psum_scatter(
-            local_grads[11].astype(jnp.bfloat16), "fsdp", scatter_dimension=0, tiled=True
-        ).astype(jnp.float32),
-        lax.psum_scatter(
-            local_grads[12].astype(jnp.bfloat16), "fsdp", scatter_dimension=0, tiled=True
-        ).astype(jnp.float32),
-    )
-    totals = (
-        lax.psum(owned[0].astype(jnp.bfloat16), "seq").astype(jnp.float32),
-        lax.psum(owned[1].astype(jnp.bfloat16), "seq").astype(jnp.float32),
-        lax.psum(owned[2].astype(jnp.bfloat16), "seq").astype(jnp.float32),
-        lax.psum(owned[3].astype(jnp.bfloat16), "seq").astype(jnp.float32),
-        lax.psum(owned[4].astype(jnp.bfloat16), "seq").astype(jnp.float32),
-        lax.psum(owned[5].astype(jnp.bfloat16), "seq").astype(jnp.float32),
-        lax.psum(owned[6].astype(jnp.bfloat16), "seq").astype(jnp.float32),
-        lax.psum(owned[7].astype(jnp.bfloat16), "seq").astype(jnp.float32),
-        lax.psum(owned[8].astype(jnp.bfloat16), "seq").astype(jnp.float32),
-        lax.psum(owned[9].astype(jnp.bfloat16), "seq").astype(jnp.float32),
-        lax.psum(owned[10].astype(jnp.bfloat16), "seq").astype(jnp.float32),
-        lax.psum(owned[11].astype(jnp.bfloat16), "seq").astype(jnp.float32),
-        lax.psum(owned[12].astype(jnp.bfloat16), "seq").astype(jnp.float32),
-    )
+    owned = [
+        lax.psum_scatter(a.astype(jnp.bfloat16), "fsdp", scatter_dimension=0, tiled=True).astype(jnp.float32)
+        for a in local_grads
+    ]
+    totals = [lax.psum(a.astype(jnp.bfloat16), "seq").astype(jnp.float32) for a in owned]
     return (output[None], grad_input.astype(jnp.bfloat16)[None]) + tuple(totals)
 
 
 def solution(mesh):
+    spread, vector, matrix = P("fsdp", "seq", None), P("fsdp"), P("fsdp", None)
     fits = mesh.shape["seq"] == 2 * CHIPS and mesh.shape["fsdp"] == PLANES
     return jax.shard_map(
         planned if fits else on_device,
         mesh=mesh,
-        in_specs=(
-            P("fsdp", "seq", None),
-            P("fsdp"),
-            P("fsdp", None),
-            P("fsdp"),
-            P("fsdp"),
-            P("fsdp", None),
-            P("fsdp"),
-            P("fsdp"),
-            P("fsdp"),
-            P("fsdp", None),
-            P("fsdp"),
-            P("fsdp", None),
-            P("fsdp"),
-            P("fsdp"),
-            P("fsdp"),
-            P("fsdp", "seq", None),
-        ),
-        out_specs=(
-            P("fsdp", "seq", None),
-            P("fsdp", "seq", None),
-            P("fsdp", None),
-            P("fsdp"),
-            P("fsdp"),
-            P("fsdp", None),
-            P("fsdp"),
-            P("fsdp"),
-            P("fsdp"),
-            P("fsdp", None),
-            P("fsdp"),
-            P("fsdp", None),
-            P("fsdp"),
-            P("fsdp"),
-            P("fsdp"),
-        ),
+        in_specs=(spread, vector, matrix, vector, vector, matrix) + (vector,) * 3
+        + (matrix, vector, matrix) + (vector,) * 3 + (spread,),
+        out_specs=(spread, spread, matrix, vector, vector, matrix) + (vector,) * 3
+        + (matrix, vector, matrix) + (vector,) * 3,
         check_vma=False,
     )

time: 241 us -> 235 us (0.975); the launches traced: 238 us -> 235 us
  Pallas kernels: 230 us -> 227 us
    pallas_call x1, Pallas kernels: 76.7 us -> 69.7 us  [run_forward(): pl.pallas_call(forward_kernel, out_shape=(S(q_shape, bf16), S(kv_shape, b...]
    pallas_call x1, Pallas kernels: 59.6 us -> 63.2 us  [run_ffn(): pl.pallas_call(ffn_kernel, out_shape=(one, S((rows, width), f32), S((4, r...]
where the time goes in v3:
time: 235 us
  Pallas kernels  227 us (97%)
  local copies, waits for them, and re-layouts  4.38 us (2%)
  other arithmetic  2.82 us (1%)
    pallas_call x1, Pallas kernels, run_backward(): pl.pallas_call(backward_kernel, out_shape=(S((4, rows, PACK), bf16), S((2...  84.8 us
    pallas_call x1, Pallas kernels, run_forward(): pl.pallas_call(forward_kernel, out_shape=(S(q_shape, bf16), S(kv_shape, b...  69.7 us
    pallas_call x1, Pallas kernels, run_ffn(): pl.pallas_call(ffn_kernel, out_shape=(one, S((rows, width), f32), S((4, r...  63.2 us
    pallas_call x1, Pallas kernels, run_final(): pl.pallas_call(final_kernel, out_shape=(S((rows, width), bf16), S((shard,...  8.98 us

profile of v3, /device:TPU:1, one launch (start us, length us, event | category | flops | bytes accessed | tf_op | source)
XLA Modules:
  0.0 235.2 jit_solution(4948995536600260146)
XLA Ops:
  1.3 0.8 pad_maximum_fusion.1
  2.1 0.8 fusion
  2.9 0.8 concatenate.11
  3.7 0.8 pad_maximum_fusion
  4.5 0.7 stack.23
  5.2 1.2 stack.27.small_ref
  6.4 69.7 %shard_map.271 = (bf16[3,1536,128]{2,1,0:T(8,128)(2,1)}, bf16[3,3072,128]{2,1,0:T(8,128)(2,1)}, bf16[3,3072,128]{2,1,0:T(8,128)(2,1)}, bf16[3,1536,128]{2,1,0:T(...) custom-call(s32[1]{0:T(128)S(6)} %copy.32.length_ref, ...), custom_call_target="tpu_custom_call" | custom-call | tf_op jit(solution)/shard_map/pallas_call | solution.py:1126
  76.1 63.2 %shard_map.272 = (bf16[384,768]{1,0:T(8,128)(2,1)}, f32[384,768]{1,0:T(8,128)}, bf16[4,384,256]{2,1,0:T(8,128)(2,1)}, bf16[2,4,4,240,384]{4,3,2,1,0:T(8,128)(2,1...) custom-call(s32[1]{0:T(128)S(6)} %copy.32.length_ref, ...), custom_call_target="tpu_custom_call" | custom-call | tf_op jit(solution)/shard_map/pallas_call | solution.py:1182
  139.3 84.8 %shard_map.273 = (bf16[4,384,640]{2,1,0:T(8,128)(2,1)}, bf16[2,4,112,384]{3,2,1,0:T(8,128)(2,1)}, bf16[2,4,112,256]{3,2,1,0:T(8,128)(2,1)}, bf16[2,4,240,384]{3,...) custom-call(bf16[4,384,256]{2,1,0:T(8,128)(2,1)} %get-tuple-element.60.do_ref, ...), custom_call_target="tpu_custom_call" | custom-call | tf_op jit(solution)/shard_map/pallas_call | solution.py:1153
  224.1 0.0 copy-start
  224.1 9.0 %shard_map.274 = (bf16[384,768]{1,0:T(8,128)(2,1)}, f32[192,2304]{1,0:T(8,128)}, f32[192,3072]{1,0:T(8,128)}, f32[768,768]{1,0:T(8,128)}, f32[192,768]{1,0:T(8,1...) custom-call(bf16[4,384,640]{2,1,0:T(8,128)(2,1)} %get-tuple-element., ...), custom_call_target="tpu_custom_call" | custom-call | tf_op jit(solution)/shard_map/pallas_call | solution.py:1209
  233.1 1.3 reduce
  234.4 0.0 copy-done
  234.4 0.8 copy.33
  (8 shorter events, 0.0 us)
Async XLA Ops:
  224.1 10.3 %copy-start = (bf16[384,768]{1,0:T(8,128)(2,1)S(1)}, bf16[384,768]{1,0:T(8,128)(2,1)}, u32[]{:S(2)}) copy-start(bf16[384,768]{1,0:T(8,128)(2,1)} %get-tuple-element.59) | copy-start | bytes 1769476

commit v4 on v3

--- a/solution.py
+++ b/solution.py
@@ -198,9 +198,10 @@
 
 
 def forward_kernel(
-    length_ref, tok_ref, wraw_ref, win_ref, wback_ref, wout_ref, small_ref,
+    length_ref, tok_ref, wraw_ref, win_ref, wback_ref, wout_ref,
+    ob_ref, g1_ref, n1_ref, bb_ref, g2_ref, n2_ref, ib_ref, qb_ref, vb_ref,
     q_out, k_out, v_out, o_out, tok_out, att_out, small_out, win_full, wout_full, wq_out, wback_full,
-    tok, wqv, q_s, k_s, v_s, o_s, att, atts, kvs, kvr, small, wraw, wq_ref, send_sems, recv_sems, line_send, line_recv, local_sems,
+    tok, wqv, q_s, k_s, v_s, o_s, att, atts, kvs, kvr, small, wraw, wq_ref, vec_s, vec_v, send_sems, recv_sems, line_send, line_recv, local_sems,
 ):
     s, z, core, chip = coordinates()
     other = 1 - core
@@ -242,8 +243,7 @@
 
     line = Line(s, z, line_send, line_recv)
     lines = line.order
-    for a in (K_IN, K_BACK):
-        line.add(a, lambda a=a: own_part(a, core, chip), lambda zz, a=a: part(a, zz, core, chip))
+    line.add(K_BACK, lambda: own_part(K_BACK, core, chip), lambda zz: part(K_BACK, zz, core, chip))
     line.add(K_OUT, lambda: wout_ref.at[:, at(core * width, width, 128)], lambda zz: side(K_OUT, zz, core))
 
     for dz in (1, 2, 3):
@@ -251,7 +251,7 @@
                 lambda: wqv.at[pl.ds(pl.multiple_of(z * shard + core * piece, 16), piece), :], plane[dz])
         net.add((K_WQM, dz), lambda dz=dz: wqv.at[pl.ds(pl.multiple_of(zs[dz] * shard + core * piece, 16), piece), :],
                 lambda dz=dz: wqv.at[pl.ds(pl.multiple_of(zs[dz] * shard + core * piece, 16), piece), :], mate)
-        net.add((K_SMALL, dz), lambda: small_ref, lambda: small.at[z], plane[dz])
+        net.add((K_SMALL, dz), lambda: small.at[z], lambda: small.at[z], plane[dz])
     top, bottom = slice(0, half), slice(half, rows)
     net.add(K_T1A, lambda: tok_ref.at[top], lambda: tok.at[1, top], peer[1])
     net.add(K_T1B, lambda: tok_ref.at[bottom], lambda: tok.at[1, bottom], peer[1])
@@ -264,28 +264,49 @@
     for j in (1, 2, 3):
         net.add((K_ATT0, j), lambda j=j: atts.at[j, :, 0:128], lambda: att.at[chip, :, 0:128], peer[j])
         net.add((K_ATT1, j), lambda j=j: atts.at[j, :, 128:256], lambda: att.at[chip, :, 128:256], peer[j])
+    where = {K_IN: zs, K_BACK: lines, K_OUT: lines}
     for a, dz in hops:
-        via, last = (1, 2) if a == K_IN else (2, 1)
+        place = lambda c, a=a, dz=dz: part(a, where[a][dz], core, c)
+
+        def half_place(c, n, a=a, dz=dz):
+            zz = where[a][dz]
+            if a == K_IN:
+                return win_full.at[at(zz * shard + n * piece, piece), at((core * 4 + c) * width, width, 128)]
+            return wback_full.at[at(zz * back + (core * 4 + c) * bpiece + n * (bpiece // 2), bpiece // 2), :]
+
         for j in (1, 2):
-            net.add((a, j, dz), lambda a=a, dz=dz: part(a, lines[dz], core, chip), lambda a=a, dz=dz: part(a, lines[dz], core, chip), peer[j])
-        net.add((a, 3, dz), lambda a=a, dz=dz, via=via: part(a, lines[dz], core, flip(chip, via)),
-                lambda a=a, dz=dz, via=via: part(a, lines[dz], core, flip(chip, via)), peer[last])
+            net.add((a, j, dz), lambda place=place: place(chip), lambda place=place: place(chip), peer[j])
+        for n, via, last in ((0, 1, 2), (1, 2, 1)):
+            there = lambda half_place=half_place, n=n, via=via: half_place(flip(chip, via), n)
+            net.add((a, 3 + n, dz), there, there, peer[last])
+    for dz in (1, 2, 3):
+        net.add((K_IN, K_Z, dz), lambda: own_part(K_IN, core, chip), lambda: part(K_IN, z, core, chip), plane[dz])
     mates = hops + [(K_OUT, dz) for dz in (1, 2, 3)]
     for a, dz in mates:
-        net.add((a, K_M, dz), lambda a=a, dz=dz: side(a, lines[dz], core), lambda a=a, dz=dz: side(a, lines[dz], core), mate)
+        net.add((a, K_M, dz), lambda a=a, dz=dz: side(a, where[a][dz], core), lambda a=a, dz=dz: side(a, where[a][dz], core), mate)
     loc.add(K_RAW, lambda: wraw_ref, lambda: wraw)
     loc.add(K_TOK, lambda: tok_ref, lambda: tok.at[0])
     loc.add(K_WQ, lambda: wq_ref.at[chip], lambda: wqv.at[pl.ds(pl.multiple_of(z * shard, 16), shard), :])
-    loc.add(K_SMALL, lambda: small_ref, lambda: small.at[z])
     outs = ((K_WQ_O, wq_ref, wq_out), (K_K_O, k_s, k_out), (K_V_O, v_s, v_out), (K_Q_O, q_s, q_out), (K_O_O, o_s, o_out),
             (K_TOK_O, tok, tok_out), (K_ATT_O, att, att_out), (K_SMALL_O, small, small_out))
     for name, src, dst in outs:
         loc.add(name, lambda src=src: src, lambda dst=dst: dst)
 
-    loc.start(K_RAW, K_TOK, K_SMALL)
+    loc.start(K_RAW, K_TOK)
     greet(peer[1:] + [mate] + plane[1:])
     net.start(K_T1A, K_T2B, K_T1B, K_T2A)
     lane = lanes_of()
+    vec_s[...] = jnp.zeros_like(vec_s)
+    vec_v[...] = jnp.zeros_like(vec_v)
+    for i, ref in enumerate((ob_ref, g1_ref, n1_ref, bb_ref, g2_ref, n2_ref)):
+        vec_s[i : i + 1, 0:shard] = ref[...].astype(f32).reshape(1, shard)
+    vec_s[6:7, :] = ib_ref[...].astype(f32).reshape(1, ib_ref.shape[0])
+    vec_s[7:8, 256 : 256 + shard] = qb_ref[...].astype(f32).reshape(1, shard)
+    vec_v[0:1, 0:shard] = vb_ref[...].astype(f32).reshape(1, shard)
+    first, last = vec_v[:, 0:128], vec_v[:, 128:256]
+    for t, tile in ((0, pltpu.roll(first, 64, 1)), (1, first), (4, pltpu.roll(last, 64, 1))):
+        vec_s[7:8, t * 128 : (t + 1) * 128] = jnp.where(lane < 64, 0.0, tile[0:1])
+    small[z] = jnp.concatenate([vec_s[...], jnp.zeros_like(vec_s)], axis=0).astype(bf16)
     loc.wait(K_RAW)
     for g in range(CHIPS):
         for t in range(PACK // 128):
@@ -304,13 +325,13 @@
     for dz in (1, 2, 3):
         net.recv((K_WQ, dz))
         net.start((K_WQM, dz))
-    line.start(K_OUT, K_IN)
-    loc.wait(K_TOK, K_WQ, K_SMALL)
+    net.start(*[(K_IN, K_Z, dz) for dz in (1, 2, 3)])
+    loc.wait(K_TOK, K_WQ)
     for dz in (1, 2, 3):
         net.recv((K_SMALL, dz), (K_WQM, dz))
 
     length = length_ref[0]
-    bias = small[chip, 3:4, 0:PACK].astype(f32)
+    bias = small[chip, 7:8, 0:PACK].astype(f32)
 
     def keep(tile, h, slot, block):
         position = block * rows + lax.broadcasted_iota(jnp.int32, (rows, 1), 0)
@@ -348,11 +369,13 @@
         net.start((a, 1, dz), (a, 2, dz))
 
     def second_hop(a, dz):
-        net.recv((a, 1, dz), (a, 2, dz))
+        net.recv((a, 1, dz))
         net.start((a, 3, dz))
+        net.recv((a, 2, dz))
+        net.start((a, 4, dz))
 
     def third_hop(a, dz):
-        net.recv((a, 3, dz))
+        net.recv((a, 3, dz), (a, 4, dz))
         net.start((a, K_M, dz))
 
     project(0)
@@ -367,9 +390,9 @@
     keep_other(0)
     keep_other(1)
     keep_other(2)
-    line.step(1, K_OUT, K_IN)
-    line.start(K_BACK)
+    net.recv((K_IN, K_Z, 1))
     first_hop(K_IN, 1)
+    line.start(K_BACK, K_OUT)
     net.recv(K_T3A, K_T3B)
     project(3)
     keep_other(3)
@@ -394,18 +417,22 @@
                 atts[j, :, place] = value.astype(bf16)
                 net.start(((K_ATT0, K_ATT1)[which], j))
 
+    def in_hop(dz):
+        net.recv((K_IN, K_Z, dz))
+        first_hop(K_IN, dz)
+
     stages = {
-        0: lambda: (line.step(2, K_OUT, K_IN), first_hop(K_IN, 2), line.step(1, K_BACK)),
-        2: lambda: second_hop(K_IN, 1),
-        3: lambda: (line.step(3, K_OUT, K_IN), first_hop(K_IN, 3), [net.start((K_OUT, K_M, dz)) for dz in (1, 2, 3)]),
-        4: lambda: (line.step(2, K_BACK), second_hop(K_IN, 2), first_hop(K_BACK, 1)),
-        5: lambda: third_hop(K_IN, 1),
-        6: lambda: third_hop(K_IN, 2),
-        7: lambda: attended_tile(0),
-        8: lambda: (second_hop(K_IN, 3), line.step(3, K_BACK)),
-        9: lambda: second_hop(K_BACK, 1),
-        10: lambda: third_hop(K_IN, 3),
-        11: lambda: (attended_tile(1), third_hop(K_BACK, 1)),
+        0: lambda: (in_hop(2), in_hop(3)),
+        1: lambda: line.step(1, K_BACK, K_OUT),
+        2: lambda: (second_hop(K_IN, 1), first_hop(K_BACK, 1)),
+        4: lambda: (second_hop(K_IN, 2), third_hop(K_IN, 1)),
+        5: lambda: line.step(2, K_BACK, K_OUT),
+        6: lambda: (second_hop(K_IN, 3), third_hop(K_IN, 2)),
+        7: lambda: (attended_tile(0), second_hop(K_BACK, 1)),
+        8: lambda: third_hop(K_IN, 3),
+        9: lambda: (line.step(3, K_BACK, K_OUT), [net.start((K_OUT, K_M, dz)) for dz in (1, 2, 3)]),
+        10: lambda: third_hop(K_BACK, 1),
+        11: lambda: attended_tile(1),
     }
 
     def progress(n):
@@ -453,7 +480,7 @@
     do_ref, q_ref, k_ref, v_ref, o_ref, tok_ref, grads_ref, sums_ref, back_ref,
     dproj_out, gw_out, hw_out, fin_out, finb_out, sums_out,
     do_s, q_s, k_s, v_s, o_s, doa, tok, tokt, dqs, dq_keep, kv_own, kvs, kvr, dall, dproj,
-    gw, gwr, gz, gzr, gwf, hw, hwr, hz, hzr, hwf, acc, rb, rx, ry, rx2, ry2, rz, rzb, fin, finb, sums, sums_r, sums_z, sums_f,
+    gw, gwr, gz, gzr, gwf, hw, hwr, hz, hzr, hwf, acc, rb, rx, ry, rx2, ry2, rz, rzb, backv, bx2, by2, fin, finb, sums, sums_r, sums_z, sums_f,
     send_sems, recv_sems, local_sems,
 ):
     s, z, core, chip = coordinates()
@@ -489,9 +516,11 @@
         if dz:
             net.add((K_RZ, dz), lambda dz=dz: acc.at[zs[dz], chip], lambda dz=dz: rz.at[dz - 1], plane[dz])
     for dz in (1, 2, 3):
-        net.add((K_RZB, dz), lambda dz=dz: back_ref.at[zs[dz]], lambda dz=dz: rzb.at[dz], plane[dz])
+        net.add((K_RZB, dz), lambda dz=dz: backv.at[zs[dz]], lambda dz=dz: rzb.at[dz - 1], plane[dz])
     bh = finb.shape[2] // 2
     bx, by = slice(0, bh), slice(bh, 2 * bh)
+    net.add((K_X2, K_BACK), lambda: back_ref.at[2, :, bx], lambda: bx2, peer[2])
+    net.add((K_Y2, K_BACK), lambda: back_ref.at[1, :, by], lambda: by2, peer[1])
     net.add(K_B1, lambda: finb.at[core, chip], lambda: finb.at[core, chip], peer[1])
     net.add(K_B2, lambda: finb.at[core, chip], lambda: finb.at[core, chip], peer[2])
     net.add(K_B3X, lambda: finb.at[core, ch[1], bx], lambda: finb.at[core, ch[1], bx], peer[2])
@@ -518,7 +547,7 @@
     loads = ((K_DO, lambda: do_ref, lambda: do_s), (K_O, lambda: o_ref, lambda: o_s),
              (K_TOK, lambda: tok_ref, lambda: tok), (K_Q, lambda: q_ref, lambda: q_s),
              (K_K, lambda: k_ref, lambda: k_s), (K_V, lambda: v_ref, lambda: v_s),
-             (K_SUMS, lambda: sums_ref, lambda: sums.at[0]), (K_BACK, lambda: back_ref.at[z], lambda: rzb.at[0]), (K_ACC, lambda: grads_ref.at[core], lambda: acc))
+             (K_SUMS, lambda: sums_ref, lambda: sums.at[0]), (K_BACK, lambda: back_ref.at[0], lambda: backv), (K_ACC, lambda: grads_ref.at[core], lambda: acc))
     for name, src, dst in loads:
         loc.add(name, src, dst)
     stores = ((K_DP_O, dproj, dproj_out), (K_GW_O, gwf, gw_out), (K_HW_O, hwf, hw_out), (K_FIN_O, fin, fin_out), (K_FINB_O, finb, finb_out))
@@ -529,7 +558,7 @@
     loc.start(*[name for name, _, _ in loads])
     greet(peer[1:] + [mate] + plane[1:])
     net.start(K_S0, *[(K_R1, dz) for dz in order])
-    net.start(*[(K_RZB, dz) for dz in (1, 2, 3)])
+    net.start((K_X2, K_BACK), (K_Y2, K_BACK))
     lane = lanes_of()
     loc.wait(K_TOK)
     for j in range(4):
@@ -582,9 +611,16 @@
         else:
             net.start(*[(K_SZ, dz) for dz in (1, 2, 3)])
 
+    def back_plane():
+        net.recv((K_X2, K_BACK), (K_Y2, K_BACK))
+        for zz in range(PLANES):
+            add_into(backv, (zz, bx), bx2, zz)
+            add_into(backv, (zz, by), by2, zz)
+        net.start(*[(K_RZB, dz) for dz in (1, 2, 3)])
+
     def back_total():
         net.recv(*[(K_RZB, dz) for dz in (1, 2, 3)])
-        total = rzb[0].astype(f32) + rzb[1].astype(f32) + rzb[2].astype(f32) + rzb[3].astype(f32)
+        total = backv[z].astype(f32) + rzb[0].astype(f32) + rzb[1].astype(f32) + rzb[2].astype(f32)
         finb[core, chip] = total.astype(bf16)
         net.start(K_B1, K_B2)
 
@@ -670,7 +706,7 @@
             net.start((K_DP, h, j))
 
     stages = {
-        0: lambda: (step_one(3), sums_step(0)),
+        0: lambda: (step_one(3), back_plane(), sums_step(0)),
         1: lambda: (step_one(2), sums_step(1)),
         2: lambda: (step_two(3), step_one(1), sums_step(2)),
         3: lambda: (step_three(3), step_two(2)),
@@ -767,13 +803,10 @@
 def wide_vectors(small):
     step = small.shape[2] // PLANES
     lane = lax.broadcasted_iota(jnp.int32, (8, small.shape[2]), 1)
-    total = [0.0] * PLANES
+    total = 0.0
     for zz in range(PLANES):
-        value = small[zz].astype(f32)[0:8]
-        for k in range(PLANES):
-            part = jnp.where((lane >= k * step) & (lane < (k + 1) * step), value, 0.0)
-            turn = (zz - k) % PLANES * step
-            total[k] = total[k] + (pltpu.roll(part, turn, 1) if turn else part)
+        part = jnp.where(lane < step, small[zz].astype(f32)[0:8], 0.0)
+        total = total + (pltpu.roll(part, zz * step, 1) if zz else part)
     return total
 
 
@@ -781,7 +814,7 @@
     length_ref, att_ref, tok_ref, cot_ref, win_ref, win_own, wout_ref, wout_own, small_ref, wback_ref, wback_own, wq_own,
     out_ref, gh1_ref, do_out, grads_ref, sums_ref, wq_full, back_out,
     winv, wbackv, woutv, act_s, gp_s, gi_s, acc, first_s, n1_s, low_s, lowt_s, gsec_s, gh2_s, isum,
-    gb, rb, rx, ry, rx2, ry2, do_ref, do_in, send_sems, recv_sems, line_send, line_recv, local_sems,
+    gb, rb, rx, ry, do_ref, do_in, send_sems, recv_sems, line_send, line_recv, local_sems,
 ):
     s, z, core, chip = coordinates()
     other = 1 - core
@@ -824,14 +857,13 @@
         net.add((K_R1, zz), lambda zz=zz: gb.at[other, zz], lambda zz=zz: rb.at[zz], mate)
         for n, j in enumerate((1, 3)):
             net.add((K_X1, n, zz), lambda zz=zz, j=j: gb.at[core, zz, ch_of[j], xs], lambda zz=zz, n=n: rx.at[zz, n], peer[1])
-        net.add((K_X2, zz), lambda zz=zz: gb.at[core, zz, ch_of[2], xs], lambda zz=zz: rx2.at[zz], peer[2])
         for n, j in enumerate((2, 3)):
             net.add((K_Y1, n, zz), lambda zz=zz, j=j: gb.at[core, zz, ch_of[j], ys], lambda zz=zz, n=n: ry.at[zz, n], peer[2])
-        net.add((K_Y2, zz), lambda zz=zz: gb.at[core, zz, ch_of[1], ys], lambda zz=zz: ry2.at[zz], peer[1])
     for j in (1, 2, 3):
         net.add((K_DO, j), lambda j=j: do_ref.at[ch_of[j]], lambda j=j: do_in.at[j], peer[j])
     loc.add(K_DO_O, lambda: do_in, lambda: do_out)
-    loc.add(K_BACK_O, lambda: gb.at[core, :, chip], lambda: back_out)
+    for j in range(3):
+        loc.add((K_BACK_O, j), lambda j=j: gb.at[core, :, ch_of[j]], lambda j=j: back_out.at[j])
     shards = {K_OUT: (wout_own, wout_ref, woutv), K_IN: (win_own, win_ref, winv), K_BACK: (wback_own, wback_ref, wbackv)}
     loads = [(name, i) for name in shards for i in range(4) if name != K_BACK or i < 2]
     for name, i in loads:
@@ -867,22 +899,16 @@
         net.recv((K_X1, 1, zz), (K_Y1, 1, zz))
         add_into(gb, (core, zz, ch_of[2], xs), rx, (zz, 1))
         add_into(gb, (core, zz, ch_of[1], ys), ry, (zz, 1))
-        net.start((K_X2, zz), (K_Y2, zz))
         net.recv((K_X1, 0, zz), (K_Y1, 0, zz))
         add_into(gb, (core, zz, chip, xs), rx, (zz, 0))
         add_into(gb, (core, zz, chip, ys), ry, (zz, 0))
 
-    def step_three(zz):
-        net.recv((K_X2, zz), (K_Y2, zz))
-        add_into(gb, (core, zz, chip, xs), rx2, zz)
-        add_into(gb, (core, zz, chip, ys), ry2, zz)
-
     def during(n, works):
         for at, work in works.items():
             pl.when(n == at)(lambda work=work: (work(), None)[1])
 
     vectors = wide_vectors(small_ref)
-    vec = lambda i: vectors[i % 4][i // 4 : i // 4 + 1, :]
+    vec = lambda i: vectors[i : i + 1, :]
     loc.wait(*[(K_OUT, dz) for dz in range(4)])
     branch = vec(0)
     for g in range(4):
@@ -900,7 +926,7 @@
 
     def forward(n, carry):
         cols = pl.ds(pl.multiple_of(n * wide, 128), wide)
-        inner = dot(low_s[...], winv[:, cols]) + small_ref[n, 2:3, :].astype(f32)
+        inner = dot(low_s[...], winv[:, cols]) + small_ref[n, 6:7, :].astype(f32)
         value, slope = gelu_parts(inner)
         value = value.astype(bf16)
         act_s[n] = value
@@ -1000,8 +1026,7 @@
             for x in range(2):
                 grads_ref[lax.div(n, 2), zz, lax.rem(n, 2) * 2 + x, 0:step, :] = gin[:, x * ch : (x + 1) * ch]
         during(n, {
-            0: lambda: (step_two(1), step_three(0)), 1: lambda: step_two(2),
-            2: lambda: (step_two(3), step_three(1)), 3: lambda: step_three(2),
+            0: lambda: step_two(1), 1: lambda: step_two(2), 2: lambda: step_two(3),
         })
         return carry
 
@@ -1016,16 +1041,15 @@
         part = jnp.where(lane < step, part, 0.0)
         part = jnp.where(place == 6, isum[zz], part)
         sums_ref[zz, 0:16, :] = jnp.concatenate([part, jnp.zeros((8, width), f32)], axis=0).astype(bf16)
-    step_three(3)
     net.recv(*[(K_DO, j) for j in (1, 2, 3)])
-    loc.start(K_BACK_O, K_DO_O)
+    loc.start(*[(K_BACK_O, j) for j in range(3)], K_DO_O)
     line.step(3, K_QKV)
     net.start((K_QKV, 3))
     net.recv(*[(K_QKV, dz) for dz in (1, 2, 3)])
     for name in net.specs:
         net.sent(name)
     line.sent()
-    loc.wait(K_BACK_O, K_DO_O)
+    loc.wait(*[(K_BACK_O, j) for j in range(3)], K_DO_O)
 
 
 Q_PLACE, K_PLACE, V_PLACE = (4, 5, 6), (0, 2, 8), (1, 3, 9)
@@ -1039,7 +1063,7 @@
 def final_kernel(
     dproj_ref, wq_ref, wq_own, gh1_ref, gw_ref, hw_ref, fin_ref, finb_ref, sums_ref,
     gt_ref, gqkv_ref, gin_ref, gback_ref, gout_ref, qb_ref, vb_ref, o0, o1, o2, o3, o4, o5, ib_ref,
-    wv, local_sems,
+    wv, row, local_sems,
 ):
     z = lax.axis_index("fsdp")
     loc = Local(local_sems)
@@ -1083,11 +1107,12 @@
     tile_of = lambda t: packed_tile(0, z, slice(piece, piece + 16), t)
     for ref, places in ((qb_ref, Q_PLACE), (vb_ref, V_PLACE)):
         first = jnp.where(lane < 64, half_tile(tile_of, places[0], 0), half_tile(tile_of, places[1], 1))
-        ref[:, 0:128] = first[0:1]
-        ref[:, 128:192] = half_tile(tile_of, places[2], 0)[0:1, 0:64]
+        row[0:1, 0:128] = first[0:1]
+        row[0:1, 128:256] = half_tile(tile_of, places[2], 0)[0:1]
+        ref[...] = row[0:1, 0:shard].reshape(shard)
     for i, ref in enumerate((o0, o1, o2, o3, o4, o5)):
-        ref[...] = up(sums_ref[...])[i : i + 1, 0:shard]
-    ib_ref[...] = up(sums_ref[...])[6:7, :]
+        ref[...] = up(sums_ref[...])[i : i + 1, 0:shard].reshape(shard)
+    ib_ref[...] = up(sums_ref[...])[6:7, :].reshape(ib_ref.shape[0])
     loc.wait(*range(PLANES))
     total = gh1_ref[...]
     for g in range(4):
@@ -1107,7 +1132,7 @@
 
 
 def semaphores(line=False):
-    counts = (SEMS, SEMS) + ((5 * 3, PLANES * 3) if line else ()) + (16,)
+    counts = (SEMS, SEMS) + ((5 * 2, PLANES * 2) if line else ()) + (16,)
     return [pltpu.SemaphoreType.DMA((n,)) for n in counts]
 
 
@@ -1117,7 +1142,7 @@
     )
 
 
-def run_forward(lengths, tokens, w_qkv, w_in, w_back, w_out, small):
+def run_forward(lengths, tokens, w_qkv, w_in, w_back, w_out, *vectors):
     rows, width = tokens.shape
     shard = w_qkv.shape[0]
     hidden = w_in.shape[1]
@@ -1131,15 +1156,16 @@
             S((PLANES * shard, hidden), bf16), S((width, width), bf16),
             S((CHIPS, shard, PACK), bf16), S((hidden, width), bf16),
         ),
-        in_specs=[SMEM] + [ANY] * 6,
+        in_specs=[SMEM] + [ANY] * 5 + [VMEM] * 9,
         out_specs=[ANY] * 11,
         scratch_shapes=[
             vmem((4, rows, width)), vmem((width, PACK)), vmem(q_shape), vmem(kv_shape), vmem(kv_shape), vmem(q_shape),
             vmem((4, rows, 256)), vmem((4, rows, 256)), vmem((4, rows, 384)), vmem((4, rows, 384)),
             vmem((PLANES, 16, width)), vmem((shard, w_qkv.shape[1])), vmem((CHIPS, shard, PACK)),
+            vmem((8, width), f32), vmem((8, 256), f32),
         ] + semaphores(line=True),
         compiler_params=params(1),
-    )(lengths, tokens, w_qkv, w_in, w_back, w_out, small)
+    )(lengths, tokens, w_qkv, w_in, w_back, w_out, *vectors)
 
 
 def run_backward(do, q, k, v, o, tok, grads, sums, back):
@@ -1153,7 +1179,7 @@
     return pl.pallas_call(
         backward_kernel,
         out_shape=(
-            S((4, rows, PACK), bf16), S((2, 4, ext, 384), bf16), S((2, 4, ext, 256), bf16), S((2, 4, length, cols), bf16), S((2, 4) + back.shape[1:], bf16), S((16, width), bf16),
+            S((4, rows, PACK), bf16), S((2, 4, ext, 384), bf16), S((2, 4, ext, 256), bf16), S((2, 4, length, cols), bf16), S((2, 4) + back.shape[2:], bf16), S((16, width), bf16),
         ),
         in_specs=[ANY] * 9,
         out_specs=[ANY] * 6,
@@ -1165,7 +1191,8 @@
             *[vmem(lead + (ext, n)) for n in (384, 256) for lead in ((2, 4), (4,), (4,), (3,), (2, 4))],
             vmem((4, 4, length, cols)), vmem((4, 4, length, cols)),
             vmem((4, 2, cut, cols)), vmem((4, 2, length - cut, cols)), vmem((4, cut, cols)), vmem((4, length - cut, cols)),
-            vmem((3, length, cols)), vmem((4,) + back.shape[1:]), vmem((2, 4, length, cols)), vmem((2, 4) + back.shape[1:]),
+            vmem((3, length, cols)), vmem((3,) + back.shape[2:]), vmem(back.shape[1:]),
+            vmem((4, back.shape[2] // 2, cols)), vmem((4, back.shape[2] // 2, cols)), vmem((2, 4, length, cols)), vmem((2, 4) + back.shape[2:]),
             vmem((4, 4, 16, width)), vmem((3, 4, 16, width)), vmem((3, 16, width)), vmem((16, width)),
         ] + semaphores(),
         compiler_params=params(2),
@@ -1183,7 +1210,7 @@
         ffn_kernel,
         out_shape=(
             one, S((rows, width), f32), S((4, rows, 256), bf16), S((2, 4, 4, width // 4 + 48, ch), bf16), S((4, 16, width), bf16),
-            S((PLANES,) + wq.shape, bf16), S((4, 2 * bp, ch), bf16),
+            S((PLANES,) + wq.shape, bf16), S((3, 4, 2 * bp, ch), bf16),
         ),
         in_specs=[SMEM] + [VMEM] * 3 + [ANY] * 4 + [VMEM] + [ANY] * 3,
         out_specs=[VMEM] * 2 + [ANY] + [VMEM] * 2 + [ANY] * 2,
@@ -1192,7 +1219,7 @@
             vmem((4, rows, 2 * ch)), vmem((4, rows, 2 * ch), f32), vmem((4, rows, 2 * ch)),
             vmem((rows, width), f32), vmem((rows, width), f32), vmem((rows, width), f32),
             vmem((rows, width)), vmem((width, rows)), vmem((rows, width)), vmem((rows, width), f32), vmem((4, 8, 2 * ch), f32),
-            vmem((2, 4, 4, 2 * bp, ch)), vmem((4, 4, 2 * bp, ch)), vmem((4, 2, bp, ch)), vmem((4, 2, bp, ch)), vmem((4, bp, ch)), vmem((4, bp, ch)),
+            vmem((2, 4, 4, 2 * bp, ch)), vmem((4, 4, 2 * bp, ch)), vmem((4, 2, bp, ch)), vmem((4, 2, bp, ch)),
             vmem((4, rows, 256)), vmem((4, rows, 256)),
             pltpu.SemaphoreType.DMA((SEMS,)), pltpu.SemaphoreType.DMA((SEMS,)),
             pltpu.SemaphoreType.DMA((5,)), pltpu.SemaphoreType.DMA((PLANES,)), pltpu.SemaphoreType.DMA((24,)),
@@ -1205,16 +1232,16 @@
     rows, width = gh1.shape
     shard = width // PLANES
     S = jax.ShapeDtypeStruct
-    one = S((1, shard), f32)
+    one = S((shard,), f32)
     return pl.pallas_call(
         final_kernel,
         out_shape=(
             S((rows, width), bf16), S((shard, 3 * width), f32), S((shard, 8 * fin.shape[3]), f32),
-            S((2 * fin.shape[3], width), f32), S((shard, width), f32), one, one, one, one, one, one, one, one, S((1, width), f32),
+            S((2 * fin.shape[3], width), f32), S((shard, width), f32), one, one, one, one, one, one, one, one, S((width,), f32),
         ),
         in_specs=[VMEM, ANY, ANY] + [VMEM] * 6,
         out_specs=[VMEM] * 14,
-        scratch_shapes=[vmem((4, width, PACK)), pltpu.SemaphoreType.DMA((4,))],
+        scratch_shapes=[vmem((4, width, PACK)), vmem((8, 256), f32), pltpu.SemaphoreType.DMA((4,))],
         compiler_params=pltpu.CompilerParams(vmem_limit_bytes=VMEM_BYTES),
     )(dproj, wq_full, wq, gh1, gw, hw, fin, finb, sums)
 
@@ -1223,26 +1250,16 @@
     tokens, lengths, w_qkv, q_bias, v_bias, w_out, out_bias, ln1_gain, ln1_bias,
     w_in, in_bias, w_back, back_bias, ln2_gain, ln2_bias, cotangent,
 ):
-    width = tokens.shape[2]
-    line = lambda *a: jnp.concatenate(a + (jnp.zeros((width - sum(x.shape[0] for x in a),), bf16),))
-    gap = jnp.zeros((64,), bf16)
-    small = jnp.stack([
-        jnp.concatenate([out_bias, ln1_gain, ln1_bias, back_bias]), line(ln2_gain, ln2_bias), in_bias,
-        line(gap, v_bias[0:64], gap, v_bias[64:128], q_bias, gap, gap, v_bias[128:192]),
-    ] + [jnp.zeros((width,), bf16)] * 12)
+    vectors = (out_bias, ln1_gain, ln1_bias, back_bias, ln2_gain, ln2_bias, in_bias, q_bias, v_bias)
     q, k, v, o, tok_all, att, small_all, full_in, full_out, wq, full_back = run_forward(
-        lengths, tokens[0], w_qkv, w_in, w_back, w_out, small
+        lengths, tokens[0], w_qkv, w_in, w_back, w_out, *vectors
     )
     output, gh1, do, grads, sums, wq_full, back = run_ffn(
         lengths, att, tokens[0], cotangent[0], full_in, w_in, full_out, w_out, small_all, full_back, w_back, wq
     )
     dproj, gw, hw, fin, finb, sums_f = run_backward(do, q, k, v, o, tok_all, grads, sums, back)
     gt, gqkv, gin, gback, gout, qb, vb, ob, g1, b1, bb, g2, b2, ib = run_final(dproj, wq_full, wq, gh1, gw, hw, fin, finb, sums_f)
-    flat = lambda a: a.reshape(a.shape[1])
-    return (
-        output[None], gt[None], gqkv, flat(qb), flat(vb), gout, flat(ob), flat(g1), flat(b1), gin, flat(ib),
-        gback, flat(bb), flat(g2), flat(b2),
-    )
+    return (output[None], gt[None], gqkv, qb, vb, gout, ob, g1, b1, gin, ib, gback, bb, g2, b2)
 
 
 masked_score = -1e30

time: 235 us -> 221 us (0.940)
  Pallas kernels: 227 us -> 219 us
  local copies, waits for them, and re-layouts: 4.38 us -> 0.82 us
  other arithmetic: 2.82 us -> 0 us
    pallas_call x1, Pallas kernels: 63.2 us -> 56.8 us  [run_ffn(): pl.pallas_call(ffn_kernel, out_shape=(one, S((rows, width), f32), S((4, r...]
where the time goes in v4:
time: 221 us
  Pallas kernels  219 us (99%)
    pallas_call x1, Pallas kernels, run_backward(): pl.pallas_call(backward_kernel, out_shape=(S((4, rows, PACK), bf16), S((2...  84.9 us
    pallas_call x1, Pallas kernels, run_forward(): pl.pallas_call(forward_kernel, out_shape=(S(q_shape, bf16), S(kv_shape, b...  67.9 us
    pallas_call x1, Pallas kernels, run_ffn(): pl.pallas_call(ffn_kernel, out_shape=(one, S((rows, width), f32), S((4, r...  56.8 us
    pallas_call x1, Pallas kernels, run_final(): pl.pallas_call(final_kernel, out_shape=(S((rows, width), bf16), S((shard,...  8.96 us

profile of v4, /device:TPU:1, one launch (start us, length us, event | category | flops | bytes accessed | tf_op | source)
XLA Modules:
  0.0 220.7 jit_solution(1477284738903796954)
XLA Ops:
  1.3 67.9 %shard_map.271 = (bf16[3,1536,128]{2,1,0:T(8,128)(2,1)}, bf16[3,3072,128]{2,1,0:T(8,128)(2,1)}, bf16[3,3072,128]{2,1,0:T(8,128)(2,1)}, bf16[3,1536,128]{2,1,0:T(...) custom-call(s32[1]{0:T(128)S(6)} %copy.32.length_ref, ...), custom_call_target="tpu_custom_call" | custom-call | tf_op jit(solution)/shard_map/pallas_call | solution.py:1151
  69.2 56.8 %shard_map.272 = (bf16[384,768]{1,0:T(8,128)(2,1)}, f32[384,768]{1,0:T(8,128)}, bf16[4,384,256]{2,1,0:T(8,128)(2,1)}, bf16[2,4,4,240,384]{4,3,2,1,0:T(8,128)(2,1...) custom-call(s32[1]{0:T(128)S(6)} %copy.32.length_ref, ...), custom_call_target="tpu_custom_call" | custom-call | tf_op jit(solution)/shard_map/pallas_call | solution.py:1209
  126.0 84.9 %shard_map.273 = (bf16[4,384,640]{2,1,0:T(8,128)(2,1)}, bf16[2,4,112,384]{3,2,1,0:T(8,128)(2,1)}, bf16[2,4,112,256]{3,2,1,0:T(8,128)(2,1)}, bf16[2,4,240,384]{3,...) custom-call(bf16[4,384,256]{2,1,0:T(8,128)(2,1)} %get-tuple-element.60.do_ref, ...), custom_call_target="tpu_custom_call" | custom-call | tf_op jit(solution)/shard_map/pallas_call | solution.py:1179
  210.9 0.0 copy-start
  210.9 9.0 %shard_map.274 = (bf16[384,768]{1,0:T(8,128)(2,1)}, f32[192,2304]{1,0:T(8,128)}, f32[192,3072]{1,0:T(8,128)}, f32[768,768]{1,0:T(8,128)}, f32[192,768]{1,0:T(8,1...) custom-call(bf16[4,384,640]{2,1,0:T(8,128)(2,1)} %get-tuple-element., ...), custom_call_target="tpu_custom_call" | custom-call | tf_op jit(solution)/shard_map/pallas_call | solution.py:1236
  219.9 0.0 copy-done
  219.9 0.8 copy.33
Async XLA Ops:
  210.9 9.0 %copy-start = (bf16[384,768]{1,0:T(8,128)(2,1)S(1)}, bf16[384,768]{1,0:T(8,128)(2,1)}, u32[]{:S(2)}) copy-start(bf16[384,768]{1,0:T(8,128)(2,1)} %get-tuple-element.59) | copy-start | bytes 1769476

commit v5 on v4

--- a/solution.py
+++ b/solution.py
@@ -30,7 +30,8 @@
     K_K_O, K_M, K_O, K_OUT, K_O_O, K_Q, K_QKV, K_Q_O, K_R1, K_RAW, K_RZ, K_RZB, K_S0, K_S1, K_S2, K_SMALL,
     K_SMALL_O, K_SUMS, K_SUMS_O, K_SZ, K_T1A, K_T1B, K_T2A, K_T2B, K_T3A, K_T3B, K_TOK, K_TOK_O, K_V, K_V_O,
     K_WQ, K_WQM, K_WQ_O, K_X1, K_X2, K_Y1, K_Y2, K_Z,
-) = range(100, 168)
+    K_GH1, K_RES, K_GR, K_DO1,
+) = range(100, 172)
 
 
 def dot(a, b, dims=NN):
@@ -296,17 +297,6 @@
     greet(peer[1:] + [mate] + plane[1:])
     net.start(K_T1A, K_T2B, K_T1B, K_T2A)
     lane = lanes_of()
-    vec_s[...] = jnp.zeros_like(vec_s)
-    vec_v[...] = jnp.zeros_like(vec_v)
-    for i, ref in enumerate((ob_ref, g1_ref, n1_ref, bb_ref, g2_ref, n2_ref)):
-        vec_s[i : i + 1, 0:shard] = ref[...].astype(f32).reshape(1, shard)
-    vec_s[6:7, :] = ib_ref[...].astype(f32).reshape(1, ib_ref.shape[0])
-    vec_s[7:8, 256 : 256 + shard] = qb_ref[...].astype(f32).reshape(1, shard)
-    vec_v[0:1, 0:shard] = vb_ref[...].astype(f32).reshape(1, shard)
-    first, last = vec_v[:, 0:128], vec_v[:, 128:256]
-    for t, tile in ((0, pltpu.roll(first, 64, 1)), (1, first), (4, pltpu.roll(last, 64, 1))):
-        vec_s[7:8, t * 128 : (t + 1) * 128] = jnp.where(lane < 64, 0.0, tile[0:1])
-    small[z] = jnp.concatenate([vec_s[...], jnp.zeros_like(vec_s)], axis=0).astype(bf16)
     loc.wait(K_RAW)
     for g in range(CHIPS):
         for t in range(PACK // 128):
@@ -321,7 +311,19 @@
                 halves.append(half_tile(tile_of, block, upper))
             wq_ref[g, :, t * 128 : (t + 1) * 128] = jnp.where(lane < 64, halves[0], halves[1]).astype(bf16)
     loc.start(K_WQ, K_WQ_O)
-    net.start(*[(K_WQ, dz) for dz in (1, 2, 3)], *[(K_SMALL, dz) for dz in (1, 2, 3)])
+    net.start(*[(K_WQ, dz) for dz in (1, 2, 3)])
+    vec_s[...] = jnp.zeros_like(vec_s)
+    vec_v[...] = jnp.zeros_like(vec_v)
+    for i, ref in enumerate((ob_ref, g1_ref, n1_ref, bb_ref, g2_ref, n2_ref)):
+        vec_s[i : i + 1, 0:shard] = ref[...].astype(f32).reshape(1, shard)
+    vec_s[6:7, :] = ib_ref[...].astype(f32).reshape(1, ib_ref.shape[0])
+    vec_s[7:8, 256 : 256 + shard] = qb_ref[...].astype(f32).reshape(1, shard)
+    vec_v[0:1, 0:shard] = vb_ref[...].astype(f32).reshape(1, shard)
+    first, last = vec_v[:, 0:128], vec_v[:, 128:256]
+    for t, tile in ((0, pltpu.roll(first, 64, 1)), (1, first), (4, pltpu.roll(last, 64, 1))):
+        vec_s[7:8, t * 128 : (t + 1) * 128] = jnp.where(lane < 64, 0.0, tile[0:1])
+    small[z] = jnp.concatenate([vec_s[...], jnp.zeros_like(vec_s)], axis=0).astype(bf16)
+    net.start(*[(K_SMALL, dz) for dz in (1, 2, 3)])
     for dz in (1, 2, 3):
         net.recv((K_WQ, dz))
         net.start((K_WQM, dz))
@@ -477,9 +479,9 @@
 
 
 def backward_kernel(
-    do_ref, q_ref, k_ref, v_ref, o_ref, tok_ref, grads_ref, sums_ref, back_ref,
+    do_ref, do1_ref, q_ref, k_ref, v_ref, o_ref, tok_ref, grads_ref, sums_ref, back_ref,
     dproj_out, gw_out, hw_out, fin_out, finb_out, sums_out,
-    do_s, q_s, k_s, v_s, o_s, doa, tok, tokt, dqs, dq_keep, kv_own, kvs, kvr, dall, dproj,
+    do_s, do1_s, q_s, k_s, v_s, o_s, doa, tok, tokt, dqs, dq_keep, kv_own, kvs, kvr, dall, fold,
     gw, gwr, gz, gzr, gwf, hw, hwr, hz, hzr, hwf, acc, rb, rx, ry, rx2, ry2, rz, rzb, backv, bx2, by2, fin, finb, sums, sums_r, sums_z, sums_f,
     send_sems, recv_sems, local_sems,
 ):
@@ -500,10 +502,18 @@
 
     for h in range(GROUP_HEADS):
         net.add((K_KV, h), lambda h=h: kvs.at[h], lambda h=h: kvr.at[h], mate)
-        place = ((0, 128), (128, 384), (384, 640))[h]
+        kv_cols = slice(KV_TILE[h] * 128, KV_TILE[h] * 128 + 128)
         for j in (1, 2, 3):
-            net.add((K_DP, h, j), lambda j=j, place=place: dall.at[j, :, place[0] : place[1]],
-                    lambda place=place: dproj.at[chip, :, place[0] : place[1]], peer[j])
+            net.add((K_DP, h, j), lambda j=j, cols=kv_cols: dall.at[j, :, cols],
+                    lambda cols=kv_cols: dproj_out.at[chip, :, cols], peer[j])
+    for j in (1, 2, 3):
+        net.add((K_DP, K_Q, j), lambda j=j: dall.at[j, :, 256:384], lambda: dproj_out.at[chip, :, 256:384], peer[j])
+        net.add((K_DP, K_O, j), lambda j=j: fold.at[j], lambda: dproj_out.at[chip, 0 : rows // 2, 384:512], peer[j])
+    loc.add((K_DP, 0), lambda: dall.at[0, :, 0:384], lambda: dproj_out.at[chip, :, 0:384])
+    loc.add((K_DP, 1), lambda: dall.at[0, :, 512:640], lambda: dproj_out.at[chip, :, 512:640])
+    loc.add((K_DP, 2), lambda: fold.at[0], lambda: dproj_out.at[chip, 0 : rows // 2, 384:512])
+    for j in (1, 2, 3):
+        net.add((K_DO, j), lambda j=j: do1_ref.at[ch[j]], lambda j=j: do1_s.at[j], peer[j])
     order = (3, 2, 1, 0)
     for dz in order:
         net.add((K_R1, dz), lambda dz=dz: grads_ref.at[other, zs[dz]], lambda dz=dz: rb.at[zs[dz]], mate)
@@ -544,29 +554,27 @@
             net.add((a, K_F, j), lambda f=f: f.at[core, chip], lambda f=f: f.at[core, chip], peer[j])
         net.add((a, K_M), lambda f=f: f.at[core], lambda f=f: f.at[core], mate)
 
-    loads = ((K_DO, lambda: do_ref, lambda: do_s), (K_O, lambda: o_ref, lambda: o_s),
+    loads = ((K_DO, lambda: do_ref, lambda: do_s), (K_DO1, lambda: do1_ref.at[chip], lambda: do1_s.at[0]), (K_O, lambda: o_ref, lambda: o_s),
              (K_TOK, lambda: tok_ref, lambda: tok), (K_Q, lambda: q_ref, lambda: q_s),
              (K_K, lambda: k_ref, lambda: k_s), (K_V, lambda: v_ref, lambda: v_s),
              (K_SUMS, lambda: sums_ref, lambda: sums.at[0]), (K_BACK, lambda: back_ref.at[0], lambda: backv), (K_ACC, lambda: grads_ref.at[core], lambda: acc))
     for name, src, dst in loads:
         loc.add(name, src, dst)
-    stores = ((K_DP_O, dproj, dproj_out), (K_GW_O, gwf, gw_out), (K_HW_O, hwf, hw_out), (K_FIN_O, fin, fin_out), (K_FINB_O, finb, finb_out))
+    stores = ((K_GW_O, gwf, gw_out), (K_HW_O, hwf, hw_out), (K_FIN_O, fin, fin_out), (K_FINB_O, finb, finb_out))
     for name, src, dst in stores:
         loc.add(name, lambda src=src: src, lambda dst=dst: dst)
     loc.add(K_SUMS_O, lambda: sums_f, lambda: sums_out)
 
-    loc.start(*[name for name, _, _ in loads])
+    loc.start(K_DO, K_O, K_Q, K_K, K_V)
     greet(peer[1:] + [mate] + plane[1:])
-    net.start(K_S0, *[(K_R1, dz) for dz in order])
-    net.start((K_X2, K_BACK), (K_Y2, K_BACK))
+    net.start((K_X2, K_BACK), (K_Y2, K_BACK), K_S0, *[(K_R1, dz) for dz in order])
+    loc.start(K_ACC, K_BACK, K_SUMS, K_TOK, K_DO1)
     lane = lanes_of()
-    loc.wait(K_TOK)
-    for j in range(4):
-        tokt[:, j * rows : (j + 1) * rows] = tok[j].T
-    loc.wait(K_DO, K_O, K_Q, K_K, K_V, K_SUMS, K_BACK, K_ACC)
-    for j in range(4):
-        for h in range(GROUP_HEADS):
-            tile = do_s[j, :, (h // 2) * 128 : (h // 2) * 128 + 128].astype(f32)
+    loc.wait(K_DO, K_O)
+
+    def output_grad(h, tiles):
+        for j in range(4):
+            tile = tiles[j].astype(f32)
             if h == 1:
                 tile = pltpu.roll(tile, 64, 1)
             tile = jnp.where(lane < 64, tile, 0.0)
@@ -575,6 +583,24 @@
             hi, mid, low = split3(-delta)
             tile = jnp.where(lane == 64, hi, jnp.where(lane == 65, mid, jnp.where(lane == 66, low, tile)))
             doa[h, r, :] = tile.astype(bf16)
+
+    output_grad(0, do_s)
+    output_grad(1, do_s)
+    loc.wait(K_Q, K_K, K_V)
+
+    def late_loads():
+        loc.wait(K_ACC, K_BACK, K_SUMS)
+        net.start(*[(K_DO, j) for j in (1, 2, 3)])
+
+    def transpose_tokens():
+        loc.wait(K_TOK)
+        for j in range(4):
+            tokt[:, j * rows : (j + 1) * rows] = tok[j].T
+
+    def last_head_grad():
+        loc.wait(K_DO1)
+        net.recv(*[(K_DO, j) for j in (1, 2, 3)])
+        output_grad(2, do1_s)
 
     def add_into(ref, index, other_ref, other_index):
         ref[index] = (ref[index].astype(f32) + other_ref[other_index].astype(f32)).astype(bf16)
@@ -684,14 +710,16 @@
     key_chunk, query_tile = 2 * rows, 256
     per_head = 4
 
-    def head_end(h):
-        net.recv((K_KV, h))
-        tile = KV_TILE[h]
-        dst = (0, 1, 4)[h] * 128
-        for j in range(4):
+    def head_keys(h, slots):
+        cols = slice(KV_TILE[h] * 128, KV_TILE[h] * 128 + 128)
+        for j in slots:
             r = slice(j * rows, (j + 1) * rows)
             both = kv_own[r, :] + kvr[h, r, :].astype(f32)
-            dall[j, :, dst : dst + 128] = both.astype(bf16)
+            dall[j, :, cols] = both.astype(bf16)
+            if j:
+                net.start((K_DP, h, j))
+
+    def head_queries(h):
         dq = dqs[...].T * 0.125
         for j in range(4):
             r = slice(j * rows, (j + 1) * rows)
@@ -700,19 +728,23 @@
                 dq_keep[r, :] = mine
             elif h == 1:
                 dall[j, :, 256:384] = jnp.where(lane < 64, dq_keep[r, :], pltpu.roll(mine, 64, 1)).astype(bf16)
+                if j:
+                    net.start((K_DP, K_Q, j))
             else:
+                upper = pltpu.roll(mine[rows // 2 :, :], 64, 1)
+                fold[j] = jnp.where(lane < 64, mine[: rows // 2, :], upper).astype(bf16)
+                if j:
+                    net.start((K_DP, K_O, j))
                 dall[j, :, 384:512] = jnp.where(lane < 64, mine, 0.0).astype(bf16)
-        for j in (1, 2, 3):
-            net.start((K_DP, h, j))
 
     stages = {
-        0: lambda: (step_one(3), back_plane(), sums_step(0)),
+        0: lambda: (late_loads(), step_one(3), back_plane(), sums_step(0)),
         1: lambda: (step_one(2), sums_step(1)),
         2: lambda: (step_two(3), step_one(1), sums_step(2)),
         3: lambda: (step_three(3), step_two(2)),
         4: lambda: (step_one(0), back_total()),
-        5: lambda: (step_three(2), step_two(1)),
-        6: lambda: (step_two(0), back_forward()),
+        5: lambda: (step_three(2), step_two(1), transpose_tokens()),
+        6: lambda: (step_two(0), back_forward(), last_head_grad()),
         7: lambda: (step_three(1), weight_part(K_G, gw, 0, 384)),
         8: lambda: (step_three(0), back_mate()),
         9: lambda: (fin_total(), weight_pair(K_G, gw, gwr, gz)),
@@ -721,7 +753,7 @@
 
     def visit(t, carry):
         h, part = lax.div(t, per_head), lax.rem(t, per_head)
-        start = pl.multiple_of(lax.rem(part + 2, 4) * key_chunk, key_chunk)
+        start = pl.multiple_of(jnp.where(part < 2, part + 2, 3 - part) * key_chunk, key_chunk)
         krows = pl.ds(start, key_chunk)
         k, v = k_s[h, krows, :], v_s[h, krows, :]
         kt = k.T
@@ -748,16 +780,22 @@
 
         @pl.when(part >= 2)
         def _():
-            kv_own[pl.ds(pl.multiple_of((part - 2) * key_chunk, key_chunk), key_chunk), :] = packed
+            kv_own[pl.ds(pl.multiple_of((3 - part) * key_chunk, key_chunk), key_chunk), :] = packed
 
         for hh in range(GROUP_HEADS):
             @pl.when(t == hh * per_head + 1)
             def _(hh=hh):
                 net.start((K_KV, hh))
 
+            @pl.when(t == hh * per_head + 2)
+            def _(hh=hh):
+                net.recv((K_KV, hh))
+                head_keys(hh, (2, 3))
+
             @pl.when(t == hh * per_head + 3)
             def _(hh=hh):
-                head_end(hh)
+                head_keys(hh, (1, 0))
+                head_queries(hh)
         for at, work in stages.items():
             pl.when(t == at)(lambda work=work: (work(), None)[1])
         return carry
@@ -765,23 +803,23 @@
     lax.fori_loop(0, GROUP_HEADS * per_head, visit, 0)
 
     weight_part(K_H, hw, 384, PACK)
-    dproj[chip] = dall[0]
+    loc.start((K_DP, 0), (K_DP, 1), (K_DP, 2))
     weight_pair(K_H, hw, hwr, hz)
     weight_mate(K_G)
     net.recv(K_F3X, K_F3Y)
     net.start(K_FM)
     weight_total(K_H, hz, hzr, hwf)
-    for h in range(GROUP_HEADS):
+    for h in (0, 1, 2, K_Q, K_O):
         for j in (1, 2, 3):
             net.recv((K_DP, h, j))
     net.recv(K_FM, K_BM, (K_G, K_M))
-    loc.start(K_DP_O, K_GW_O, K_FIN_O, K_FINB_O)
+    loc.start(K_GW_O, K_FIN_O, K_FINB_O)
     weight_mate(K_H)
     net.recv((K_H, K_M))
     loc.start(K_HW_O)
     for name in net.specs:
         net.sent(name)
-    loc.wait(K_DP_O, K_GW_O, K_HW_O, K_FIN_O, K_FINB_O, K_SUMS_O)
+    loc.wait((K_DP, 0), (K_DP, 1), (K_DP, 2), K_GW_O, K_HW_O, K_FIN_O, K_FINB_O, K_SUMS_O)
 
 
 def gelu_parts(u):
@@ -812,9 +850,9 @@
 
 def ffn_kernel(
     length_ref, att_ref, tok_ref, cot_ref, win_ref, win_own, wout_ref, wout_own, small_ref, wback_ref, wback_own, wq_own,
-    out_ref, gh1_ref, do_out, grads_ref, sums_ref, wq_full, back_out,
+    res_out, gh1_out, do_out, do1_out, grads_out, sums_ref, wq_full, back_out,
     winv, wbackv, woutv, act_s, gp_s, gi_s, acc, first_s, n1_s, low_s, lowt_s, gsec_s, gh2_s, isum,
-    gb, rb, rx, ry, do_ref, do_in, send_sems, recv_sems, line_send, line_recv, local_sems,
+    gb, rb, rx, ry, do_ref, do_in, out_ref, gh1_ref, grads_ref, send_sems, recv_sems, line_send, line_recv, local_sems,
 ):
     s, z, core, chip = coordinates()
     other = 1 - core
@@ -860,8 +898,14 @@
         for n, j in enumerate((2, 3)):
             net.add((K_Y1, n, zz), lambda zz=zz, j=j: gb.at[core, zz, ch_of[j], ys], lambda zz=zz, n=n: ry.at[zz, n], peer[2])
     for j in (1, 2, 3):
-        net.add((K_DO, j), lambda j=j: do_ref.at[ch_of[j]], lambda j=j: do_in.at[j], peer[j])
+        net.add((K_DO, j), lambda j=j: do_ref.at[0, ch_of[j]], lambda j=j: do_in.at[j], peer[j])
     loc.add(K_DO_O, lambda: do_in, lambda: do_out)
+    loc.add(K_DO1, lambda: do_ref.at[1], lambda: do1_out)
+    loc.add(K_GH1, lambda: gh1_ref, lambda: gh1_out)
+    loc.add(K_RES, lambda: out_ref, lambda: res_out)
+    for n in range(PLANES):
+        cut_of = lambda ref, n=n: ref.at[n // 2, :, pl.ds(n % 2 * 2, 2)]
+        loc.add((K_GR, n), lambda cut_of=cut_of: cut_of(grads_ref), lambda cut_of=cut_of: cut_of(grads_out))
     for j in range(3):
         loc.add((K_BACK_O, j), lambda j=j: gb.at[core, :, ch_of[j]], lambda j=j: back_out.at[j])
     shards = {K_OUT: (wout_own, wout_ref, woutv), K_IN: (win_own, win_ref, winv), K_BACK: (wback_own, wback_ref, wbackv)}
@@ -922,7 +966,7 @@
     first_s[...] = first
     low_s[...] = first.astype(bf16)
     lowt_s[...] = first.astype(bf16).T
-    loc.wait(*[(name, i) for name, i in loads if name != K_OUT])
+    loc.wait(*[(K_IN, i) for i in range(4)])
 
     def forward(n, carry):
         cols = pl.ds(pl.multiple_of(n * wide, 128), wide)
@@ -940,6 +984,7 @@
         zz = lines[i]
         return dot(act_s[zz], wbackv[pl.ds(pl.multiple_of(zz * back, 16), back), :])
 
+    loc.wait((K_BACK, 0), (K_BACK, 1))
     acc[...] = second_layer(0)
     acc[...] += second_layer(1)
     hop_three(2)
@@ -956,6 +1001,7 @@
     inverse = lax.rsqrt(row_mean(centred * centred) + 1e-5)
     normed = centred * inverse
     out_ref[...] = ((normed * vec(4) + vec(5)) * valid).astype(bf16)
+    loc.start(K_RES)
     grad = cot_ref[...].astype(f32) * valid
     sum_rows = lambda a: jnp.sum(a, axis=0, keepdims=True)
     g2_gain, g2_bias = sum_rows(grad * normed), sum_rows(grad)
@@ -1003,16 +1049,20 @@
     scaled = grad * vec(1)
     gh1 = inverse1 * (scaled - row_mean(scaled) - normed * row_mean(scaled * normed))
     gh1_ref[...] = gh1
+    loc.start(K_GH1)
     gbranch = gh1.astype(bf16)
     out_sum = sum_rows(gbranch.astype(f32))
     for g in range(4):
         w = woutv[g * step : (g + 1) * step, :]
-        do_ref[g, :, 0:step] = dot(gbranch, w, NT).astype(bf16)
-        do_ref[g, :, step:] = jnp.zeros((rows, do_ref.shape[2] - step), bf16)
+        part = dot(gbranch, w, NT).astype(bf16)
+        do_ref[0, g] = part[:, 0:128]
+        do_ref[1, g, :, 0 : step - 128] = part[:, 128:step]
+        do_ref[1, g, :, step - 128 :] = jnp.zeros((rows, 256 - step), bf16)
     net.start(*[(K_DO, j) for j in (1, 2, 3)])
     line.step(2, K_QKV)
     net.start((K_QKV, 1), (K_QKV, 2))
-    do_in[0] = do_ref[chip]
+    do_in[0] = do_ref[0, chip]
+    loc.start(K_DO1)
     for g in range(4):
         gw = dot(att_ref[g, :, 0:step].T, gbranch).astype(bf16)
         part = step // 4
@@ -1026,7 +1076,8 @@
             for x in range(2):
                 grads_ref[lax.div(n, 2), zz, lax.rem(n, 2) * 2 + x, 0:step, :] = gin[:, x * ch : (x + 1) * ch]
         during(n, {
-            0: lambda: step_two(1), 1: lambda: step_two(2), 2: lambda: step_two(3),
+            0: lambda: (loc.start((K_GR, 0)), step_two(1)), 1: lambda: (loc.start((K_GR, 1)), step_two(2)),
+            2: lambda: (loc.start((K_GR, 2)), step_two(3)), 3: lambda: loc.start((K_GR, 3)),
         })
         return carry
 
@@ -1049,7 +1100,7 @@
     for name in net.specs:
         net.sent(name)
     line.sent()
-    loc.wait(*[(K_BACK_O, j) for j in range(3)], K_DO_O)
+    loc.wait(*[(K_BACK_O, j) for j in range(3)], K_DO_O, K_DO1, K_GH1, K_RES, *[(K_GR, n) for n in range(PLANES)])
 
 
 Q_PLACE, K_PLACE, V_PLACE = (4, 5, 6), (0, 2, 8), (1, 3, 9)
@@ -1063,10 +1114,11 @@
 def final_kernel(
     dproj_ref, wq_ref, wq_own, gh1_ref, gw_ref, hw_ref, fin_ref, finb_ref, sums_ref,
     gt_ref, gqkv_ref, gin_ref, gback_ref, gout_ref, qb_ref, vb_ref, o0, o1, o2, o3, o4, o5, ib_ref,
-    wv, row, local_sems,
+    wv, row, last, local_sems,
 ):
     z = lax.axis_index("fsdp")
     loc = Local(local_sems)
+    rows = gh1_ref.shape[0]
     shard = wq_ref.shape[2]
     for dz in range(PLANES):
         zz = flip(z, dz)
@@ -1116,7 +1168,12 @@
     loc.wait(*range(PLANES))
     total = gh1_ref[...]
     for g in range(4):
-        total = total + dot(dproj_ref[g], wv[g], NT)
+        total = total + dot(dproj_ref[g, :, 0:384], wv[g, :, 0:384], NT)
+        folded = up(dproj_ref[g, 0 : rows // 2, 384:512])
+        last[0 : rows // 2, 0:128] = jnp.where(lane < 64, folded, 0.0).astype(bf16)
+        last[rows // 2 :, 0:128] = jnp.where(lane < 64, pltpu.roll(folded, 64, 1), 0.0).astype(bf16)
+        last[:, 128:256] = dproj_ref[g, :, 512:640]
+        total = total + dot(last[...], wv[g, :, 384:640], NT)
     gt_ref[...] = total.astype(bf16)
 
 
@@ -1128,11 +1185,11 @@
 SMEM = pl.BlockSpec(memory_space=pltpu.SMEM)
 VMEM = pl.BlockSpec(memory_space=pltpu.VMEM)
 VMEM_BYTES = 60 * 2**20
-SEMS = 96
+SEMS = 112
 
 
 def semaphores(line=False):
-    counts = (SEMS, SEMS) + ((5 * 2, PLANES * 2) if line else ()) + (16,)
+    counts = (SEMS, SEMS) + ((5 * 2, PLANES * 2) if line else ()) + (32,)
     return [pltpu.SemaphoreType.DMA((n,)) for n in counts]
 
 
@@ -1168,7 +1225,7 @@
     )(lengths, tokens, w_qkv, w_in, w_back, w_out, *vectors)
 
 
-def run_backward(do, q, k, v, o, tok, grads, sums, back):
+def run_backward(do, do1, q, k, v, o, tok, grads, sums, back):
     rows = do.shape[1]
     width = tok.shape[2]
     shard = width // PLANES
@@ -1181,13 +1238,13 @@
         out_shape=(
             S((4, rows, PACK), bf16), S((2, 4, ext, 384), bf16), S((2, 4, ext, 256), bf16), S((2, 4, length, cols), bf16), S((2, 4) + back.shape[2:], bf16), S((16, width), bf16),
         ),
-        in_specs=[ANY] * 9,
+        in_specs=[ANY] * 10,
         out_specs=[ANY] * 6,
         scratch_shapes=[
-            vmem((4, rows, 256)), vmem(q.shape), vmem(k.shape), vmem(v.shape), vmem(o.shape), vmem(q.shape),
+            vmem((4, rows, 128)), vmem((4, rows, 128)), vmem(q.shape), vmem(k.shape), vmem(v.shape), vmem(o.shape), vmem(q.shape),
             vmem(tok.shape), vmem((width, 4 * rows)), vmem((128, 4 * rows), f32), vmem((4 * rows, 128), f32),
             vmem((4 * rows, 128), f32), vmem((3, 4 * rows, 128)), vmem((3, 4 * rows, 128)),
-            vmem((4, rows, PACK)), vmem((4, rows, PACK)),
+            vmem((4, rows, PACK)), vmem((4, rows // 2, 128)),
             *[vmem(lead + (ext, n)) for n in (384, 256) for lead in ((2, 4), (4,), (4,), (3,), (2, 4))],
             vmem((4, 4, length, cols)), vmem((4, 4, length, cols)),
             vmem((4, 2, cut, cols)), vmem((4, 2, length - cut, cols)), vmem((4, cut, cols)), vmem((4, length - cut, cols)),
@@ -1196,7 +1253,7 @@
             vmem((4, 4, 16, width)), vmem((3, 4, 16, width)), vmem((3, 16, width)), vmem((16, width)),
         ] + semaphores(),
         compiler_params=params(2),
-    )(do, q, k, v, o, tok, grads, sums, back)
+    )(do, do1, q, k, v, o, tok, grads, sums, back)
 
 
 def run_ffn(lengths, att, tokens, cotangent, full_in, w_in, full_out, w_out, small, full_back, w_back, wq):
@@ -1209,20 +1266,21 @@
     return pl.pallas_call(
         ffn_kernel,
         out_shape=(
-            one, S((rows, width), f32), S((4, rows, 256), bf16), S((2, 4, 4, width // 4 + 48, ch), bf16), S((4, 16, width), bf16),
+            one, S((rows, width), f32), S((4, rows, 128), bf16), S((4, rows, 128), bf16), S((2, 4, 4, width // 4 + 48, ch), bf16), S((4, 16, width), bf16),
             S((PLANES,) + wq.shape, bf16), S((3, 4, 2 * bp, ch), bf16),
         ),
         in_specs=[SMEM] + [VMEM] * 3 + [ANY] * 4 + [VMEM] + [ANY] * 3,
-        out_specs=[VMEM] * 2 + [ANY] + [VMEM] * 2 + [ANY] * 2,
+        out_specs=[ANY] * 5 + [VMEM] + [ANY] * 2,
         scratch_shapes=[
             vmem((width, hidden)), vmem((hidden, width)), vmem((width, width)),
             vmem((4, rows, 2 * ch)), vmem((4, rows, 2 * ch), f32), vmem((4, rows, 2 * ch)),
             vmem((rows, width), f32), vmem((rows, width), f32), vmem((rows, width), f32),
             vmem((rows, width)), vmem((width, rows)), vmem((rows, width)), vmem((rows, width), f32), vmem((4, 8, 2 * ch), f32),
             vmem((2, 4, 4, 2 * bp, ch)), vmem((4, 4, 2 * bp, ch)), vmem((4, 2, bp, ch)), vmem((4, 2, bp, ch)),
-            vmem((4, rows, 256)), vmem((4, rows, 256)),
+            vmem((2, 4, rows, 128)), vmem((4, rows, 128)),
+            vmem((rows, width)), vmem((rows, width), f32), vmem((2, 4, 4, width // 4 + 48, ch)),
             pltpu.SemaphoreType.DMA((SEMS,)), pltpu.SemaphoreType.DMA((SEMS,)),
-            pltpu.SemaphoreType.DMA((5,)), pltpu.SemaphoreType.DMA((PLANES,)), pltpu.SemaphoreType.DMA((24,)),
+            pltpu.SemaphoreType.DMA((5,)), pltpu.SemaphoreType.DMA((PLANES,)), pltpu.SemaphoreType.DMA((32,)),
         ],
         compiler_params=params(3),
     )(lengths, att, tokens, cotangent, full_in, w_in, full_out, w_out, small, full_back, w_back, wq)
@@ -1241,7 +1299,7 @@
         ),
         in_specs=[VMEM, ANY, ANY] + [VMEM] * 6,
         out_specs=[VMEM] * 14,
-        scratch_shapes=[vmem((4, width, PACK)), vmem((8, 256), f32), pltpu.SemaphoreType.DMA((4,))],
+        scratch_shapes=[vmem((4, width, PACK)), vmem((8, 256), f32), vmem((rows, 256)), pltpu.SemaphoreType.DMA((4,))],
         compiler_params=pltpu.CompilerParams(vmem_limit_bytes=VMEM_BYTES),
     )(dproj, wq_full, wq, gh1, gw, hw, fin, finb, sums)
 
@@ -1254,10 +1312,10 @@
     q, k, v, o, tok_all, att, small_all, full_in, full_out, wq, full_back = run_forward(
         lengths, tokens[0], w_qkv, w_in, w_back, w_out, *vectors
     )
-    output, gh1, do, grads, sums, wq_full, back = run_ffn(
+    output, gh1, do, do1, grads, sums, wq_full, back = run_ffn(
         lengths, att, tokens[0], cotangent[0], full_in, w_in, full_out, w_out, small_all, full_back, w_back, wq
     )
-    dproj, gw, hw, fin, finb, sums_f = run_backward(do, q, k, v, o, tok_all, grads, sums, back)
+    dproj, gw, hw, fin, finb, sums_f = run_backward(do, do1, q, k, v, o, tok_all, grads, sums, back)
     gt, gqkv, gin, gback, gout, qb, vb, ob, g1, b1, bb, g2, b2, ib = run_final(dproj, wq_full, wq, gh1, gw, hw, fin, finb, sums_f)
     return (output[None], gt[None], gqkv, qb, vb, gout, ob, g1, b1, gin, ib, gback, bb, g2, b2)
 

time: 221 us -> 217 us (0.982)
  Pallas kernels: 219 us -> 214 us
    pallas_call x1, Pallas kernels: 56.8 us -> 53.1 us  [run_ffn(): pl.pallas_call(ffn_kernel, out_shape=(one, S((rows, width), f32), S((4, r...]
where the time goes in v5:
time: 217 us
  Pallas kernels  214 us (99%)
    pallas_call x1, Pallas kernels, run_backward(): pl.pallas_call(backward_kernel, out_shape=(S((4, rows, PACK), bf16), S((2...  85 us
    pallas_call x1, Pallas kernels, run_forward(): pl.pallas_call(forward_kernel, out_shape=(S(q_shape, bf16), S(kv_shape, b...  66.6 us
    pallas_call x1, Pallas kernels, run_ffn(): pl.pallas_call(ffn_kernel, out_shape=(one, S((rows, width), f32), S((4, r...  53.1 us
    pallas_call x1, Pallas kernels, run_final(): pl.pallas_call(final_kernel, out_shape=(S((rows, width), bf16), S((shard,...  9.69 us

profile of v5, /device:TPU:1, one launch (start us, length us, event | category | flops | bytes accessed | tf_op | source)
XLA Modules:
  0.0 216.6 jit_solution(6496411599042621978)
XLA Ops:
  1.3 66.6 %shard_map.271 = (bf16[3,1536,128]{2,1,0:T(8,128)(2,1)}, bf16[3,3072,128]{2,1,0:T(8,128)(2,1)}, bf16[3,3072,128]{2,1,0:T(8,128)(2,1)}, bf16[3,1536,128]{2,1,0:T(...) custom-call(s32[1]{0:T(128)S(6)} %copy.32.length_ref, ...), custom_call_target="tpu_custom_call" | custom-call | tf_op jit(solution)/shard_map/pallas_call | solution.py:1208
  67.9 53.1 %shard_map.272 = (bf16[384,768]{1,0:T(8,128)(2,1)}, f32[384,768]{1,0:T(8,128)}, bf16[4,384,128]{2,1,0:T(8,128)(2,1)}, bf16[4,384,128]{2,1,0:T(8,128)(2,1)}, bf16...) custom-call(s32[1]{0:T(128)S(6)} %copy.32.length_ref, ...), custom_call_target="tpu_custom_call" | custom-call | tf_op jit(solution)/shard_map/pallas_call | solution.py:1266
  121.1 85.0 %shard_map.273 = (bf16[4,384,640]{2,1,0:T(8,128)(2,1)}, bf16[2,4,112,384]{3,2,1,0:T(8,128)(2,1)}, bf16[2,4,112,256]{3,2,1,0:T(8,128)(2,1)}, bf16[2,4,240,384]{3,...) custom-call(bf16[4,384,128]{2,1,0:T(8,128)(2,1)} %get-tuple-element.61.do_ref, ...), custom_call_target="tpu_custom_call" | custom-call | tf_op jit(solution)/shard_map/pallas_call | solution.py:1236
  206.1 0.0 copy-start
  206.1 9.7 %shard_map.274 = (bf16[384,768]{1,0:T(8,128)(2,1)}, f32[192,2304]{1,0:T(8,128)}, f32[192,3072]{1,0:T(8,128)}, f32[768,768]{1,0:T(8,128)}, f32[192,768]{1,0:T(8,1...) custom-call(bf16[4,384,640]{2,1,0:T(8,128)(2,1)} %get-tuple-element., ...), custom_call_target="tpu_custom_call" | custom-call | tf_op jit(solution)/shard_map/pallas_call | solution.py:1294
  215.8 0.0 copy-done
  215.8 0.8 copy.33
Async XLA Ops:
  206.1 9.7 %copy-start = (bf16[384,768]{1,0:T(8,128)(2,1)S(1)}, bf16[384,768]{1,0:T(8,128)(2,1)}, u32[]{:S(2)}) copy-start(bf16[384,768]{1,0:T(8,128)(2,1)} %get-tuple-element.60) | copy-start | bytes 1769476

commit v6 on v5

--- a/solution.py
+++ b/solution.py
@@ -429,12 +429,12 @@
         2: lambda: (second_hop(K_IN, 1), first_hop(K_BACK, 1)),
         4: lambda: (second_hop(K_IN, 2), third_hop(K_IN, 1)),
         5: lambda: line.step(2, K_BACK, K_OUT),
-        6: lambda: (second_hop(K_IN, 3), third_hop(K_IN, 2)),
-        7: lambda: (attended_tile(0), second_hop(K_BACK, 1)),
-        8: lambda: third_hop(K_IN, 3),
-        9: lambda: (line.step(3, K_BACK, K_OUT), [net.start((K_OUT, K_M, dz)) for dz in (1, 2, 3)]),
-        10: lambda: third_hop(K_BACK, 1),
-        11: lambda: attended_tile(1),
+        6: lambda: second_hop(K_IN, 3),
+        7: lambda: (attended_tile(0), third_hop(K_IN, 2)),
+        8: lambda: second_hop(K_BACK, 1),
+        9: lambda: third_hop(K_IN, 3),
+        10: lambda: (line.step(3, K_BACK, K_OUT), [net.start((K_OUT, K_M, dz)) for dz in (1, 2, 3)]),
+        11: lambda: (attended_tile(1), third_hop(K_BACK, 1)),
     }
 
     def progress(n):
@@ -1038,7 +1038,8 @@
         acc[...] += dot(grad_inner, winv[:, cols], NT)
         during(n, {
             0: lambda: step_one(0), 1: lambda: step_one(1),
-            2: lambda: (step_one(2), step_two(0)), 3: lambda: step_one(3),
+            2: lambda: (step_one(2), step_two(0)),
+            3: lambda: (step_one(3), line.step(2, K_QKV), net.start((K_QKV, 1), (K_QKV, 2))),
         })
         return carry
 
@@ -1059,8 +1060,6 @@
         do_ref[1, g, :, 0 : step - 128] = part[:, 128:step]
         do_ref[1, g, :, step - 128 :] = jnp.zeros((rows, 256 - step), bf16)
     net.start(*[(K_DO, j) for j in (1, 2, 3)])
-    line.step(2, K_QKV)
-    net.start((K_QKV, 1), (K_QKV, 2))
     do_in[0] = do_ref[0, chip]
     loc.start(K_DO1)
     for g in range(4):

time: 217 us -> 213 us (0.982)
  Pallas kernels: 214 us -> 211 us
where the time goes in v6:
time: 213 us
  Pallas kernels  211 us (99%)
    pallas_call x1, Pallas kernels, run_backward(): pl.pallas_call(backward_kernel, out_shape=(S((4, rows, PACK), bf16), S((2...  83.9 us
    pallas_call x1, Pallas kernels, run_forward(): pl.pallas_call(forward_kernel, out_shape=(S(q_shape, bf16), S(kv_shape, b...  65 us
    pallas_call x1, Pallas kernels, run_ffn(): pl.pallas_call(ffn_kernel, out_shape=(one, S((rows, width), f32), S((4, r...  52.1 us
    pallas_call x1, Pallas kernels, run_final(): pl.pallas_call(final_kernel, out_shape=(S((rows, width), bf16), S((shard,...  9.69 us

profile of v6, /device:TPU:1, one launch (start us, length us, event | category | flops | bytes accessed | tf_op | source)
XLA Modules:
  0.0 212.9 jit_solution(15502123799946767515)
XLA Ops:
  1.3 65.0 %shard_map.271 = (bf16[3,1536,128]{2,1,0:T(8,128)(2,1)}, bf16[3,3072,128]{2,1,0:T(8,128)(2,1)}, bf16[3,3072,128]{2,1,0:T(8,128)(2,1)}, bf16[3,1536,128]{2,1,0:T(...) custom-call(s32[1]{0:T(128)S(6)} %copy.32.length_ref, ...), custom_call_target="tpu_custom_call" | custom-call | tf_op jit(solution)/shard_map/pallas_call | solution.py:1207
  66.3 52.1 %shard_map.272 = (bf16[384,768]{1,0:T(8,128)(2,1)}, f32[384,768]{1,0:T(8,128)}, bf16[4,384,128]{2,1,0:T(8,128)(2,1)}, bf16[4,384,128]{2,1,0:T(8,128)(2,1)}, bf16...) custom-call(s32[1]{0:T(128)S(6)} %copy.32.length_ref, ...), custom_call_target="tpu_custom_call" | custom-call | tf_op jit(solution)/shard_map/pallas_call | solution.py:1265
  118.5 83.9 %shard_map.273 = (bf16[4,384,640]{2,1,0:T(8,128)(2,1)}, bf16[2,4,112,384]{3,2,1,0:T(8,128)(2,1)}, bf16[2,4,112,256]{3,2,1,0:T(8,128)(2,1)}, bf16[2,4,240,384]{3,...) custom-call(bf16[4,384,128]{2,1,0:T(8,128)(2,1)} %get-tuple-element.61.do_ref, ...), custom_call_target="tpu_custom_call" | custom-call | tf_op jit(solution)/shard_map/pallas_call | solution.py:1235
  202.3 0.0 copy-start
  202.3 9.7 %shard_map.274 = (bf16[384,768]{1,0:T(8,128)(2,1)}, f32[192,2304]{1,0:T(8,128)}, f32[192,3072]{1,0:T(8,128)}, f32[768,768]{1,0:T(8,128)}, f32[192,768]{1,0:T(8,1...) custom-call(bf16[4,384,640]{2,1,0:T(8,128)(2,1)} %get-tuple-element., ...), custom_call_target="tpu_custom_call" | custom-call | tf_op jit(solution)/shard_map/pallas_call | solution.py:1293
  212.0 0.0 copy-done
  212.1 0.8 copy.33
Async XLA Ops:
  202.3 9.7 %copy-start = (bf16[384,768]{1,0:T(8,128)(2,1)S(1)}, bf16[384,768]{1,0:T(8,128)(2,1)}, u32[]{:S(2)}) copy-start(bf16[384,768]{1,0:T(8,128)(2,1)} %get-tuple-element.60) | copy-start | bytes 1769476

commit v7 on v6

--- a/solution.py
+++ b/solution.py
@@ -427,8 +427,8 @@
         0: lambda: (in_hop(2), in_hop(3)),
         1: lambda: line.step(1, K_BACK, K_OUT),
         2: lambda: (second_hop(K_IN, 1), first_hop(K_BACK, 1)),
-        4: lambda: (second_hop(K_IN, 2), third_hop(K_IN, 1)),
-        5: lambda: line.step(2, K_BACK, K_OUT),
+        4: lambda: second_hop(K_IN, 2),
+        5: lambda: (third_hop(K_IN, 1), line.step(2, K_BACK, K_OUT)),
         6: lambda: second_hop(K_IN, 3),
         7: lambda: (attended_tile(0), third_hop(K_IN, 2)),
         8: lambda: second_hop(K_BACK, 1),

time: 213 us -> 212 us (level)
  no operation moved by 1% of the time
where the time goes in v7:
time: 212 us
  Pallas kernels  210 us (99%)
    pallas_call x1, Pallas kernels, run_backward(): pl.pallas_call(backward_kernel, out_shape=(S((4, rows, PACK), bf16), S((2...  84.5 us
    pallas_call x1, Pallas kernels, run_forward(): pl.pallas_call(forward_kernel, out_shape=(S(q_shape, bf16), S(kv_shape, b...  64.5 us
    pallas_call x1, Pallas kernels, run_ffn(): pl.pallas_call(ffn_kernel, out_shape=(one, S((rows, width), f32), S((4, r...  51.2 us
    pallas_call x1, Pallas kernels, run_final(): pl.pallas_call(final_kernel, out_shape=(S((rows, width), bf16), S((shard,...  9.69 us

profile of v7, /device:TPU:1, one launch (start us, length us, event | category | flops | bytes accessed | tf_op | source)
XLA Modules:
  0.0 212.1 jit_solution(1283425718454702476)
XLA Ops:
  1.3 64.5 %shard_map.271 = (bf16[3,1536,128]{2,1,0:T(8,128)(2,1)}, bf16[3,3072,128]{2,1,0:T(8,128)(2,1)}, bf16[3,3072,128]{2,1,0:T(8,128)(2,1)}, bf16[3,1536,128]{2,1,0:T(...) custom-call(s32[1]{0:T(128)S(6)} %copy.32.length_ref, ...), custom_call_target="tpu_custom_call" | custom-call | tf_op jit(solution)/shard_map/pallas_call | solution.py:1207
  65.8 51.2 %shard_map.272 = (bf16[384,768]{1,0:T(8,128)(2,1)}, f32[384,768]{1,0:T(8,128)}, bf16[4,384,128]{2,1,0:T(8,128)(2,1)}, bf16[4,384,128]{2,1,0:T(8,128)(2,1)}, bf16...) custom-call(s32[1]{0:T(128)S(6)} %copy.32.length_ref, ...), custom_call_target="tpu_custom_call" | custom-call | tf_op jit(solution)/shard_map/pallas_call | solution.py:1265
  117.1 84.5 %shard_map.273 = (bf16[4,384,640]{2,1,0:T(8,128)(2,1)}, bf16[2,4,112,384]{3,2,1,0:T(8,128)(2,1)}, bf16[2,4,112,256]{3,2,1,0:T(8,128)(2,1)}, bf16[2,4,240,384]{3,...) custom-call(bf16[4,384,128]{2,1,0:T(8,128)(2,1)} %get-tuple-element.61.do_ref, ...), custom_call_target="tpu_custom_call" | custom-call | tf_op jit(solution)/shard_map/pallas_call | solution.py:1235
  201.6 0.0 copy-start
  201.6 9.7 %shard_map.274 = (bf16[384,768]{1,0:T(8,128)(2,1)}, f32[192,2304]{1,0:T(8,128)}, f32[192,3072]{1,0:T(8,128)}, f32[768,768]{1,0:T(8,128)}, f32[192,768]{1,0:T(8,1...) custom-call(bf16[4,384,640]{2,1,0:T(8,128)(2,1)} %get-tuple-element., ...), custom_call_target="tpu_custom_call" | custom-call | tf_op jit(solution)/shard_map/pallas_call | solution.py:1293
  211.3 0.0 copy-done
  211.3 0.8 copy.33
Async XLA Ops:
  201.6 9.7 %copy-start = (bf16[384,768]{1,0:T(8,128)(2,1)S(1)}, bf16[384,768]{1,0:T(8,128)(2,1)}, u32[]{:S(2)}) copy-start(bf16[384,768]{1,0:T(8,128)(2,1)} %get-tuple-element.60) | copy-start | bytes 1769476
